TPU v7x, 32 devices: a whole 2x2x4 slice. The times are simulated.
32 devices in a mesh: gx: 2 (over x), gy: 4 (over y, core), dp: 4 (over z).
Axes of the slice: x: 2, y: 2, z: 4, core: 2. Of those that a mesh axis runs over, the one named last changes fastest.
Arguments:
- features: bfloat16 [4, 32, 1024, 128], P('dp', 'gx', 'gy'), may hold values from -6 to 6
- kernel: bfloat16 [3, 3, 3, 64, 64], replicated, may hold values from -0.15625 to 0.15625
- offsets: float32 [64], replicated, may hold values from -3 to 3
- upstream: bfloat16 [4, 32, 1024, 128], P('dp', 'gx', 'gy'), may hold values from -6 to 6
- grad_exponents: int32 [3, 3, 3], replicated, may hold values from -2 to 2
Outputs:
- activation: bfloat16 [4, 32, 1024, 128], P('dp', 'gx', 'gy')
- input_grad: bfloat16 [4, 32, 1024, 128], P('dp', 'gx', 'gy')
- kernel_grad: bfloat16 [3, 3, 3, 64, 64], P(None, None, None, None, 'dp')
- bias_grad: float32 [64], P('dp')
All inputs are finite; a program needn't handle non-finite values.
Results may differ from a plain program's by a relative error of at most 0.007.
Values may be sent and summed in bfloat16 or wider, within the bound.
No kernel may reach another device: no remote copies, remote signals or barrier semaphores. Data moves between devices by JAX's collectives and lax.ppermute only.
A program may use at most 128 MiB of HBM per device.

v0:
```python
import math

import jax
import jax.numpy as jnp
from jax import lax
from jax.sharding import PartitionSpec as P


def extended(cells, sides, width):
    for axis, dim in sides:
        count = lax.axis_size(axis)
        ends = count - 1
        head = lax.slice_in_dim(cells, 0, width, axis=dim)
        tail = lax.slice_in_dim(cells, cells.shape[dim] - width, cells.shape[dim], axis=dim)
        cells = jnp.concatenate(
            [
                lax.ppermute(tail, axis, [(i, (i + 1) % count) for i in range(ends)]),
                cells,
                lax.ppermute(head, axis, [((i + 1) % count, i) for i in range(ends)]),
            ],
            axis=dim,
        )
    return cells


def build_matrices(kernel):
    upper = jnp.concatenate([kernel[:, :, 1], kernel[:, :, 0]], axis=-1)
    lower = jnp.concatenate([kernel[:, :, 2], kernel[:, :, 1]], axis=-1)
    return jnp.concatenate([upper, lower], axis=2)


def forward_conv(padded, matrices, size_x, size_y, bias_full):
    total = bias_full
    for shift_x in range(3):
        for shift_y in range(3):
            window = padded[:, shift_x : shift_x + size_x, shift_y : shift_y + size_y]
            total = total + jnp.einsum(
                "sxyc,cd->sxyd",
                window,
                matrices[shift_x, shift_y],
                preferred_element_type=jnp.float32,
            )
    return total


def backward_conv(grad_pad, matrices, size_x, size_y):
    total = None
    for shift_x in range(3):
        for shift_y in range(3):
            window = grad_pad[
                :, 2 - shift_x : 2 - shift_x + size_x, 2 - shift_y : 2 - shift_y + size_y
            ]
            term = jnp.einsum(
                "sxyd,cd->sxyc",
                window,
                matrices[shift_x, shift_y],
                preferred_element_type=jnp.float32,
            )
            total = term if total is None else total + term
    return total


def weight_blocks(source_pad, pre_grad, start, size_x, size_y):
    blocks = []
    for shift_x in range(3):
        for shift_y in range(3):
            window = source_pad[
                :,
                start + shift_x : start + shift_x + size_x,
                start + shift_y : start + shift_y + size_y,
            ]
            blocks.append(
                jnp.einsum("sxyc,sxyd->cd", window, pre_grad, preferred_element_type=jnp.float32)
            )
    width = pre_grad.shape[3]
    return jnp.stack(blocks).reshape(3, 3, width, width)


def local(features, kernel, offsets, upstream, grad_exponents):
    matrices = build_matrices(kernel)
    size_x, size_y, width = (features.shape[1], features.shape[2], features.shape[3])
    chans = width // 2
    bias_full = jnp.concatenate([offsets, offsets])
    padded = extended(features, (("gx", 1), ("gy", 2)), 1)
    preact = forward_conv(padded, matrices, size_x, size_y, bias_full)
    sigma = jax.nn.sigmoid(preact)
    activation = (preact * sigma).astype(jnp.bfloat16)
    pre_grad = (upstream.astype(jnp.float32) * sigma * (1.0 + preact * (1.0 - sigma))).astype(
        jnp.bfloat16
    )
    grad_pad = extended(pre_grad, (("gx", 1), ("gy", 2)), 1)
    matrix_grad = weight_blocks(padded, pre_grad, 0, size_x, size_y)
    input_grad = backward_conv(grad_pad, matrices, size_x, size_y).astype(jnp.bfloat16)
    tap_low = matrix_grad[:, :, :chans, chans:]
    tap_mid = matrix_grad[:, :, :chans, :chans] + matrix_grad[:, :, chans:, chans:]
    tap_high = matrix_grad[:, :, chans:, :chans]
    tap_grad = jnp.stack([tap_low, tap_mid, tap_high], axis=2)
    summed = jnp.sum(pre_grad.astype(jnp.float32), axis=(0, 1, 2))
    bias_sum = summed[:chans] + summed[chans:]
    tap_grad, bias_sum = lax.psum((tap_grad, bias_sum), ("gx", "gy"))
    tap_grad, bias_sum = (
        lax.psum_scatter(tap_grad, "dp", scatter_dimension=4, tiled=True),
        lax.psum_scatter(bias_sum, "dp", scatter_dimension=0, tiled=True),
    )
    count = (
        features.shape[0]
        * lax.axis_size("dp")
        * size_x
        * lax.axis_size("gx")
        * size_y
        * lax.axis_size("gy")
        * 2
    )
    inverse = 1.0 / math.sqrt(count)
    scales = jnp.exp2(grad_exponents.astype(jnp.float32))[:, :, :, None, None]
    kernel_grad = (tap_grad * scales * inverse).astype(jnp.bfloat16)
    bias_grad = bias_sum * inverse
    return (activation, input_grad, kernel_grad, bias_grad)


def solution(mesh):
    placed = (P("dp", "gx", "gy", None), P(), P(), P("dp", "gx", "gy", None), P())
    return jax.shard_map(
        local,
        mesh=mesh,
        in_specs=placed,
        out_specs=(
            P("dp", "gx", "gy", None),
            P("dp", "gx", "gy", None),
            P(None, None, None, None, "dp"),
            P("dp"),
        ),
        check_vma=False,
    )
```

profile of v0, /device:TPU:0, one launch (start us, length us, event | category | flops | bytes accessed | tf_op | source)
XLA Modules:
  0.0 155.2 jit_solution(7710295497685129155)
XLA Ops:
  7.2 0.0 reduce-scatter.2.cloned.1.call-start
  7.2 1.0 fusion.95
  8.2 4.8 %collective-permute-start = (bf16[1,1,256,128]{3,2,1,0:T(8,128)(2,1)S(1)}, bf16[1,1,256,128]{3,2,1,0:T(8,128)(2,1)S(1)}, u32[]{:S(2)}, u32[]{:S(2)}) collective-permute-start(bf16[1,1,256,128]{3,2,1,0:T(8,128)(2,1)S(1)} %get-tuple-element.14), channel_id=1, source_target_pairs={{0,16},{1,17},{2,18},{3,19},{4,20},{5,21},{6,22},{7,23},{8,24},{9,... | collective-permute-start | bytes 196616 | tf_op jit(solution)/shard_map/ppermute | solution.py:17
  13.0 1.3 collective-permute-start.1
  14.3 1.1 slice_bitcast_fusion.15
  15.5 0.2 maximum_maximum_fusion.1
  15.7 1.8 %fusion.53 = f32[128,16,256]{0,2,1:T(8,128)} fusion(bf16[1,16,256,128]{3,2,1,0:T(8,128)(2,1)S(1)} %copy-done, bf16[3,3,128,128]{3,2,1,0:T(8,128)(2,1)S(1)} %maximum_maximum_fusion.1), kind=kOutput, calls=%fused_computation.89 | convolution fusion | flops 134217728 | bytes 3178496 | tf_op jit(solution)/shard_map/sxyc,cd->sxyd/dot_general | solution.py:37
  17.4 0.6 dynamic-slice
  18.7 0.1 pad_maximum_fusion.11
  18.8 0.2 constant_dynamic-update-slice_fusion.1
  18.9 0.3 collective-permute-done.1
  19.2 1.3 collective-permute-start.3
  20.5 3.0 %collective-permute-start.2 = (bf16[1,18,1,128]{3,2,1,0:T(2,128)(2,1)S(1)}, bf16[1,18,1,128]{3,2,1,0:T(2,128)(2,1)S(1)}, u32[]{:S(2)}, u32[]{:S(2)}) collective-permute-start(bf16[1,18,1,128]{3,2,1,0:T(2,128)(2,1)S(1)} %get-tuple-element.11), channel_id=1, source_target_pairs={{0,4},{4,8},{8,12},{1,5},{5,9},{9,13},{2,6},{6,10},{10,14},{3,7},{... | collective-permute-start | bytes 13832 | tf_op jit(solution)/shard_map/ppermute | solution.py:17
  23.6 0.4 fusion.60
  24.0 0.4 fusion.57
  24.4 0.4 fusion.70
  24.9 0.4 fusion.63
  25.3 0.4 fusion.72
  25.8 0.4 fusion.71
  26.2 0.4 fusion.73
  26.7 1.1 copy-done.1
  27.8 0.3 copy-done.4
  28.1 3.6 %convert_reduce_fusion = (f32[128]{0:T(128)S(1)}, bf16[1,16,256,128]{3,2,1,0:T(8,128)(2,1)S(1)}, f32[16,256,128]{2,1,0:T(8,128)}) fusion(bf16[1,16,256,128]{3,2,1,0:T(8,128)(2,1)S(1)} %copy-done.4, bf16[3,3,128,128]{3,2,1,0:T(8,128)(2,1)} %copy-done.2, bf16[1,18,1,128]{3,2,1,0:T(2,128)(2,1)S(1)} %collective-permute-done.3, ...), kind=kOutput, calls=%fused_computation.8 | convolution fusion | flops 147324800 | bytes 22189568 | tf_op jit(solution)/shard_map/sxyc,cd->sxyd/dot_general | solution.py:37
  31.7 0.1 slice_add_fusion
  31.8 11.9 %all-reduce = f32[64]{0:T(128)S(1)} all-reduce(f32[64]{0:T(128)S(1)} %slice_add_fusion), channel_id=3, replica_groups=mesh['gx'=2,'gy'=4,'dp'=4] {'dp'}, use_global_device_ids=true, to_apply=%region_4.0.clone | all-reduce | flops 64 | bytes 512
  43.7 0.1 dynamic-slice.1
  43.8 13.8 %psum.17 = f32[16]{0:T(128)S(1)} all-reduce(f32[16]{0:T(128)S(1)} %dynamic-slice.1), channel_id=1, replica_groups=mesh['gx'=2,'gy'=4,'dp'=4] {'gx','gy'}, use_global_device_ids=true, to_apply=%region_3.0 | all-reduce | flops 16 | bytes 128 | tf_op jit(solution)/shard_map/psum | solution.py:100
  57.6 0.5 broadcast_multiply_fusion
  58.1 0.7 fusion.94
  58.8 1.3 collective-permute-start.5
  60.1 4.5 %collective-permute-start.4 = (bf16[1,1,256,128]{3,2,1,0:T(8,128)(2,1)}, bf16[1,1,256,128]{3,2,1,0:T(8,128)(2,1)S(1)}, u32[]{:S(2)}, u32[]{:S(2)}) collective-permute-start(bf16[1,1,256,128]{3,2,1,0:T(8,128)(2,1)} %get-tuple-element.13), channel_id=1, source_target_pairs={{0,16},{1,17},{2,18},{3,19},{4,20},{5,21},{6,22},{7,23},{8,24},{9,... | collective-permute-start | bytes 196616 | tf_op jit(solution)/shard_map/ppermute | solution.py:17
  64.6 0.5 fusion.13
  65.1 1.3 fusion.12
  66.5 0.5 fusion.11
  66.9 0.5 fusion.10
  67.4 0.5 fusion.9
  67.9 0.5 fusion.8
  68.4 0.5 fusion.7
  68.9 0.5 fusion.6
  69.4 0.5 fusion.5
  69.9 0.2 fusion.96
  70.1 0.1 copy.64
  70.3 0.1 copy.66
  70.4 0.2 copy.65
  70.6 0.2 copy.67
  70.8 1.0 pad_maximum_fusion.7
  71.8 0.0 reduce-scatter.2.cloned.1.call-update
  71.8 0.0 all-reduce.3.cloned.1.call-start
  71.8 3.1 %fusion.55 = bf16[1,16,256,128]{3,2,1,0:T(8,128)(2,1)} fusion(f32[16,256,128]{2,1,0:T(8,128)} %get-tuple-element.23), kind=kLoop, calls=%fused_computation.91 | loop fusion | flops 2621440 | bytes 3145728 | tf_op jit(solution)/shard_map/convert_element_type | solution.py:87
  75.0 1.8 %fusion.50 = f32[16,256,128]{2,1,0:T(8,128)} fusion(bf16[1,16,256,128]{3,2,1,0:T(8,128)(2,1)S(1)} %get-tuple-element.5, bf16[3,3,128,128]{3,2,1,0:T(8,128)(2,1)S(1)} %copy-done.3), kind=kOutput, calls=%fused_computation.86 | convolution fusion | flops 134217728 | bytes 3178496 | tf_op jit(solution)/shard_map/sxyd,cd->sxyc/dot_general | solution.py:53
  76.8 1.7 %collective-permute-start.7 = (bf16[1,18,1,128]{3,2,1,0:T(2,128)(2,1)S(1)}, bf16[1,18,1,128]{3,2,1,0:T(2,128)(2,1)S(1)}, u32[]{:S(2)}, u32[]{:S(2)}) collective-permute-start(bf16[1,18,1,128]{3,2,1,0:T(2,128)(2,1)S(1)} %get-tuple-element.8), channel_id=1, source_target_pairs={{0,4},{4,8},{8,12},{1,5},{5,9},{9,13},{2,6},{6,10},{10,14},{3,7},{... | collective-permute-start | bytes 13832 | tf_op jit(solution)/shard_map/ppermute | solution.py:17
  78.5 1.5 collective-permute-start.6
  80.0 1.8 %fusion.25 = f32[16,256,128]{2,1,0:T(8,128)} fusion(bf16[1,16,256,128]{3,2,1,0:T(8,128)(2,1)S(1)} %get-tuple-element.5, bf16[1,1,256,128]{3,2,1,0:T(8,128)(2,1)S(1)} %collective-permute-done.4, bf16[3,3,128,128]{3,2,1,0:T(8,128)(2,1)S(1)} %copy-done.3), kind=kOutput, calls=%fused_computation.53 | convolution fusion | flops 134742016 | bytes 3244032 | tf_op jit(solution)/shard_map/sxyd,cd->sxyc/dot_general | solution.py:53
  81.7 1.7 %fusion.33 = f32[16,256,128]{2,1,0:T(8,128)} fusion(bf16[1,1,256,128]{3,2,1,0:T(8,128)(2,1)S(1)} %collective-permute-done.5, bf16[1,16,256,128]{3,2,1,0:T(8,128)(2,1)S(1)} %get-tuple-element.5, bf16[3,3,128,128]{3,2,1,0:T(8,128)(2,1)S(1)} %copy-done.3), kind=kOutput, calls=%fused_computation.65 | convolution fusion | flops 134742016 | bytes 3244032 | tf_op jit(solution)/shard_map/sxyd,cd->sxyc/dot_general | solution.py:53
  83.5 0.6 maximum_maximum_fusion
  84.1 1.8 %fusion.29 = f32[16,256,128]{2,1,0:T(8,128)} fusion(bf16[1,18,257,128]{3,2,1,0:T(8,128)(2,1)S(1)} %get-tuple-element.6, bf16[3,3,128,128]{3,2,1,0:T(8,128)(2,1)S(1)} %copy-done.3), kind=kOutput, calls=%fused_computation.58 | convolution fusion | flops 134217728 | bytes 3178496 | tf_op jit(solution)/shard_map/sxyd,cd->sxyc/dot_general | solution.py:53
  85.9 1.8 %fusion.31 = f32[16,256,128]{2,1,0:T(8,128)} fusion(bf16[1,18,257,128]{3,2,1,0:T(8,128)(2,1)S(1)} %get-tuple-element.6, bf16[3,3,128,128]{3,2,1,0:T(8,128)(2,1)S(1)} %copy-done.3), kind=kOutput, calls=%fused_computation.62 | convolution fusion | flops 134217728 | bytes 3178496 | tf_op jit(solution)/shard_map/sxyd,cd->sxyc/dot_general | solution.py:53
  87.7 1.8 %fusion.28 = f32[16,256,128]{2,1,0:T(8,128)} fusion(bf16[1,18,257,128]{3,2,1,0:T(8,128)(2,1)S(1)} %get-tuple-element.7, bf16[3,3,128,128]{3,2,1,0:T(8,128)(2,1)S(1)} %copy-done.3), kind=kOutput, calls=%fused_computation.56 | convolution fusion | flops 134217728 | bytes 3178496 | tf_op jit(solution)/shard_map/sxyd,cd->sxyc/dot_general | solution.py:53
  89.5 1.8 %fusion.30 = f32[16,256,128]{2,1,0:T(8,128)} fusion(bf16[1,18,257,128]{3,2,1,0:T(8,128)(2,1)S(1)} %get-tuple-element.7, bf16[3,3,128,128]{3,2,1,0:T(8,128)(2,1)S(1)} %copy-done.3), kind=kOutput, calls=%fused_computation.60 | convolution fusion | flops 134217728 | bytes 3178496 | tf_op jit(solution)/shard_map/sxyd,cd->sxyc/dot_general | solution.py:53
  91.3 1.8 %fusion.36 = f32[16,256,128]{2,1,0:T(8,128)} fusion(bf16[1,18,257,128]{3,2,1,0:T(8,128)(2,1)S(1)} %get-tuple-element.7, bf16[3,3,128,128]{3,2,1,0:T(8,128)(2,1)S(1)} %copy-done.3), kind=kOutput, calls=%fused_computation.68 | convolution fusion | flops 134217728 | bytes 3178496 | tf_op jit(solution)/shard_map/sxyd,cd->sxyc/dot_general | solution.py:53
  93.1 0.0 all-reduce.3.cloned.1.call-update
  93.1 7.7 %fusion.22 = bf16[1,16,256,128]{3,2,1,0:T(8,128)(2,1)} fusion(f32[16,256,128]{2,1,0:T(8,128)} %fusion.25, f32[16,256,128]{2,1,0:T(8,128)} %fusion.28, f32[16,256,128]{2,1,0:T(8,128)} %fusion.29, f32[16,256,128]{2,1,0:T(8,128)} %fusion.50, f32[16,256,128]{2,1,0:T(8,128)} %fusion.30, f32[16,256,128]{2,1,0:T(8,128)} %fusion.31, f32[16,256,128]{2,1,0:T(8,128)} %fusion.36, ...), kind=kOutput, calls=%fused_computation.48 | convolution fusion | flops 138936320 | bytes 18907136 | tf_op jit(solution)/shard_map/sxyd,cd->sxyc/dot_general | solution.py:53
  100.8 45.8 %all-reduce.3.cloned.1.call-done = f32[3,3,3,64,16]{3,4,2,1,0:T(8,128)} async-done(((f32[3,3,3,64,16]{3,4,2,1,0:T(8,128)}), f32[3,3,3,64,16]{3,4,2,1,0:T(8,128)}) %all-reduce.3.cloned.1.call-update) | async-done | bytes 110608 | tf_op jit(solution)/shard_map/psum | solution.py:100
  146.7 1.7 %multiply_convert_fusion.1 = bf16[3,3,3,64,16]{3,4,2,1,0:T(8,128)(2,1)} fusion(f32[3,3,3,64,16]{3,4,2,1,0:T(8,128)} %all-reduce.3.cloned.1.call-done, f32[3,3,3]{2,1,0:T(4,128)S(1)} %multiply_exponential_fusion), kind=kLoop, calls=%fused_computation.99 | loop fusion | flops 82944 | bytes 165996 | tf_op jit(solution)/shard_map/convert_element_type | solution.py:116
  (30 shorter events, 0.2 us)
Async XLA Ops:
  7.2 8.5 %copy-start = (bf16[1,16,256,128]{3,2,1,0:T(8,128)(2,1)S(1)}, bf16[1,16,256,128]{3,2,1,0:T(8,128)(2,1)}, u32[]{:S(2)}) copy-start(bf16[1,16,256,128]{3,2,1,0:T(8,128)(2,1)} %param.5) | copy-start | bytes 3145732
  7.2 85.9 %reduce-scatter.2.cloned.1.call-start = ((), (), s32[]{:S(2)}) async-start(), calls=%async_computation.1 | async-start | bytes 1105920 | tf_op jit(solution)/shard_map/reduce_scatter | solution.py:102
  8.2 10.6 %collective-permute-start = (bf16[1,1,256,128]{3,2,1,0:T(8,128)(2,1)S(1)}, bf16[1,1,256,128]{3,2,1,0:T(8,128)(2,1)S(1)}, u32[]{:S(2)}, u32[]{:S(2)}) collective-permute-start(bf16[1,1,256,128]{3,2,1,0:T(8,128)(2,1)S(1)} %get-tuple-element.14), channel_id=1, source_target_pairs={{0,16},{1,17},{2,18},{3,19},{4,20},{5,21},{6,22},{7,23},{8,24},{9,... | collective-permute-start | bytes 196616 | tf_op jit(solution)/shard_map/ppermute | solution.py:17
  13.0 6.2 %collective-permute-start.1 = (bf16[1,1,256,128]{3,2,1,0:T(8,128)(2,1)S(1)}, bf16[1,1,256,128]{3,2,1,0:T(8,128)(2,1)S(1)}, u32[]{:S(2)}, u32[]{:S(2)}) collective-permute-start(bf16[1,1,256,128]{3,2,1,0:T(8,128)(2,1)S(1)} %get-tuple-element.15), channel_id=1, source_target_pairs={{16,0},{17,1},{18,2},{19,3},{20,4},{21,5},{22,6},{23,7},{24,8},{25... | collective-permute-start | bytes 196616 | tf_op jit(solution)/shard_map/ppermute | solution.py:19
  15.4 2.0 %copy-start.8 = (u32[32]{0:T(128)S(1)}, u32[32]{0:T(128)}, u32[]{:S(2)}) copy-start(u32[32]{0:T(128)} %constant.13) | copy-start | bytes 388
  15.5 3.2 %copy-start.7 = (f32[64]{0:T(128)S(1)}, f32[64]{0:T(128)}, u32[]{:S(2)}) copy-start(f32[64]{0:T(128)} %param.7) | copy-start | bytes 772
  15.6 10.5 %copy-start.2 = (bf16[3,3,128,128]{3,2,1,0:T(8,128)(2,1)}, bf16[3,3,128,128]{3,2,1,0:T(8,128)(2,1)S(1)}, u32[]{:S(2)}) copy-start(bf16[3,3,128,128]{3,2,1,0:T(8,128)(2,1)S(1)} %maximum_maximum_fusion.1) | copy-start | bytes 884740
  18.7 5.3 %copy-start.5 = (bf16[1,1,256,128]{3,2,1,0:T(8,128)(2,1)}, bf16[1,1,256,128]{3,2,1,0:T(8,128)(2,1)S(1)}, u32[]{:S(2)}) copy-start(bf16[1,1,256,128]{3,2,1,0:T(8,128)(2,1)S(1)} %collective-permute-done) | copy-start | bytes 196612
  19.2 6.5 %collective-permute-start.3 = (bf16[1,18,1,128]{3,2,1,0:T(2,128)(2,1)S(1)}, bf16[1,18,1,128]{3,2,1,0:T(2,128)(2,1)S(1)}, u32[]{:S(2)}, u32[]{:S(2)}) collective-permute-start(bf16[1,18,1,128]{3,2,1,0:T(2,128)(2,1)S(1)} %get-tuple-element.10), channel_id=1, source_target_pairs={{4,0},{8,4},{12,8},{5,1},{9,5},{13,9},{6,2},{10,6},{14,10},{7,3},{... | collective-permute-start | bytes 13832 | tf_op jit(solution)/shard_map/ppermute | solution.py:19
  20.5 3.9 %collective-permute-start.2 = (bf16[1,18,1,128]{3,2,1,0:T(2,128)(2,1)S(1)}, bf16[1,18,1,128]{3,2,1,0:T(2,128)(2,1)S(1)}, u32[]{:S(2)}, u32[]{:S(2)}) collective-permute-start(bf16[1,18,1,128]{3,2,1,0:T(2,128)(2,1)S(1)} %get-tuple-element.11), channel_id=1, source_target_pairs={{0,4},{4,8},{8,12},{1,5},{5,9},{9,13},{2,6},{6,10},{10,14},{3,7},{... | collective-permute-start | bytes 13832 | tf_op jit(solution)/shard_map/ppermute | solution.py:17
  26.2 1.6 %copy-start.1 = (f32[128,16,256]{0,2,1:T(8,128)S(1)}, f32[128,16,256]{0,2,1:T(8,128)}, u32[]{:S(2)}) copy-start(f32[128,16,256]{0,2,1:T(8,128)} %fusion.53) | copy-start | bytes 6291460
  26.2 1.8 %copy-start.4 = (bf16[1,16,256,128]{3,2,1,0:T(8,128)(2,1)S(1)}, bf16[1,16,256,128]{3,2,1,0:T(8,128)(2,1)}, u32[]{:S(2)}) copy-start(bf16[1,16,256,128]{3,2,1,0:T(8,128)(2,1)} %param.8) | copy-start | bytes 3145732
  28.1 15.7 %copy-start.6 = (s32[3,3,3]{2,1,0:T(4,128)S(1)}, s32[3,3,3]{2,1,0:T(4,128)}, u32[]{:S(2)}) copy-start(s32[3,3,3]{2,1,0:T(4,128)} %param.9) | copy-start | bytes 328
  58.8 18.0 %collective-permute-start.5 = (bf16[1,1,256,128]{3,2,1,0:T(8,128)(2,1)}, bf16[1,1,256,128]{3,2,1,0:T(8,128)(2,1)S(1)}, u32[]{:S(2)}, u32[]{:S(2)}) collective-permute-start(bf16[1,1,256,128]{3,2,1,0:T(8,128)(2,1)} %get-tuple-element.12), channel_id=1, source_target_pairs={{16,0},{17,1},{18,2},{19,3},{20,4},{21,5},{22,6},{23,7},{24,8},{25... | collective-permute-start | bytes 196616 | tf_op jit(solution)/shard_map/ppermute | solution.py:19
  60.1 16.7 %collective-permute-start.4 = (bf16[1,1,256,128]{3,2,1,0:T(8,128)(2,1)}, bf16[1,1,256,128]{3,2,1,0:T(8,128)(2,1)S(1)}, u32[]{:S(2)}, u32[]{:S(2)}) collective-permute-start(bf16[1,1,256,128]{3,2,1,0:T(8,128)(2,1)} %get-tuple-element.13), channel_id=1, source_target_pairs={{0,16},{1,17},{2,18},{3,19},{4,20},{5,21},{6,22},{7,23},{8,24},{9,... | collective-permute-start | bytes 196616 | tf_op jit(solution)/shard_map/ppermute | solution.py:17
  71.8 3.2 %copy-start.3 = (bf16[3,3,128,128]{3,2,1,0:T(8,128)(2,1)S(1)}, bf16[3,3,128,128]{3,2,1,0:T(8,128)(2,1)}, u32[]{:S(2)}) copy-start(bf16[3,3,128,128]{3,2,1,0:T(8,128)(2,1)} %copy-done.2) | copy-start | bytes 884740
  71.8 74.9 %all-reduce.3.cloned.1.call-start = ((), (), s32[]{:S(2)}) async-start(), calls=%async_computation.2 | async-start | bytes 442368 | tf_op jit(solution)/shard_map/psum | solution.py:100
  76.8 6.7 %collective-permute-start.7 = (bf16[1,18,1,128]{3,2,1,0:T(2,128)(2,1)S(1)}, bf16[1,18,1,128]{3,2,1,0:T(2,128)(2,1)S(1)}, u32[]{:S(2)}, u32[]{:S(2)}) collective-permute-start(bf16[1,18,1,128]{3,2,1,0:T(2,128)(2,1)S(1)} %get-tuple-element.8), channel_id=1, source_target_pairs={{0,4},{4,8},{8,12},{1,5},{5,9},{9,13},{2,6},{6,10},{10,14},{3,7},{... | collective-permute-start | bytes 13832 | tf_op jit(solution)/shard_map/ppermute | solution.py:17
  78.5 5.0 %collective-permute-start.6 = (bf16[1,18,1,128]{3,2,1,0:T(2,128)(2,1)S(1)}, bf16[1,18,1,128]{3,2,1,0:T(2,128)(2,1)S(1)}, u32[]{:S(2)}, u32[]{:S(2)}) collective-permute-start(bf16[1,18,1,128]{3,2,1,0:T(2,128)(2,1)S(1)} %get-tuple-element.9), channel_id=1, source_target_pairs={{4,0},{8,4},{12,8},{5,1},{9,5},{13,9},{6,2},{10,6},{14,10},{7,3},{... | collective-permute-start | bytes 13832 | tf_op jit(solution)/shard_map/ppermute | solution.py:19
Sparse Core Ops, SparseCore 0:
  71.9 20.4 reduce-scatter.1
  95.5 51.1 all-reduce.2
where the time goes:
time: 156 us; the launch traced here: 155 us
  waiting for transfers between devices  46.1 us (30%)
  matrix products  35.6 us (23%)
  blocking collectives  25.8 us (17%)
  starting transfers between devices  19.5 us (12%)
  between operations  15 us (10%)
  other arithmetic  7.35 us (5%)
  local copies, waits for them, and re-layouts  5.83 us (4%)
    psum x1, waiting for transfers between devices, local(): tap_grad, bias_sum = lax.psum((tap_grad, bias_sum), ('gx', 'gy'))  45.8 us
    dot_general x9, matrix products, backward_conv(): jnp.einsum('sxyd,cd->sxyc', window, matrices[shift_x, shift_y], preferred...  22 us
    ppermute x4, starting transfers between devices, extended(): lax.ppermute(tail, axis, [(i, (i + 1) % count) for i in range(ends)])  14.1 us
    psum x1, blocking collectives, local(): tap_grad, bias_sum = lax.psum((tap_grad, bias_sum), ('gx', 'gy'))  13.8 us
    unnamed x1, blocking collectives  11.9 us
    dot_general x9, matrix products, forward_conv(): jnp.einsum('sxyc,cd->sxyd', window, matrices[shift_x, shift_y], preferred...  8.38 us
    ppermute x4, starting transfers between devices, extended(): lax.ppermute(head, axis, [((i + 1) % count, i) for i in range(ends)])  5.34 us
    dot_general x9, matrix products, weight_blocks(): jnp.einsum('sxyc,sxyd->cd', window, pre_grad, preferred_element_type=jnp....  5.22 us
  transfers between devices with their start and end apart: 10, of which 2 were waited for; matrix products, arithmetic and copies ran while one was open for 25% of the time, Pallas kernels for 0%

commit v1 on v0

v1 whole, which is shorter than its diff:
```python
import math

import jax
import jax.numpy as jnp
from jax import lax
from jax.experimental import pallas as pl
from jax.experimental.pallas import tpu as pltpu
from jax.sharding import PartitionSpec as P

PAD = 16
RIM = 8
VMEM = pl.BlockSpec(memory_space=pltpu.VMEM)
HBM = pl.BlockSpec(memory_space=pl.ANY)


def swap(value, axis, first):
    count = lax.axis_size(axis)
    links = []
    for low in range(first, count - 1, 2):
        links += [(low, low + 1), (low + 1, low)]
    if not links:
        return jnp.zeros_like(value)
    return lax.ppermute(value, axis, links)


def exchange(value, axis, step):
    return lax.ppermute(value, axis, [(i, i ^ step) for i in range(lax.axis_size(axis))])


def build_matrices(kernel):
    upper = jnp.concatenate([kernel[:, :, 1], kernel[:, :, 0]], axis=-1)
    lower = jnp.concatenate([kernel[:, :, 2], kernel[:, :, 1]], axis=-1)
    return jnp.concatenate([upper, lower], axis=2)


def conv_rows(planes, x, weights):
    rows, width = planes.shape[1], planes.shape[2]
    stacked = jnp.concatenate([planes[x], planes[x + 1], planes[x + 2]], axis=1)
    taps = jnp.dot(stacked, weights, preferred_element_type=jnp.float32)
    return (
        pltpu.roll(taps[:, :width], 1, 0)
        + taps[:, width : 2 * width]
        + pltpu.roll(taps[:, 2 * width :], rows - 1, 0)
    )


def clear_margins(planes):
    count, rows, width = planes.shape
    blank = jnp.zeros((count, RIM, width), planes.dtype)
    planes[:, :RIM, :] = blank
    planes[:, rows - RIM :, :] = blank


def place_rims(position, near, far, place):
    @pl.when(position == 0)
    def _():
        place(far, near)

    @pl.when(position == 1)
    def _():
        place(near, far)


def main_kernel(
    f_hbm, u_hbm, y_near, y_far, x_near, x_far, w_ref, bias_ref,
    act_hbm, grad_hbm, edge_near, edge_far, keep_ref, send_ref,
    fp, up, act, grad, turned, acc, in_sem, out_sem,
):
    size_x, size_y, width = f_hbm.shape
    half = width // 2
    parts = keep_ref.shape[0]
    share = keep_ref.shape[2]
    inner = pl.ds(PAD, size_y)
    loads = []
    for x in range(size_x):
        loads.append((
            pltpu.make_async_copy(f_hbm.at[x], fp.at[x + 1, inner], in_sem.at[0, x]),
            pltpu.make_async_copy(u_hbm.at[x], up.at[x, inner], in_sem.at[1, x]),
        ))
        for copy in loads[-1]:
            copy.start()
    y_side = lax.axis_index("gy") % 2
    x_side = lax.axis_index("gx") % 2
    clear_margins(fp)
    clear_margins(up)

    def place_y(left, right):
        fp[1 : size_x + 1, PAD - RIM : PAD, :] = left[:, :RIM, :]
        fp[1 : size_x + 1, PAD + size_y : PAD + size_y + RIM, :] = right[:, :RIM, :]
        up[:, PAD - RIM : PAD, :] = left[:, RIM:, :]
        up[:, PAD + size_y : PAD + size_y + RIM, :] = right[:, RIM:, :]

    def place_x(below, above):
        fp[0] = below[...]
        fp[size_x + 1] = above[...]

    place_rims(y_side, y_near, y_far, place_y)
    place_rims(x_side, x_near, x_far, place_x)

    weights = w_ref[...]
    bias = bias_ref[...]
    bias_sum = jnp.zeros((8, width), jnp.float32)

    def turn(x):
        turned[x] = fp[x, PAD : PAD + size_y, :].T

    turn(0)
    loads[0][0].wait()
    turn(1)
    stores = []
    for x in range(size_x):
        if x + 1 < size_x:
            loads[x + 1][0].wait()
        turn(x + 2)
        preact = conv_rows(fp, x, weights) + bias
        sigma = 0.5 * jnp.tanh(0.5 * preact) + 0.5
        act[x] = (preact * sigma)[PAD : PAD + size_y].astype(jnp.bfloat16)
        loads[x][1].wait()
        cotangent = up[x].astype(jnp.float32)
        rounded = (cotangent * sigma * (1.0 + preact * (1.0 - sigma))).astype(jnp.bfloat16)
        grad[x] = rounded
        wide = rounded.astype(jnp.float32)
        rows = wide.shape[0]
        ahead = pltpu.roll(wide, rows - 1, 0)[PAD : PAD + size_y]
        behind = pltpu.roll(wide, 1, 0)[PAD : PAD + size_y]
        middle = wide[PAD : PAD + size_y]
        bias_sum = bias_sum + jnp.sum(middle.reshape(size_y // 8, 8, width), axis=0)
        shifted = jnp.concatenate([ahead, middle, behind], axis=1).astype(jnp.bfloat16)
        source = turned[x : x + 3].reshape(3 * width, size_y)
        term = jnp.dot(source, shifted, preferred_element_type=jnp.float32)
        if x == 0:
            acc[...] = term
        else:
            acc[...] += term
        stores.append(pltpu.make_async_copy(act.at[x], act_hbm.at[x], out_sem.at[0, x]))
        stores.append(pltpu.make_async_copy(grad.at[x], grad_hbm.at[x], out_sem.at[1, x]))
        stores[-2].start()
        stores[-1].start()

    def place_edges(first, second):
        second[...] = grad[size_x - 1]
        first[...] = grad[0]

    place_rims(x_side, edge_near, edge_far, place_edges)

    lane = lax.broadcasted_iota(jnp.int32, (half, width), 1)
    lower = lane < half
    column = jnp.broadcast_to(jnp.sum(bias_sum, axis=0, keepdims=True), (width, width)).T
    column = column[:half] + column[half:]
    slots, tails = [], []
    for a in range(3):
        for b in range(3):
            block = acc[a * width : (a + 1) * width, b * width : (b + 1) * width].T
            top, bottom = block[:half], block[half:]
            rolled = pltpu.roll(bottom, half, 1)
            slots.append(top + jnp.where(lower, rolled, 0.0))
            tails.append((bottom, rolled))
    for t in range(0, 9, 2):
        second = tails[t + 1][1] if t + 1 < 9 else column
        slots.append(jnp.where(lower, tails[t][0], second))
    count = len(slots) // 2

    def emit(first, second):
        for s in range(count):
            for d in range(parts):
                first[d, s] = slots[s][d * share : (d + 1) * share]
                second[d, s] = slots[count + s][d * share : (d + 1) * share]

    @pl.when(y_side == 0)
    def _():
        emit(keep_ref, send_ref)

    @pl.when(y_side == 1)
    def _():
        emit(send_ref, keep_ref)

    for copy in stores:
        copy.wait()


def back_kernel(grad_hbm, x_near, x_far, w_ref, out_hbm, gp, out, in_sem, out_sem):
    size_x = grad_hbm.shape[0]
    size_y = out.shape[1]
    loads = []
    for x in range(size_x):
        loads.append(pltpu.make_async_copy(grad_hbm.at[x], gp.at[x + 1], in_sem.at[x]))
        loads[-1].start()

    def place_x(below, above):
        gp[0] = below[...]
        gp[size_x + 1] = above[...]

    place_rims(lax.axis_index("gx") % 2, x_near, x_far, place_x)
    weights = w_ref[...]
    loads[0].wait()
    stores = []
    for x in range(size_x):
        if x + 1 < size_x:
            loads[x + 1].wait()
        out[x] = conv_rows(gp, x, weights)[PAD : PAD + size_y].astype(jnp.bfloat16)
        stores.append(pltpu.make_async_copy(out.at[x], out_hbm.at[x], out_sem.at[x]))
        stores[-1].start()
    for copy in stores:
        copy.wait()


def finish_kernel(own, other, scale_ref, grad_ref, bias_ref, both):
    side = lax.axis_index("gy") % 2
    half_slots = own.shape[0]
    both[side] = own[...]
    both[1 - side] = other[...]
    half = own.shape[2] // 2
    for s in range(2 * half_slots):
        block = both[s // half_slots, s % half_slots].T * scale_ref[s]
        rounded = block.astype(jnp.bfloat16)
        if s < 9:
            grad_ref[3 * s + 1] = rounded[:half]
            grad_ref[3 * s + 2] = rounded[half:]
        else:
            t = 2 * (s - 9)
            grad_ref[3 * t] = rounded[:half]
            if t + 1 < 9:
                grad_ref[3 * (t + 1)] = rounded[half:]
            else:
                bias_ref[...] = block[half : half + 8]


def local(features, kernel, offsets, upstream, grad_exponents):
    cells, cotangent = features[0], upstream[0]
    size_x, size_y, width = cells.shape
    half = width // 2
    rows = size_y + 2 * PAD
    parts = lax.axis_size("dp")
    share = half // parts
    y_side = lax.axis_index("gy") % 2
    x_side = lax.axis_index("gx") % 2

    def rim(start):
        return jnp.concatenate(
            [
                lax.dynamic_slice_in_dim(cells, start, RIM, axis=1),
                lax.dynamic_slice_in_dim(cotangent, start, RIM, axis=1),
            ],
            axis=1,
        )

    last = size_y - RIM
    y_near = swap(rim((1 - y_side) * last), "gy", 0)
    y_far = swap(rim(y_side * last), "gy", 1)

    def plane(index):
        near = lax.dynamic_slice_in_dim(y_near, index, 1, axis=0)[0, :RIM]
        far = lax.dynamic_slice_in_dim(y_far, index, 1, axis=0)[0, :RIM]
        body = lax.dynamic_slice_in_dim(cells, index, 1, axis=0)[0]
        blank = jnp.zeros((PAD - RIM, width), cells.dtype)
        left = jnp.where(y_side == 0, far, near)
        right = jnp.where(y_side == 0, near, far)
        return jnp.concatenate([blank, left, body, right, blank], axis=0)

    x_near = swap(plane((1 - x_side) * (size_x - 1)), "gx", 0)
    x_far = swap(plane(x_side * (size_x - 1)), "gx", 1)

    matrices = build_matrices(kernel)
    forward_weights = matrices.transpose(0, 2, 1, 3).reshape(3 * width, 3 * width)
    backward_weights = matrices[::-1, ::-1].transpose(0, 3, 1, 2).reshape(3 * width, 3 * width)
    bias = jnp.concatenate([offsets, offsets])[None, :]

    bf16, f32 = jnp.bfloat16, jnp.float32
    activation, grad, edge_near, edge_far, keep, send = pl.pallas_call(
        main_kernel,
        out_shape=(
            jax.ShapeDtypeStruct((size_x, size_y, width), bf16),
            jax.ShapeDtypeStruct((size_x, rows, width), bf16),
            jax.ShapeDtypeStruct((rows, width), bf16),
            jax.ShapeDtypeStruct((rows, width), bf16),
            jax.ShapeDtypeStruct((parts, 7, share, width), f32),
            jax.ShapeDtypeStruct((parts, 7, share, width), f32),
        ),
        in_specs=[HBM, HBM] + [VMEM] * 6,
        out_specs=(HBM, HBM) + (VMEM,) * 4,
        scratch_shapes=[
            pltpu.VMEM((size_x + 2, rows, width), bf16),
            pltpu.VMEM((size_x, rows, width), bf16),
            pltpu.VMEM((size_x, size_y, width), bf16),
            pltpu.VMEM((size_x, rows, width), bf16),
            pltpu.VMEM((size_x + 2, width, size_y), bf16),
            pltpu.VMEM((3 * width, 3 * width), f32),
            pltpu.SemaphoreType.DMA((2, size_x)),
            pltpu.SemaphoreType.DMA((2, size_x)),
        ],
        compiler_params=pltpu.CompilerParams(vmem_limit_bytes=32 * 2**20),
        name="forward_and_weight_grad",
    )(cells, cotangent, y_near, y_far, x_near, x_far, forward_weights, bias)

    back_near = swap(edge_near, "gx", 0)
    back_far = swap(edge_far, "gx", 1)
    input_grad = pl.pallas_call(
        back_kernel,
        out_shape=jax.ShapeDtypeStruct((size_x, size_y, width), bf16),
        in_specs=[HBM] + [VMEM] * 3,
        out_specs=HBM,
        scratch_shapes=[
            pltpu.VMEM((size_x + 2, rows, width), bf16),
            pltpu.VMEM((size_x, size_y, width), bf16),
            pltpu.SemaphoreType.DMA((size_x,)),
            pltpu.SemaphoreType.DMA((size_x,)),
        ],
        compiler_params=pltpu.CompilerParams(vmem_limit_bytes=32 * 2**20),
        cost_estimate=pl.CostEstimate(
            flops=2 * 9 * size_x * size_y * width * width,
            bytes_accessed=4 * size_x * size_y * width,
            transcendentals=0,
        ),
        name="input_grad",
    )(grad, back_near, back_far, backward_weights)

    total = keep + swap(send, "gy", 0)
    me = lax.axis_index("dp")
    step = 1
    while step < parts:
        paired = total.reshape(total.shape[0] // 2, 2, 7, share, width)
        bit = (me // step) % 2
        mine = lax.dynamic_index_in_dim(paired, bit, 1, keepdims=False)
        theirs = lax.dynamic_index_in_dim(paired, 1 - bit, 1, keepdims=False)
        total = mine + exchange(theirs, "dp", step)
        step *= 2
    total = total[0]
    step = 2
    while step < lax.axis_size("gy"):
        total = total + exchange(total, "gy", step)
        step *= 2
    step = 1
    while step < lax.axis_size("gx"):
        total = total + exchange(total, "gx", step)
        step *= 2
    other = swap(total, "gy", 0)

    voxels = (
        features.shape[0] * parts * size_x * lax.axis_size("gx") * size_y * lax.axis_size("gy") * 2
    )
    inverse = 1.0 / math.sqrt(voxels)
    scales = jnp.exp2(grad_exponents.astype(f32)).reshape(9, 3) * inverse
    pairs = jnp.concatenate([scales[:, 0], jnp.full((1,), inverse, f32)]).reshape(5, 2)
    scales = jnp.concatenate([scales[:, 1:], pairs])
    scales = jnp.broadcast_to(jnp.repeat(scales, half, axis=1)[:, :, None], (14, width, share))
    kernel_grad, bias_grad = pl.pallas_call(
        finish_kernel,
        out_shape=(
            jax.ShapeDtypeStruct((27, half, share), bf16),
            jax.ShapeDtypeStruct((8, share), f32),
        ),
        in_specs=[VMEM] * 3,
        out_specs=(VMEM, VMEM),
        scratch_shapes=[pltpu.VMEM((2, 7, share, width), f32)],
        name="scale_weight_grad",
    )(total, other, scales)
    return (
        activation[None],
        input_grad[None],
        kernel_grad.reshape(3, 3, 3, half, share),
        bias_grad[0],
    )


def solution(mesh):
    placed = (P("dp", "gx", "gy", None), P(), P(), P("dp", "gx", "gy", None), P())
    return jax.shard_map(
        local,
        mesh=mesh,
        in_specs=placed,
        out_specs=(
            P("dp", "gx", "gy", None),
            P("dp", "gx", "gy", None),
            P(None, None, None, None, "dp"),
            P("dp"),
        ),
        check_vma=False,
    )
```

time: 156 us -> 63.1 us (0.40)
  matrix products: 35.6 us -> 0 us
  waiting for transfers between devices: 46.1 us -> 10.9 us
  blocking collectives: 25.8 us -> 0 us
  Pallas kernels: 0 us -> 23.9 us
  between operations: 15 us -> 1.03 us
  other arithmetic: 7.35 us -> 1.61 us
  starting transfers between devices: 19.5 us -> 15.9 us
  local copies, waits for them, and re-layouts: 5.83 us -> 9.28 us
    psum x1 -> x0, waiting for transfers between devices: 45.8 us -> none  [local(): tap_grad, bias_sum = lax.psum((tap_grad, bias_sum), ('gx', 'gy'))]
    dot_general x27 -> x0, matrix products: 35.6 us -> none  [the longest x9 22 us: backward_conv(): jnp.einsum('sxyd,cd->sxyc', window, matrices[shift_x, shift_y], preferred...]
    pallas_call x0 -> x3, Pallas kernels: none -> 23.9 us  [the longest x1 14.1 us: local(): pl.pallas_call(main_kernel, out_shape=(jax.ShapeDtypeStruct((size_x, size...]
    psum x1 -> x0, blocking collectives: 13.8 us -> none  [local(): tap_grad, bias_sum = lax.psum((tap_grad, bias_sum), ('gx', 'gy'))]
    unnamed x1 -> x0, blocking collectives: 11.9 us -> none
    ppermute x8 -> x10, waiting for transfers between devices: 0.29 us -> 10.9 us  [the longest x4 7.74 us: exchange(): lax.ppermute(value, axis, [(i, i ^ step) for i in range(lax.axis_size(axi...]
    convert_element_type x2 -> x0, other arithmetic: 4.83 us -> none  [the longest x1 3.15 us: local(): activation = (preact * sigma).astype(jnp.bfloat16)]
    ppermute x8 -> x10, starting transfers between devices: 19.4 us -> 15.9 us  [the longest x4 8.3 us: exchange(): lax.ppermute(value, axis, [(i, i ^ step) for i in range(lax.axis_size(axi...]
  transfers between devices with their start and end apart: 10 -> 10, of which waited for: 2 -> 6; matrix products, arithmetic and copies ran while one was open for 25% -> 6% of each run, Pallas kernels for 0% -> 12%
where the time goes in v1:
time: 63.1 us; the launch traced here: 62.6 us
  Pallas kernels  23.9 us (38%)
  starting transfers between devices  15.9 us (25%)
  waiting for transfers between devices  10.9 us (17%)
  local copies, waits for them, and re-layouts  9.28 us (15%)
  other arithmetic  1.61 us (3%)
  between operations  1.03 us (2%)
    pallas_call x1, Pallas kernels, local(): pl.pallas_call(main_kernel, out_shape=(jax.ShapeDtypeStruct((size_x, size...  14.1 us
    ppermute x4, starting transfers between devices, exchange(): lax.ppermute(value, axis, [(i, i ^ step) for i in range(lax.axis_size(axi...  8.3 us
    ppermute x4, waiting for transfers between devices, exchange(): lax.ppermute(value, axis, [(i, i ^ step) for i in range(lax.axis_size(axi...  7.74 us
    ppermute x6, starting transfers between devices, swap(): return lax.ppermute(value, axis, links)  7.59 us
    pallas_call x1, Pallas kernels, local(): pl.pallas_call(back_kernel, out_shape=jax.ShapeDtypeStruct((size_x, size_...  7.48 us
    unnamed x23, local copies, waits for them, and re-layouts  3.71 us
    ppermute x6, waiting for transfers between devices, swap(): return lax.ppermute(value, axis, links)  3.12 us
    pallas_call x1, Pallas kernels, local(): pl.pallas_call(finish_kernel, out_shape=(jax.ShapeDtypeStruct((27, half,...  2.35 us
  transfers between devices with their start and end apart: 10, of which 6 were waited for; matrix products, arithmetic and copies ran while one was open for 6% of the time, Pallas kernels for 12%

profile of v1, /device:TPU:0, one launch (start us, length us, event | category | flops | bytes accessed | tf_op | source)
XLA Modules:
  0.0 62.6 jit_solution(1763509721633085614)
XLA Ops:
  0.7 0.8 %dynamic-slice_bitcast_fusion.1 = (bf16[16,8,128]{2,1,0:T(8,128)(2,1)S(1)}, bf16[16,8,128]{2,1,0:T(8,128)(2,1)S(1)}, bf16[16,8,128]{2,1,0:T(8,128)(2,1)S(1)}, bf16[16,8,128]{2,1,0:T(8,128)(2,1)S(1)}) fusion(bf16[1,16,256,128]{3,2,1,0:T(8,128)(2,1)} %param.8, s32[]{:T(128)S(6)} %select_n.71, s32[]{:T(128)S(6)} %select_n.70, bf16[1,16,256,128]{3,2,1,0:T(8,128)(2,1)} %param.5), kind=kLoop, calls=%fused_computation.13 | loop fusion | bytes 262152 | tf_op jit(solution)/shard_map/dynamic_slice | solution.py:242
  1.5 0.5 collective-permute-start
  2.0 0.7 %collective-permute-start.1 = (bf16[16,16,128]{2,1,0:T(8,128)(2,1)S(1)}, bf16[16,16,128]{2,1,0:T(8,128)(2,1)S(1)}, u32[]{:S(2)}, u32[]{:S(2)}) collective-permute-start(bf16[16,16,128]{2,1,0:T(8,128)(2,1)S(1)} %pad_maximum_fusion.1), channel_id=1, source_target_pairs={{4,8},{8,4},{5,9},{9,5},{6,10},{10,6},{7,11},{11,7},{20,24},{24,20... | collective-permute-start | bytes 196616 | tf_op jit(solution)/shard_map/ppermute | solution.py:23
  2.7 1.1 %slice_bitcast_fusion.1 = (bf16[3,3,64,64]{3,2,1,0:T(8,128)(2,1)S(1)}, bf16[3,3,64,64]{3,2,1,0:T(8,128)(2,1)S(1)}, bf16[3,3,64,64]{3,2,1,0:T(8,128)(2,1)S(1)}) fusion(bf16[3,3,3,64,64]{4,3,2,1,0:T(8,128)(2,1)} %param.6), kind=kLoop, calls=%fused_computation.5 | loop fusion | bytes 442368 | tf_op jit(solution)/shard_map/squeeze | solution.py:31
  3.8 0.0 copy-start.4
  3.8 0.0 copy-start
  3.8 0.0 copy-start.8
  3.9 0.0 copy-start.1
  3.9 0.6 copy-done.4
  4.5 0.2 fusion
  4.7 0.3 copy.21
  5.0 0.0 collective-permute-done.y_near
  5.0 0.0 collective-permute-done.1.y_far
  5.0 0.1 copy-done
  5.2 2.6 %collective-permute-start.2 = (bf16[288,128]{1,0:T(8,128)(2,1)S(1)}, bf16[288,128]{1,0:T(8,128)(2,1)S(1)}, u32[]{:S(2)}, u32[]{:S(2)}) collective-permute-start(bf16[288,128]{1,0:T(8,128)(2,1)S(1)} %constant_dynamic-update-slice_fusion), channel_id=1, source_target_pairs={{0,16},{16,0},{1,17},{17,1},{2,18},{18,2},{3,19},{19,3},{4,20},{20... | collective-permute-start | bytes 221192 | tf_op jit(solution)/shard_map/ppermute | solution.py:23
  7.7 0.0 copy-done.8
  7.7 0.1 maximum_bitcast_fusion.bias_ref
  7.8 2.3 %collective-permute-done.2.x_near = bf16[288,128]{1,0:T(8,128)(2,1)S(1)} collective-permute-done((bf16[288,128]{1,0:T(8,128)(2,1)S(1)}, bf16[288,128]{1,0:T(8,128)(2,1)S(1)}, u32[]{:S(2)}, u32[]{:S(2)}) %collective-permute-start.2) | collective-permute-done | bytes 73760 | tf_op jit(solution)/shard_map/ppermute | solution.py:23
  10.1 0.0 copy-done.1
  10.1 0.0 copy-start.7
  10.1 14.1 %forward_and_weight_grad.1 = (bf16[16,256,128]{2,1,0:T(8,128)(2,1)}, bf16[16,288,128]{2,1,0:T(8,128)(2,1)S(1)}, bf16[288,128]{1,0:T(8,128)(2,1)S(1)}, bf16[288,1...) custom-call(bf16[16,256,128]{2,1,0:T(8,128)(2,1)S(1)} %bitcast.62, ...), custom_call_target="tpu_custom_call" | custom-call | tf_op jit(solution)/shard_map/forward_and_weight_grad/pallas_call | solution.py:269
  24.2 0.0 copy-start.2
  24.2 1.0 %copy-done.2 = bf16[16,288,128]{2,1,0:T(8,128)(2,1)} copy-done((bf16[16,288,128]{2,1,0:T(8,128)(2,1)}, bf16[16,288,128]{2,1,0:T(8,128)(2,1)S(1)}, u32[]{:S(2)}) %copy-start.2) | copy-done | bytes 1179672
  25.2 2.3 %collective-permute-start.4 = (f32[4,7,16,128]{3,2,1,0:T(8,128)S(1)}, f32[4,7,16,128]{3,2,1,0:T(8,128)S(1)}, u32[]{:S(2)}, u32[]{:S(2)}) collective-permute-start(f32[4,7,16,128]{3,2,1,0:T(8,128)S(1)} %get-tuple-element.15), channel_id=1, source_target_pairs={{0,4},{4,0},{8,12},{12,8},{1,5},{5,1},{9,13},{13,9},{2,6},{6,2},{1... | collective-permute-start | bytes 688136 | tf_op jit(solution)/shard_map/ppermute | solution.py:23
  27.5 0.0 copy-done.7
  27.6 0.1 copy.25
  27.7 0.1 mul.19
  27.8 0.9 %collective-permute-done.4 = f32[4,7,16,128]{3,2,1,0:T(8,128)S(1)} collective-permute-done((f32[4,7,16,128]{3,2,1,0:T(8,128)S(1)}, f32[4,7,16,128]{3,2,1,0:T(8,128)S(1)}, u32[]{:S(2)}, u32[]{:S(2)}) %collective-permute-start.4) | collective-permute-done | bytes 229408 | tf_op jit(solution)/shard_map/ppermute | solution.py:23
  28.7 1.8 %collective-permute-start.5 = (f32[2,7,16,128]{3,2,1,0:T(8,128)S(1)}, f32[2,7,16,128]{3,2,1,0:T(8,128)S(1)}, u32[]{:S(2)}, u32[]{:S(2)}) collective-permute-start(f32[2,7,16,128]{3,2,1,0:T(8,128)S(1)} %dynamic-slice_bitcast_fusion), channel_id=1, source_target_pairs={{0,1},{1,0},{2,3},{3,2},{4,5},{5,4},{6,7},{7,6},{8,9},{9,8},{10,11... | collective-permute-start | bytes 344072 | tf_op jit(solution)/shard_map/ppermute | solution.py:27
  30.5 1.1 %maximum_maximum_fusion = bf16[3,3,128,128]{3,2,1,0:T(8,128)(2,1)S(1)} fusion(bf16[3,3,64,64]{3,2,1,0:T(8,128)(2,1)S(1)} %get-tuple-element.31, bf16[3,3,64,64]{3,2,1,0:T(8,128)(2,1)} %copy-done.4, bf16[3,3,64,64]{3,2,1,0:T(8,128)(2,1)S(1)} %get-tuple-element.30), kind=kLoop, calls=%fused_computation.2 | loop fusion | flops 1179648 | bytes 516096 | tf_op jit(solution)/shard_map/concatenate | solution.py:33
  31.6 2.6 %collective-permute-done.5 = f32[2,7,16,128]{3,2,1,0:T(8,128)S(1)} collective-permute-done((f32[2,7,16,128]{3,2,1,0:T(8,128)S(1)}, f32[2,7,16,128]{3,2,1,0:T(8,128)S(1)}, u32[]{:S(2)}, u32[]{:S(2)}) %collective-permute-start.5) | collective-permute-done | bytes 114720 | tf_op jit(solution)/shard_map/ppermute | solution.py:27
  34.2 0.0 copy-start.3
  34.2 2.8 %collective-permute-start.6 = (f32[1,7,16,128]{3,2,1,0:T(8,128)S(1)}, f32[1,7,16,128]{3,2,1,0:T(8,128)S(1)}, u32[]{:S(2)}, u32[]{:S(2)}) collective-permute-start(f32[1,7,16,128]{3,2,1,0:T(8,128)S(1)} %constant_dynamic-slice_fusion), channel_id=1, source_target_pairs={{0,2},{1,3},{2,0},{3,1},{4,6},{5,7},{6,4},{7,5},{8,10},{9,11},{10,... | collective-permute-start | bytes 172040 | tf_op jit(solution)/shard_map/ppermute | solution.py:27
  37.1 0.2 copy.22
  37.4 2.3 %collective-permute-done.6 = f32[1,7,16,128]{3,2,1,0:T(8,128)S(1)} collective-permute-done((f32[1,7,16,128]{3,2,1,0:T(8,128)S(1)}, f32[1,7,16,128]{3,2,1,0:T(8,128)S(1)}, u32[]{:S(2)}, u32[]{:S(2)}) %collective-permute-start.6) | collective-permute-done | bytes 57376 | tf_op jit(solution)/shard_map/ppermute | solution.py:27
  39.7 2.2 %collective-permute-start.7 = (f32[7,16,128]{2,1,0:T(8,128)S(1)}, f32[7,16,128]{2,1,0:T(8,128)S(1)}, u32[]{:S(2)}, u32[]{:S(2)}) collective-permute-start(f32[7,16,128]{2,1,0:T(8,128)S(1)} %add_bitcast_fusion), channel_id=1, source_target_pairs={{0,8},{4,12},{8,0},{12,4},{1,9},{5,13},{9,1},{13,5},{2,10},{6,14},... | collective-permute-start | bytes 172040 | tf_op jit(solution)/shard_map/ppermute | solution.py:27
  41.9 0.1 pad_maximum_fusion.3
  42.0 0.1 reshape.45
  42.1 0.1 copy.26
  42.2 1.5 %collective-permute-start.3 = (bf16[288,128]{1,0:T(8,128)(2,1)S(1)}, bf16[288,128]{1,0:T(8,128)(2,1)S(1)}, u32[]{:S(2)}, u32[]{:S(2)}) collective-permute-start(bf16[288,128]{1,0:T(8,128)(2,1)S(1)} %get-tuple-element.13), channel_id=1, source_target_pairs={{0,16},{16,0},{1,17},{17,1},{2,18},{18,2},{3,19},{19,3},{4,20},{20... | collective-permute-start | bytes 221192 | tf_op jit(solution)/shard_map/ppermute | solution.py:23
  43.6 0.4 collective-permute-done.7
  44.1 1.6 %collective-permute-start.8 = (f32[7,16,128]{2,1,0:T(8,128)S(1)}, f32[7,16,128]{2,1,0:T(8,128)S(1)}, u32[]{:S(2)}, u32[]{:S(2)}) collective-permute-start(f32[7,16,128]{2,1,0:T(8,128)S(1)} %add.73), channel_id=1, source_target_pairs={{0,16},{16,0},{1,17},{17,1},{2,18},{18,2},{3,19},{19,3},{4,20},{20... | collective-permute-start | bytes 172040 | tf_op jit(solution)/shard_map/ppermute | solution.py:27
  45.6 0.1 pad_maximum_fusion.2
  45.7 0.1 copy.27
  45.8 0.1 broadcast_in_dim.26
  45.9 0.1 broadcast_in_dim.27
  46.0 2.4 %collective-permute-done.8 = f32[7,16,128]{2,1,0:T(8,128)S(1)} collective-permute-done((f32[7,16,128]{2,1,0:T(8,128)S(1)}, f32[7,16,128]{2,1,0:T(8,128)S(1)}, u32[]{:S(2)}, u32[]{:S(2)}) %collective-permute-start.8) | collective-permute-done | bytes 57376 | tf_op jit(solution)/shard_map/ppermute | solution.py:27
  48.3 0.0 copy-start.5
  48.3 0.1 collective-permute-start.9
  48.4 0.0 collective-permute-done.3.x_near
  48.4 0.0 copy-done.3
  48.4 7.5 %input_grad.1 = bf16[16,256,128]{2,1,0:T(8,128)(2,1)} custom-call(bf16[16,288,128]{2,1,0:T(8,128)(2,1)S(1)} %copy-done.3, bf16[288,128]{1,0:T(8,128)(2,1)S(1)} %collective-permute-done.3.x_near, bf16[288,128]{1,0:T(8,128)(2,1)S(1)} %broadcast_5_x_far.2.x_far, bf16[384,384]{1,0:T(8,128)(2,1)S(1)} %bitcast.65), custom_call_target="tpu_custom_call" | custom-call | flops 1207959552 | bytes 2097152 | tf_op jit(solution)/shard_map/input_grad/pallas_call | solution.py:297
  55.9 0.0 copy-done.5
  55.9 0.0 collective-permute-done.9.other
  55.9 0.0 copy-start.6
  56.0 1.2 %broadcast_in_dim.28.scale_ref = f32[14,128,16]{2,1,0:T(8,128)} broadcast(f32[14,128]{1,0:T(8,128)S(1)} %broadcast_in_dim.27), dimensions={0,1} | broadcast | bytes 121856 | tf_op jit(solution)/shard_map/broadcast_in_dim | solution.py:345
  57.2 0.0 copy-done.6
  57.2 2.4 %scale_weight_grad.1 = (bf16[27,64,16]{2,1,0:T(8,128)(2,1)}, f32[8,16]{1,0:T(8,128)}) custom-call(f32[7,16,128]{2,1,0:T(8,128)} %copy-done.5, f32[7,16,128]{2,1,0:T(8,128)} %copy-done.6, f32[14,128,16]{2,1,0:T(8,128)} %broadcast_in_dim.28.scale_ref), custom_call_target="tpu_custom_call" | custom-call | tf_op jit(solution)/shard_map/scale_weight_grad/pallas_call | solution.py:346
  59.6 1.8 %copy.28 = bf16[3,3,3,64,16]{3,4,2,1,0:T(8,128)(2,1)} copy(bf16[3,3,3,64,16]{4,3,2,1,0:T(8,128)(2,1)} %bitcast.70) | data formatting | bytes 110592
  61.4 1.2 %slice_bitcast_fusion.3 = f32[16]{0:T(128)} fusion(f32[8,16]{1,0:T(8,128)} %get-tuple-element.17), kind=kLoop, calls=%fused_computation.28 | loop fusion | bytes 128 | tf_op jit(solution)/shard_map/squeeze | solution.py:361
  (21 shorter events, 0.3 us)
Async XLA Ops:
  1.5 3.5 %collective-permute-start = (bf16[16,16,128]{2,1,0:T(8,128)(2,1)S(1)}, bf16[16,16,128]{2,1,0:T(8,128)(2,1)S(1)}, u32[]{:S(2)}, u32[]{:S(2)}) collective-permute-start(bf16[16,16,128]{2,1,0:T(8,128)(2,1)S(1)} %pad_maximum_fusion), channel_id=1, source_target_pairs={{0,4},{4,0},{8,12},{12,8},{1,5},{5,1},{9,13},{13,9},{2,6},{6,2},{1... | collective-permute-start | bytes 196616 | tf_op jit(solution)/shard_map/ppermute | solution.py:23
  2.0 3.0 %collective-permute-start.1 = (bf16[16,16,128]{2,1,0:T(8,128)(2,1)S(1)}, bf16[16,16,128]{2,1,0:T(8,128)(2,1)S(1)}, u32[]{:S(2)}, u32[]{:S(2)}) collective-permute-start(bf16[16,16,128]{2,1,0:T(8,128)(2,1)S(1)} %pad_maximum_fusion.1), channel_id=1, source_target_pairs={{4,8},{8,4},{5,9},{9,5},{6,10},{10,6},{7,11},{11,7},{20,24},{24,20... | collective-permute-start | bytes 196616 | tf_op jit(solution)/shard_map/ppermute | solution.py:23
  3.8 0.7 %copy-start.4 = (bf16[3,3,64,64]{3,2,1,0:T(8,128)(2,1)}, bf16[3,3,64,64]{3,2,1,0:T(8,128)(2,1)S(1)}, u32[]{:S(2)}) copy-start(bf16[3,3,64,64]{3,2,1,0:T(8,128)(2,1)S(1)} %get-tuple-element.32) | copy-start | bytes 221188
  3.8 1.3 %copy-start = (bf16[1,16,256,128]{3,2,1,0:T(8,128)(2,1)S(1)}, bf16[1,16,256,128]{3,2,1,0:T(8,128)(2,1)}, u32[]{:S(2)}) copy-start(bf16[1,16,256,128]{3,2,1,0:T(8,128)(2,1)} %param.5) | copy-start | bytes 3145732
  3.8 3.9 %copy-start.8 = (f32[64]{0:T(128)S(1)}, f32[64]{0:T(128)}, u32[]{:S(2)}) copy-start(f32[64]{0:T(128)} %param.7) | copy-start | bytes 772
  3.9 6.2 %copy-start.1 = (bf16[1,16,256,128]{3,2,1,0:T(8,128)(2,1)S(1)}, bf16[1,16,256,128]{3,2,1,0:T(8,128)(2,1)}, u32[]{:S(2)}) copy-start(bf16[1,16,256,128]{3,2,1,0:T(8,128)(2,1)} %param.8) | copy-start | bytes 3145732
  5.2 4.9 %collective-permute-start.2 = (bf16[288,128]{1,0:T(8,128)(2,1)S(1)}, bf16[288,128]{1,0:T(8,128)(2,1)S(1)}, u32[]{:S(2)}, u32[]{:S(2)}) collective-permute-start(bf16[288,128]{1,0:T(8,128)(2,1)S(1)} %constant_dynamic-update-slice_fusion), channel_id=1, source_target_pairs={{0,16},{16,0},{1,17},{17,1},{2,18},{18,2},{3,19},{19,3},{4,20},{20... | collective-permute-start | bytes 221192 | tf_op jit(solution)/shard_map/ppermute | solution.py:23
  10.1 17.4 %copy-start.7 = (s32[3,3,3]{2,1,0:T(4,128)S(1)}, s32[3,3,3]{2,1,0:T(4,128)}, u32[]{:S(2)}) copy-start(s32[3,3,3]{2,1,0:T(4,128)} %param.9) | copy-start | bytes 328
  24.2 1.0 %copy-start.2 = (bf16[16,288,128]{2,1,0:T(8,128)(2,1)}, bf16[16,288,128]{2,1,0:T(8,128)(2,1)S(1)}, u32[]{:S(2)}) copy-start(bf16[16,288,128]{2,1,0:T(8,128)(2,1)S(1)} %get-tuple-element.12.grad_hbm) | copy-start | bytes 3538948
  25.2 3.4 %collective-permute-start.4 = (f32[4,7,16,128]{3,2,1,0:T(8,128)S(1)}, f32[4,7,16,128]{3,2,1,0:T(8,128)S(1)}, u32[]{:S(2)}, u32[]{:S(2)}) collective-permute-start(f32[4,7,16,128]{3,2,1,0:T(8,128)S(1)} %get-tuple-element.15), channel_id=1, source_target_pairs={{0,4},{4,0},{8,12},{12,8},{1,5},{5,1},{9,13},{13,9},{2,6},{6,2},{1... | collective-permute-start | bytes 688136 | tf_op jit(solution)/shard_map/ppermute | solution.py:23
  28.7 5.5 %collective-permute-start.5 = (f32[2,7,16,128]{3,2,1,0:T(8,128)S(1)}, f32[2,7,16,128]{3,2,1,0:T(8,128)S(1)}, u32[]{:S(2)}, u32[]{:S(2)}) collective-permute-start(f32[2,7,16,128]{3,2,1,0:T(8,128)S(1)} %dynamic-slice_bitcast_fusion), channel_id=1, source_target_pairs={{0,1},{1,0},{2,3},{3,2},{4,5},{5,4},{6,7},{7,6},{8,9},{9,8},{10,11... | collective-permute-start | bytes 344072 | tf_op jit(solution)/shard_map/ppermute | solution.py:27
  34.2 14.2 %copy-start.3 = (bf16[16,288,128]{2,1,0:T(8,128)(2,1)S(1)}, bf16[16,288,128]{2,1,0:T(8,128)(2,1)}, u32[]{:S(2)}) copy-start(bf16[16,288,128]{2,1,0:T(8,128)(2,1)} %copy-done.2) | copy-start | bytes 3538948
  34.2 5.5 %collective-permute-start.6 = (f32[1,7,16,128]{3,2,1,0:T(8,128)S(1)}, f32[1,7,16,128]{3,2,1,0:T(8,128)S(1)}, u32[]{:S(2)}, u32[]{:S(2)}) collective-permute-start(f32[1,7,16,128]{3,2,1,0:T(8,128)S(1)} %constant_dynamic-slice_fusion), channel_id=1, source_target_pairs={{0,2},{1,3},{2,0},{3,1},{4,6},{5,7},{6,4},{7,5},{8,10},{9,11},{10,... | collective-permute-start | bytes 172040 | tf_op jit(solution)/shard_map/ppermute | solution.py:27
  39.7 4.3 %collective-permute-start.7 = (f32[7,16,128]{2,1,0:T(8,128)S(1)}, f32[7,16,128]{2,1,0:T(8,128)S(1)}, u32[]{:S(2)}, u32[]{:S(2)}) collective-permute-start(f32[7,16,128]{2,1,0:T(8,128)S(1)} %add_bitcast_fusion), channel_id=1, source_target_pairs={{0,8},{4,12},{8,0},{12,4},{1,9},{5,13},{9,1},{13,5},{2,10},{6,14},... | collective-permute-start | bytes 172040 | tf_op jit(solution)/shard_map/ppermute | solution.py:27
  42.2 6.3 %collective-permute-start.3 = (bf16[288,128]{1,0:T(8,128)(2,1)S(1)}, bf16[288,128]{1,0:T(8,128)(2,1)S(1)}, u32[]{:S(2)}, u32[]{:S(2)}) collective-permute-start(bf16[288,128]{1,0:T(8,128)(2,1)S(1)} %get-tuple-element.13), channel_id=1, source_target_pairs={{0,16},{16,0},{1,17},{17,1},{2,18},{18,2},{3,19},{19,3},{4,20},{20... | collective-permute-start | bytes 221192 | tf_op jit(solution)/shard_map/ppermute | solution.py:23
  44.1 4.2 %collective-permute-start.8 = (f32[7,16,128]{2,1,0:T(8,128)S(1)}, f32[7,16,128]{2,1,0:T(8,128)S(1)}, u32[]{:S(2)}, u32[]{:S(2)}) collective-permute-start(f32[7,16,128]{2,1,0:T(8,128)S(1)} %add.73), channel_id=1, source_target_pairs={{0,16},{16,0},{1,17},{17,1},{2,18},{18,2},{3,19},{19,3},{4,20},{20... | collective-permute-start | bytes 172040 | tf_op jit(solution)/shard_map/ppermute | solution.py:27
  48.3 7.6 %copy-start.5 = (f32[7,16,128]{2,1,0:T(8,128)}, f32[7,16,128]{2,1,0:T(8,128)S(1)}, u32[]{:S(2)}) copy-start(f32[7,16,128]{2,1,0:T(8,128)S(1)} %add.74.own) | copy-start | bytes 172036
  48.3 7.6 %collective-permute-start.9 = (f32[7,16,128]{2,1,0:T(8,128)S(1)}, f32[7,16,128]{2,1,0:T(8,128)S(1)}, u32[]{:S(2)}, u32[]{:S(2)}) collective-permute-start(f32[7,16,128]{2,1,0:T(8,128)S(1)} %add.74.own), channel_id=1, source_target_pairs={{0,4},{4,0},{8,12},{12,8},{1,5},{5,1},{9,13},{13,9},{2,6},{6,2},{1... | collective-permute-start | bytes 172040 | tf_op jit(solution)/shard_map/ppermute | solution.py:23
  55.9 1.3 %copy-start.6 = (f32[7,16,128]{2,1,0:T(8,128)}, f32[7,16,128]{2,1,0:T(8,128)S(1)}, u32[]{:S(2)}) copy-start(f32[7,16,128]{2,1,0:T(8,128)S(1)} %collective-permute-done.9.other) | copy-start | bytes 172036

commit v2 on v0

v2 whole, which is shorter than its diff:
```python
import math

import jax
import jax.numpy as jnp
from jax import lax
from jax.experimental import pallas as pl
from jax.experimental.pallas import tpu as pltpu
from jax.sharding import PartitionSpec as P

RIM = 8
PAD = 16
CHUNK = 64
SLOTS = 14
VMEM = pl.BlockSpec(memory_space=pltpu.VMEM)
SMEM = pl.BlockSpec(memory_space=pltpu.SMEM)
ANY = pl.BlockSpec(memory_space=pl.ANY)
PARAMS = pltpu.CompilerParams(vmem_limit_bytes=32 * 2**20)
BF16, F32 = jnp.bfloat16, jnp.float32


def swap(value, axis, first):
    count = lax.axis_size(axis)
    links = []
    for low in range(first, count - 1, 2):
        links += [(low, low + 1), (low + 1, low)]
    if not links:
        return jnp.zeros_like(value)
    return lax.ppermute(value, axis, links)


def exchange(value, axis, step):
    return lax.ppermute(value, axis, [(i, i ^ step) for i in range(lax.axis_size(axis))])


def weights_kernel(taps, ahead, back):
    half = taps.shape[3]
    width = 2 * half
    for out in (ahead, back):
        out[...] = jnp.zeros(out.shape, BF16)
    for a in range(3):
        for b in range(3):
            low, mid, high = taps[a, b, 0], taps[a, b, 1], taps[a, b, 2]
            block = jnp.concatenate(
                [jnp.concatenate([mid, low], axis=1), jnp.concatenate([high, mid], axis=1)], axis=0
            )
            turned = block.T
            for k in range(2):
                row, col = (a + k) * width, (3 * k + b) * width
                ahead[row : row + width, col : col + width] = block
                row, col = (2 - a + k) * width, (3 * k + 2 - b) * width
                back[row : row + width, col : col + width] = turned


def plane_taps(taps, slots, bodies, weights):
    size_y, width = bodies[0].shape
    result = jnp.dot(
        jnp.concatenate(bodies, axis=1), weights, preferred_element_type=F32
    )
    for k, p in enumerate(slots):
        for b in range(3):
            col = (3 * k + b) * width
            taps[b, p, PAD : PAD + size_y, :] = result[:, col : col + width]


def rim_taps(taps, slots, triples, weights):
    width = triples[0][0].shape[1]
    rows = 2 * RIM
    last = taps.shape[2] - PAD
    stacked = jnp.concatenate(
        [jnp.concatenate([triple[j] for triple in triples], axis=0) for j in range(3)], axis=1
    )
    result = jnp.dot(stacked, weights, preferred_element_type=F32)
    for k, p in enumerate(slots):
        for b in range(3):
            block = result[k * rows : (k + 1) * rows, b * width : (b + 1) * width]
            taps[b, p, PAD - RIM : PAD, :] = block[:RIM]
            taps[b, p, last : last + RIM, :] = block[RIM:]


def shifted_sum(taps, p, start, rows):
    return (
        taps[0, p, start - 1 : start - 1 + rows, :]
        + taps[1, p, start : start + rows, :]
        + taps[2, p, start + 1 : start + 1 + rows, :]
    )


def activate(taps, wide, p, bias, sums, u_body, u_rim, act, grad_body, grad_rim):
    size_y = taps.shape[2] - 2 * PAD
    spans = [(PAD - RIM, RIM)]
    spans += [(PAD + y, CHUNK) for y in range(0, size_y, CHUNK)]
    spans += [(PAD + size_y, RIM)]
    for start, rows in spans:
        body = rows == CHUNK
        y = start - PAD if body else (0 if start < PAD else RIM)
        preact = shifted_sum(taps, p, start, rows) + bias
        sigma = 0.5 * jnp.tanh(0.5 * preact) + 0.5
        cotangent = (u_body if body else u_rim)[y : y + rows, :].astype(F32)
        rounded = (cotangent * sigma * (1.0 + preact * (1.0 - sigma))).astype(BF16)
        exact = rounded.astype(F32)
        wide[p, start : start + rows, :] = exact
        if body:
            act[y : y + rows, :] = (preact * sigma).astype(BF16)
            grad_body[y : y + rows, :] = rounded
            sums = sums + jnp.sum(exact.reshape(rows // 8, 8, exact.shape[1]), axis=0)
        else:
            grad_rim[y : y + rows, :] = rounded
    return sums


def shifted_grads(wide, p):
    size_y = wide.shape[1] - 2 * PAD
    return jnp.concatenate(
        [wide[p, PAD + 1 - b : PAD + 1 - b + size_y, :].astype(BF16) for b in range(3)], axis=1
    )


def outer(sources, grads):
    return jnp.dot(
        jnp.concatenate([jnp.concatenate(three, axis=0) for three in sources], axis=1),
        jnp.concatenate(grads, axis=0),
        preferred_element_type=F32,
    )


def oriented(near, far, side, place):
    @pl.when(side == 0)
    def _():
        place(far, near)

    @pl.when(side == 1)
    def _():
        place(near, far)


def place_rims(y_near, y_far, f_rim, u_rim):
    def place(left, right):
        f_rim[:, :RIM, :] = left[:, :RIM, :]
        f_rim[:, RIM:, :] = right[:, :RIM, :]
        u_rim[:, :RIM, :] = left[:, RIM:, :]
        u_rim[:, RIM:, :] = right[:, RIM:, :]

    oriented(y_near, y_far, lax.axis_index("gy") % 2, place)


def inner_kernel(
    f_ref, u_ref, y_near, y_far, w_ref, bias_ref,
    act_hbm, grad_ref, rim_ref, acc_ref, sums_ref,
    f_rim, u_rim, act, taps, wide, turned, sems,
):
    size_x, size_y, width = f_ref.shape
    inner = size_x - 2
    place_rims(y_near, y_far, f_rim, u_rim)
    bias = bias_ref[...]
    rim_taps(
        taps,
        range(inner),
        [[f_rim[x + j] for j in range(3)] for x in range(inner)],
        w_ref[: 3 * width, : 3 * width],
    )
    sums = jnp.zeros((8, width), F32)
    stores = []
    pairs = range(0, inner, 2)

    def multiply(p):
        plane_taps(taps, (p, p + 1), [f_ref[p + j] for j in range(4)], w_ref[...])
        for x in range(0 if p == 0 else p + 2, p + 4):
            turned[x] = f_ref[x].T

    multiply(0)
    for p in pairs:
        if p + 2 < inner:
            multiply(p + 2)
        for q in (p, p + 1):
            sums = activate(
                taps, wide, q, bias, sums, u_ref.at[q + 1], u_rim.at[q + 1],
                act.at[q], grad_ref.at[q], rim_ref.at[q],
            )
        stores.append(
            pltpu.make_async_copy(
                act.at[pl.ds(p, 2)], act_hbm.at[pl.ds(p + 1, 2)], sems.at[p // 2]
            )
        )
        stores[-1].start()
        term = outer(
            [[turned[q + j] for j in range(3)] for q in (p, p + 1)],
            [shifted_grads(wide, q) for q in (p, p + 1)],
        )
        if p == 0:
            acc_ref[...] = term
        else:
            acc_ref[...] += term
    sums_ref[...] = sums
    for copy in stores:
        copy.wait()


def edge_kernel(
    f_ref, u_ref, y_near, y_far, x_near, x_far, w_ref, bias_ref, acc_ref, sums_ref, act_in,
    act_hbm, first_ref, last_ref, near_ref, far_ref, keep_ref, send_ref,
    f_rim, u_rim, around, act, taps, wide, acc, sems,
):
    size_x, size_y, width = f_ref.shape
    half = width // 2
    parts, _, share, _ = keep_ref.shape
    y_side = lax.axis_index("gy") % 2
    x_side = lax.axis_index("gx") % 2
    place_rims(y_near, y_far, f_rim, u_rim)

    def place(below, above):
        around[0] = below[...]
        around[1] = above[...]

    oriented(x_near, x_far, x_side, place)
    bias = bias_ref[...]
    weights = w_ref[: 3 * width, : 3 * width]
    tall = size_y + 2 * RIM
    bodies = [
        [around[0, :size_y], f_ref[0], f_ref[1]],
        [f_ref[size_x - 2], f_ref[size_x - 1], around[1, :size_y]],
    ]
    rims = [
        [around[0, size_y:tall], f_rim[0], f_rim[1]],
        [f_rim[size_x - 2], f_rim[size_x - 1], around[1, size_y:tall]],
    ]
    rim_taps(taps, (0, 1), rims, weights)
    for p in range(2):
        plane_taps(taps, (p,), bodies[p], weights)
    sums = sums_ref[...]
    outs = (first_ref, last_ref)
    places = (0, size_x - 1)
    for p in range(2):
        x = places[p]
        sums = activate(
            taps, wide, p, bias, sums, u_ref.at[x], u_rim.at[x], act.at[p],
            outs[p].at[pl.ds(0, size_y)], outs[p].at[pl.ds(size_y, 2 * RIM)],
        )
    stores = [
        pltpu.make_async_copy(act.at[p], act_hbm.at[places[p]], sems.at[p]) for p in range(2)
    ]
    for copy in stores:
        copy.start()
    acc[...] = acc_ref[...] + outer(
        [[plane.T for plane in bodies[p]] for p in range(2)],
        [shifted_grads(wide, p) for p in range(2)],
    )

    def hand(second, first):
        first[...] = first_ref[...]
        second[...] = last_ref[...]

    oriented(far_ref, near_ref, x_side, lambda low, high: hand(low, high))

    lane = lax.broadcasted_iota(jnp.int32, (half, width), 1)
    lower = lane < half
    slots, tails = [], []
    for a in range(3):
        for b in range(3):
            block = acc[a * width : (a + 1) * width, b * width : (b + 1) * width].T
            top, bottom = block[:half], block[half:]
            rolled = pltpu.roll(bottom, half, 1)
            slots.append(top + jnp.where(lower, rolled, 0.0))
            tails.append((bottom, rolled))
    for t in range(0, 8, 2):
        slots.append(jnp.where(lower, tails[t][0], tails[t + 1][1]))
    both = jnp.sum(sums, axis=0, keepdims=True)
    both = jnp.broadcast_to(both + pltpu.roll(both, half, 1), (share, width))
    spare = [
        jnp.where(
            lower[:share],
            tails[8][0][d * share : (d + 1) * share],
            pltpu.roll(both, (half - d * share) % width, 1),
        )
        for d in range(parts)
    ]

    def emit(first, second):
        for s in range(SLOTS):
            out = first if s < SLOTS // 2 else second
            for d in range(parts):
                part = spare[d] if s == SLOTS - 1 else slots[s][d * share : (d + 1) * share]
                out[d, s % (SLOTS // 2)] = part

    @pl.when(y_side == 0)
    def _():
        emit(keep_ref, send_ref)

    @pl.when(y_side == 1)
    def _():
        emit(send_ref, keep_ref)

    for copy in stores:
        copy.wait()


def back_kernel(pairs, edges, grad_ref, rim_ref, first_ref, last_ref, *refs):
    x_near, x_far = refs[:2] if edges else (None, None)
    w_ref = refs[2 * edges]
    out_hbm, out, taps, around, sems = refs[-5:]
    size_y, width = grad_ref.shape[1:]
    size_x = grad_ref.shape[0] + 2
    tall = size_y + 2 * RIM

    def body(x):
        if x == 0:
            return first_ref[:size_y]
        if x == size_x - 1:
            return last_ref[:size_y]
        if x < 0 or x >= size_x:
            return around[int(x > 0), :size_y]
        return grad_ref[x - 1]

    def rim(x):
        if x == 0:
            return first_ref[size_y:tall]
        if x == size_x - 1:
            return last_ref[size_y:tall]
        if x < 0 or x >= size_x:
            return around[int(x > 0), size_y:tall]
        return rim_ref[x - 1]

    if edges:

        def place(below, above):
            around[0] = below[...]
            around[1] = above[...]

        oriented(x_near, x_far, lax.axis_index("gx") % 2, place)
    narrow = w_ref[: 3 * width, : 3 * width]
    planes = [0, size_x - 1] if edges else [x for first in pairs for x in (first, first + 1)]
    rim_taps(taps, range(len(planes)), [[rim(x + j) for j in (-1, 0, 1)] for x in planes], narrow)
    stores = []

    def multiply(k):
        x = planes[k]
        if edges:
            for i in range(2):
                plane_taps(taps, (i,), [body(planes[i] + j) for j in (-1, 0, 1)], narrow)
        else:
            plane_taps(taps, (k, k + 1), [body(x + j) for j in (-1, 0, 1, 2)], w_ref[...])

    multiply(0)
    for k in range(0, len(planes), 2):
        if k + 2 < len(planes):
            multiply(k + 2)
        for i in (k, k + 1):
            for y in range(0, size_y, CHUNK):
                out[i, y : y + CHUNK, :] = shifted_sum(taps, i, PAD + y, CHUNK).astype(BF16)
            stores.append(
                pltpu.make_async_copy(out.at[i], out_hbm.at[planes[i]], sems.at[i])
            )
            stores[-1].start()
    for copy in stores:
        copy.wait()


def finish_kernel(inverse, own, other, exponents, grad_ref, bias_ref):
    half = own.shape[2] // 2

    def emit(first, second):
        def scaled(block, a, b, c):
            power = lax.shift_left(jnp.int32(1), exponents[a, b, c] + 2).astype(F32)
            return (block * (power * (0.25 * inverse))).astype(BF16)

        for s in range(SLOTS):
            block = (first if s < SLOTS // 2 else second)[s % (SLOTS // 2)]
            low, high = block[:, :half], pltpu.roll(block, half, 1)[:, :half]
            if s < 9:
                a, b = s // 3, s % 3
                grad_ref[3 * s + 1] = scaled(low, a, b, 1)
                grad_ref[3 * s + 2] = scaled(high, a, b, 2)
            else:
                t = 2 * (s - 9)
                grad_ref[3 * t] = scaled(low, t // 3, t % 3, 0)
                if t + 1 < 9:
                    grad_ref[3 * t + 3] = scaled(high, (t + 1) // 3, (t + 1) % 3, 0)
                else:
                    bias_ref[...] = high[:1, : bias_ref.shape[1]] * inverse

    @pl.when(lax.axis_index("gy") % 2 == 0)
    def _():
        emit(own, other)

    @pl.when(lax.axis_index("gy") % 2 == 1)
    def _():
        emit(other, own)


def shape(*dims, dtype=BF16):
    return jax.ShapeDtypeStruct(dims, dtype)


def local(features, kernel, offsets, upstream, grad_exponents):
    cells, cotangent = features[0], upstream[0]
    size_x, size_y, width = cells.shape
    half = width // 2
    tall, rows = size_y + 2 * RIM, size_y + 2 * PAD
    parts = lax.axis_size("dp")
    share = half // parts
    y_side = lax.axis_index("gy") % 2
    x_side = lax.axis_index("gx") % 2

    def rim(start):
        return jnp.concatenate(
            [
                lax.dynamic_slice_in_dim(cells, start, RIM, axis=1),
                lax.dynamic_slice_in_dim(cotangent, start, RIM, axis=1),
            ],
            axis=1,
        )

    last = size_y - RIM
    y_near = swap(rim((1 - y_side) * last), "gy", 0)
    y_far = swap(rim(y_side * last), "gy", 1)

    forward_weights, backward_weights = pl.pallas_call(
        weights_kernel,
        out_shape=(shape(4 * width, 6 * width), shape(4 * width, 6 * width)),
        in_specs=[VMEM],
        out_specs=(VMEM, VMEM),
        name="tap_matrices",
    )(kernel)
    bias = jnp.concatenate([offsets, offsets])[None, :]

    def plane(index):
        near = lax.dynamic_slice_in_dim(y_near, index, 1, axis=0)[0, :RIM]
        far = lax.dynamic_slice_in_dim(y_far, index, 1, axis=0)[0, :RIM]
        body = lax.dynamic_slice_in_dim(cells, index, 1, axis=0)[0]
        left = jnp.where(y_side == 0, far, near)
        right = jnp.where(y_side == 0, near, far)
        return jnp.concatenate([body, left, right], axis=0)

    x_near = swap(plane((1 - x_side) * (size_x - 1)), "gx", 0)
    x_far = swap(plane(x_side * (size_x - 1)), "gx", 1)

    inner = size_x - 2
    rims = [
        pltpu.VMEM((size_x, 2 * RIM, width), BF16),
        pltpu.VMEM((size_x, 2 * RIM, width), BF16),
    ]
    activation, grad, grad_rim, acc, sums = pl.pallas_call(
        inner_kernel,
        out_shape=(
            shape(size_x, size_y, width),
            shape(inner, size_y, width),
            shape(inner, 2 * RIM, width),
            shape(3 * width, 3 * width, dtype=F32),
            shape(8, width, dtype=F32),
        ),
        in_specs=[VMEM] * 6,
        out_specs=(ANY, VMEM, VMEM, VMEM, VMEM),
        scratch_shapes=rims + [
            pltpu.VMEM((inner, size_y, width), BF16),
            pltpu.VMEM((3, inner, rows, width), F32),
            pltpu.VMEM((inner, rows, width), F32),
            pltpu.VMEM((size_x, width, size_y), BF16),
            pltpu.SemaphoreType.DMA((inner // 2,)),
        ],
        compiler_params=PARAMS,
        cost_estimate=pl.CostEstimate(
            flops=2 * 18 * inner * size_y * width * width, bytes_accessed=0, transcendentals=0
        ),
        name="inner_planes",
    )(cells, cotangent, y_near, y_far, forward_weights, bias)

    activation, first, final, near, far, keep, send = pl.pallas_call(
        edge_kernel,
        out_shape=(
            shape(size_x, size_y, width),
            shape(tall, width),
            shape(tall, width),
            shape(tall, width),
            shape(tall, width),
            shape(parts, SLOTS // 2, share, width, dtype=F32),
            shape(parts, SLOTS // 2, share, width, dtype=F32),
        ),
        in_specs=[VMEM] * 10 + [ANY],
        out_specs=(ANY,) + (VMEM,) * 6,
        scratch_shapes=rims + [
            pltpu.VMEM((2, tall, width), BF16),
            pltpu.VMEM((2, size_y, width), BF16),
            pltpu.VMEM((3, 2, rows, width), F32),
            pltpu.VMEM((2, rows, width), F32),
            pltpu.VMEM((3 * width, 3 * width), F32),
            pltpu.SemaphoreType.DMA((2,)),
        ],
        input_output_aliases={10: 0},
        compiler_params=PARAMS,
        name="edge_planes",
    )(
        cells, cotangent, y_near, y_far, x_near, x_far, forward_weights, bias, acc, sums,
        activation,
    )

    back_near = swap(near, "gx", 0)
    back_far = swap(far, "gx", 1)

    def back(pairs, edges, previous, after):
        operands = [grad, grad_rim, first, final]
        operands += [back_near, back_far] if edges else []
        operands += [backward_weights]
        specs = [VMEM] * len(operands)
        aliases = {}
        if previous is not None:
            aliases = {len(operands): 0}
            operands.append(previous)
            specs.append(ANY)
        operands.append(after)
        specs.append(ANY)
        planes = 2 if edges else 2 * len(pairs)
        return pl.pallas_call(
            lambda *refs: back_kernel(pairs, edges, *refs),
            out_shape=shape(size_x, size_y, width),
            in_specs=specs,
            out_specs=ANY,
            scratch_shapes=[
                pltpu.VMEM((planes, size_y, width), BF16),
                pltpu.VMEM((3, planes, rows, width), F32),
                pltpu.VMEM((2, tall, width), BF16),
                pltpu.SemaphoreType.DMA((planes,)),
            ],
            input_output_aliases=aliases,
            compiler_params=PARAMS,
            cost_estimate=pl.CostEstimate(
                flops=2 * 9 * planes * size_y * width * width,
                bytes_accessed=0,
                transcendentals=0,
            ),
            name="input_grad",
        )(*operands)

    total = keep + swap(send, "gy", 0)
    me = lax.axis_index("dp")
    step = 1
    while step < parts:
        paired = total.reshape(total.shape[0] // 2, 2, SLOTS // 2, share, width)
        bit = (me // step) % 2
        mine = lax.dynamic_index_in_dim(paired, bit, 1, keepdims=False)
        theirs = lax.dynamic_index_in_dim(paired, 1 - bit, 1, keepdims=False)
        total = mine + exchange(theirs, "dp", step)
        step *= 2
    total = total[0]
    rounds = [("gy", 1 << i) for i in range(1, lax.axis_size("gy").bit_length() - 1)]
    rounds += [("gx", 1 << i) for i in range(lax.axis_size("gx").bit_length() - 1)]
    for axis, step in rounds:
        total = total + exchange(total, axis, step)
    other = swap(total, "gy", 0)

    starts = list(range(1, size_x - 1, 2))
    cut = (len(starts) + 1) // 2
    input_grad = back(starts[:cut], False, None, send)
    input_grad = back(starts[cut:], False, input_grad, send)
    input_grad = back([], True, input_grad, send)

    voxels = (
        features.shape[0] * parts * size_x * lax.axis_size("gx") * size_y * lax.axis_size("gy") * 2
    )
    kernel_grad, bias_grad = pl.pallas_call(
        lambda *refs: finish_kernel(1.0 / math.sqrt(voxels), *refs),
        out_shape=(shape(27, share, half), shape(1, share, dtype=F32)),
        in_specs=[VMEM, VMEM, SMEM],
        out_specs=(VMEM, VMEM),
        name="scale_weight_grad",
    )(total, other, grad_exponents)
    return (
        activation[None],
        input_grad[None],
        jnp.swapaxes(kernel_grad.reshape(3, 3, 3, share, half), 3, 4),
        bias_grad.reshape(share),
    )


def solution(mesh):
    placed = (P("dp", "gx", "gy", None), P(), P(), P("dp", "gx", "gy", None), P())
    return jax.shard_map(
        local,
        mesh=mesh,
        in_specs=placed,
        out_specs=(
            P("dp", "gx", "gy", None),
            P("dp", "gx", "gy", None),
            P(None, None, None, None, "dp"),
            P("dp"),
        ),
        check_vma=False,
    )
```

time: 156 us -> 47.6 us (0.31)
  matrix products: 35.6 us -> 0 us
  waiting for transfers between devices: 46.1 us -> 13.6 us
  blocking collectives: 25.8 us -> 0 us
  Pallas kernels: 0 us -> 14.5 us
  between operations: 15 us -> 0.89 us
  other arithmetic: 7.35 us -> 0.19 us
  starting transfers between devices: 19.5 us -> 13.5 us
    psum x1 -> x0, waiting for transfers between devices: 45.8 us -> none  [local(): tap_grad, bias_sum = lax.psum((tap_grad, bias_sum), ('gx', 'gy'))]
    dot_general x27 -> x0, matrix products: 35.6 us -> none  [the longest x9 22 us: backward_conv(): jnp.einsum('sxyd,cd->sxyc', window, matrices[shift_x, shift_y], preferred...]
    pallas_call x0 -> x7, Pallas kernels: none -> 14.5 us  [the longest x3 4.69 us: back(): pl.pallas_call(lambda *refs: back_kernel(pairs, edges, *refs), out_shape=...]
    psum x1 -> x0, blocking collectives: 13.8 us -> none  [local(): tap_grad, bias_sum = lax.psum((tap_grad, bias_sum), ('gx', 'gy'))]
    ppermute x8 -> x10, waiting for transfers between devices: 0.29 us -> 13.6 us  [the longest x4 12.2 us: exchange(): lax.ppermute(value, axis, [(i, i ^ step) for i in range(lax.axis_size(axi...]
    unnamed x1 -> x0, blocking collectives: 11.9 us -> none
    ppermute x8 -> x10, starting transfers between devices: 19.4 us -> 13.5 us  [the longest x6 8.24 us: swap(): return lax.ppermute(value, axis, links)]
    convert_element_type x2 -> x0, other arithmetic: 4.83 us -> none  [the longest x1 3.15 us: local(): activation = (preact * sigma).astype(jnp.bfloat16)]
  transfers between devices with their start and end apart: 10 -> 10, of which waited for: 2 -> 5; matrix products, arithmetic and copies ran while one was open for 25% -> 0% of each run, Pallas kernels for 0% -> 23%
where the time goes in v2:
time: 47.6 us; the launch traced here: 47.3 us
  Pallas kernels  14.5 us (30%)
  waiting for transfers between devices  13.6 us (29%)
  starting transfers between devices  13.5 us (28%)
  local copies, waits for them, and re-layouts  4.59 us (10%)
  between operations  0.89 us (2%)
    ppermute x4, waiting for transfers between devices, exchange(): lax.ppermute(value, axis, [(i, i ^ step) for i in range(lax.axis_size(axi...  12.2 us
    ppermute x6, starting transfers between devices, swap(): return lax.ppermute(value, axis, links)  8.24 us
    ppermute x4, starting transfers between devices, exchange(): lax.ppermute(value, axis, [(i, i ^ step) for i in range(lax.axis_size(axi...  5.23 us
    pallas_call x3, Pallas kernels, back(): pl.pallas_call(lambda *refs: back_kernel(pairs, edges, *refs), out_shape=...  4.69 us
    pallas_call x1, Pallas kernels, local(): pl.pallas_call(inner_kernel, out_shape=(shape(size_x, size_y, width), sha...  3.77 us
    unnamed x14, local copies, waits for them, and re-layouts  3.63 us
    pallas_call x1, Pallas kernels, local(): pl.pallas_call(weights_kernel, out_shape=(shape(4 * width, 6 * width), sh...  2.46 us
    pallas_call x1, Pallas kernels, local(): pl.pallas_call(edge_kernel, out_shape=(shape(size_x, size_y, width), shap...  1.93 us
  transfers between devices with their start and end apart: 10, of which 5 were waited for; matrix products, arithmetic and copies ran while one was open for 0% of the time, Pallas kernels for 23%

profile of v2, /device:TPU:0, one launch (start us, length us, event | category | flops | bytes accessed | tf_op | source)
XLA Modules:
  0.0 47.3 jit_solution(5999136730973642688)
XLA Ops:
  0.6 0.0 copy-start.1
  0.7 0.9 %dynamic-slice_bitcast_fusion.2 = (bf16[16,8,128]{2,1,0:T(8,128)(2,1)S(1)}, bf16[16,8,128]{2,1,0:T(8,128)(2,1)S(1)}, bf16[16,8,128]{2,1,0:T(8,128)(2,1)S(1)}, bf16[16,8,128]{2,1,0:T(8,128)(2,1)S(1)}) fusion(bf16[1,16,256,128]{3,2,1,0:T(8,128)(2,1)} %param.8, s32[]{:T(128)S(6)} %select_n.71, s32[]{:T(128)S(6)} %select_n.70, bf16[1,16,256,128]{3,2,1,0:T(8,128)(2,1)} %param.5), kind=kLoop, calls=%fused_computation.7 | loop fusion | bytes 262152 | tf_op jit(solution)/shard_map/dynamic_slice | solution.py:407
  1.6 0.7 %collective-permute-start.1 = (bf16[16,16,128]{2,1,0:T(8,128)(2,1)S(1)}, bf16[16,16,128]{2,1,0:T(8,128)(2,1)S(1)}, u32[]{:S(2)}, u32[]{:S(2)}) collective-permute-start(bf16[16,16,128]{2,1,0:T(8,128)(2,1)S(1)} %pad_maximum_fusion.2), channel_id=1, source_target_pairs={{4,8},{8,4},{5,9},{9,5},{6,10},{10,6},{7,11},{11,7},{20,24},{24,20... | collective-permute-start | bytes 196616 | tf_op jit(solution)/shard_map/ppermute | solution.py:28
  2.3 4.4 %collective-permute-start = (bf16[16,16,128]{2,1,0:T(8,128)(2,1)S(1)}, bf16[16,16,128]{2,1,0:T(8,128)(2,1)S(1)}, u32[]{:S(2)}, u32[]{:S(2)}) collective-permute-start(bf16[16,16,128]{2,1,0:T(8,128)(2,1)S(1)} %pad_maximum_fusion.1), channel_id=1, source_target_pairs={{0,4},{4,0},{8,12},{12,8},{1,5},{5,1},{9,13},{13,9},{2,6},{6,2},{1... | collective-permute-start | bytes 196616 | tf_op jit(solution)/shard_map/ppermute | solution.py:28
  6.7 2.5 %tap_matrices.1 = (bf16[512,768]{1,0:T(8,128)(2,1)}, bf16[512,768]{1,0:T(8,128)(2,1)}) custom-call(bf16[3,3,3,64,64]{4,3,2,1,0:T(8,128)(2,1)} %taps.1), custom_call_target="tpu_custom_call" | custom-call | tf_op jit(solution)/shard_map/tap_matrices/pallas_call | solution.py:416
  9.1 0.0 copy-done.1
  9.1 0.0 copy-start.6
  9.2 0.6 %copy-done.6 = f32[64]{0:T(128)S(1)} copy-done((f32[64]{0:T(128)S(1)}, f32[64]{0:T(128)}, u32[]{:S(2)}) %copy-start.6) | copy-done | bytes 280
  9.8 0.1 maximum_bitcast_fusion.bias_ref
  9.9 0.0 collective-permute-done.1.y_far
  9.9 0.0 collective-permute-done.y_near
  9.9 1.6 %collective-permute-start.2 = (bf16[272,128]{1,0:T(8,128)(2,1)S(1)}, bf16[272,128]{1,0:T(8,128)(2,1)S(1)}, u32[]{:S(2)}, u32[]{:S(2)}) collective-permute-start(bf16[272,128]{1,0:T(8,128)(2,1)S(1)} %pad_maximum_fusion), channel_id=1, source_target_pairs={{0,16},{16,0},{1,17},{17,1},{2,18},{18,2},{3,19},{19,3},{4,20},{20... | collective-permute-start | bytes 208904 | tf_op jit(solution)/shard_map/ppermute | solution.py:28
  11.5 0.0 copy-start.2
  11.5 1.2 %copy-done.2 = bf16[1,16,256,128]{3,2,1,0:T(8,128)(2,1)S(1)} copy-done((bf16[1,16,256,128]{3,2,1,0:T(8,128)(2,1)S(1)}, bf16[1,16,256,128]{3,2,1,0:T(8,128)(2,1)}, u32[]{:S(2)}) %copy-start.2) | copy-done | bytes 1048600
  12.7 0.0 copy-start.3
  12.7 1.1 %copy-done.3 = bf16[512,768]{1,0:T(8,128)(2,1)S(1)} copy-done((bf16[512,768]{1,0:T(8,128)(2,1)S(1)}, bf16[512,768]{1,0:T(8,128)(2,1)}, u32[]{:S(2)}) %copy-start.3) | copy-done | bytes 786456
  13.8 3.8 %inner_planes.1 = (bf16[16,256,128]{2,1,0:T(8,128)(2,1)}, bf16[14,256,128]{2,1,0:T(8,128)(2,1)S(1)}, bf16[14,16,128]{2,1,0:T(8,128)(2,1)S(1)}, f32[384,384]{1,0:T(8,128)S(1)}, f32[8,128]{1,0:T(8,128)S(1)}) custom-call(bf16[16,256,128]{2,1,0:T(8,128)(2,1)S(1)} %bitcast.35, bf16[16,256,128]{2,1,0:T(8,128)(2,1)S(1)} %bitcast.37, ...), custom_call_target="tpu_custom_call" | custom-call | flops 2113929216 | tf_op jit(solution)/shard_map/inner_planes/pallas_call | solution.py:441
  17.6 0.0 collective-permute-done.2.x_near
  17.6 1.9 %edge_planes.1 = (bf16[16,256,128]{2,1,0:T(8,128)(2,1)}, bf16[272,128]{1,0:T(8,128)(2,1)S(1)}, bf16[272,128]{1,0:T(8,128)(2,1)S(1)}, bf16[272,128]{1,0:T(8,128)(...) custom-call(bf16[16,256,128]{2,1,0:T(8,128)(2,1)S(1)} %bitcast.36, ...), custom_call_target="tpu_custom_call", output_to_operand_aliasing={{0}: (10, {})} | custom-call | tf_op jit(solution)/shard_map/edge_planes/pallas_call | solution.py:466
  19.6 0.1 collective-permute-start.4
  19.7 1.5 %collective-permute-done.4 = f32[4,7,16,128]{3,2,1,0:T(8,128)S(1)} collective-permute-done((f32[4,7,16,128]{3,2,1,0:T(8,128)S(1)}, f32[4,7,16,128]{3,2,1,0:T(8,128)S(1)}, u32[]{:S(2)}, u32[]{:S(2)}) %collective-permute-start.4) | collective-permute-done | bytes 229408 | tf_op jit(solution)/shard_map/ppermute | solution.py:28
  21.2 0.0 copy-start
  21.2 1.6 %collective-permute-start.5 = (f32[2,7,16,128]{3,2,1,0:T(8,128)S(1)}, f32[2,7,16,128]{3,2,1,0:T(8,128)S(1)}, u32[]{:S(2)}, u32[]{:S(2)}) collective-permute-start(f32[2,7,16,128]{3,2,1,0:T(8,128)S(1)} %dynamic-slice_bitcast_fusion), channel_id=1, source_target_pairs={{0,1},{1,0},{2,3},{3,2},{4,5},{5,4},{6,7},{7,6},{8,9},{9,8},{10,11... | collective-permute-start | bytes 344072 | tf_op jit(solution)/shard_map/ppermute | solution.py:32
  22.8 3.6 %collective-permute-done.5 = f32[2,7,16,128]{3,2,1,0:T(8,128)S(1)} collective-permute-done((f32[2,7,16,128]{3,2,1,0:T(8,128)S(1)}, f32[2,7,16,128]{3,2,1,0:T(8,128)S(1)}, u32[]{:S(2)}, u32[]{:S(2)}) %collective-permute-start.5) | collective-permute-done | bytes 114720 | tf_op jit(solution)/shard_map/ppermute | solution.py:32
  26.5 2.7 %collective-permute-start.6 = (f32[1,7,16,128]{3,2,1,0:T(8,128)S(1)}, f32[1,7,16,128]{3,2,1,0:T(8,128)S(1)}, u32[]{:S(2)}, u32[]{:S(2)}) collective-permute-start(f32[1,7,16,128]{3,2,1,0:T(8,128)S(1)} %constant_dynamic-slice_fusion), channel_id=1, source_target_pairs={{0,2},{1,3},{2,0},{3,1},{4,6},{5,7},{6,4},{7,5},{8,10},{9,11},{10,... | collective-permute-start | bytes 172040 | tf_op jit(solution)/shard_map/ppermute | solution.py:32
  29.1 2.5 %collective-permute-done.6 = f32[1,7,16,128]{3,2,1,0:T(8,128)S(1)} collective-permute-done((f32[1,7,16,128]{3,2,1,0:T(8,128)S(1)}, f32[1,7,16,128]{3,2,1,0:T(8,128)S(1)}, u32[]{:S(2)}, u32[]{:S(2)}) %collective-permute-start.6) | collective-permute-done | bytes 57376 | tf_op jit(solution)/shard_map/ppermute | solution.py:32
  31.6 0.3 collective-permute-start.7
  32.0 3.9 %collective-permute-done.7 = f32[7,16,128]{2,1,0:T(8,128)S(1)} collective-permute-done((f32[7,16,128]{2,1,0:T(8,128)S(1)}, f32[7,16,128]{2,1,0:T(8,128)S(1)}, u32[]{:S(2)}, u32[]{:S(2)}) %collective-permute-start.7) | collective-permute-done | bytes 57376 | tf_op jit(solution)/shard_map/ppermute | solution.py:32
  35.9 0.6 %collective-permute-start.8 = (f32[7,16,128]{2,1,0:T(8,128)S(1)}, f32[7,16,128]{2,1,0:T(8,128)S(1)}, u32[]{:S(2)}, u32[]{:S(2)}) collective-permute-start(f32[7,16,128]{2,1,0:T(8,128)S(1)} %add.73), channel_id=1, source_target_pairs={{0,16},{16,0},{1,17},{17,1},{2,18},{18,2},{3,19},{19,3},{4,20},{20... | collective-permute-start | bytes 172040 | tf_op jit(solution)/shard_map/ppermute | solution.py:32
  36.5 1.5 %collective-permute-start.3 = (bf16[272,128]{1,0:T(8,128)(2,1)S(1)}, bf16[272,128]{1,0:T(8,128)(2,1)S(1)}, u32[]{:S(2)}, u32[]{:S(2)}) collective-permute-start(bf16[272,128]{1,0:T(8,128)(2,1)S(1)} %get-tuple-element.28), channel_id=1, source_target_pairs={{0,16},{16,0},{1,17},{17,1},{2,18},{18,2},{3,19},{19,3},{4,20},{20... | collective-permute-start | bytes 208904 | tf_op jit(solution)/shard_map/ppermute | solution.py:28
  38.0 2.2 %collective-permute-done.8 = f32[7,16,128]{2,1,0:T(8,128)S(1)} collective-permute-done((f32[7,16,128]{2,1,0:T(8,128)S(1)}, f32[7,16,128]{2,1,0:T(8,128)S(1)}, u32[]{:S(2)}, u32[]{:S(2)}) %collective-permute-start.8) | collective-permute-done | bytes 57376 | tf_op jit(solution)/shard_map/ppermute | solution.py:32
  40.2 0.0 copy-start.4
  40.2 0.1 collective-permute-start.9
  40.2 0.0 copy-done
  40.3 1.9 %input_grad.3.refs_5_ = bf16[16,256,128]{2,1,0:T(8,128)(2,1)} custom-call(bf16[14,256,128]{2,1,0:T(8,128)(2,1)S(1)} %get-tuple-element.24.refs_0_, bf16[14,16,128]{2,1,0:T(8,128)(2,1)S(1)} %get-tuple-element.25.refs_1_, bf16[272,128]{1,0:T(8,128)(2,1)S(1)} %get-tuple-element.26.refs_2_, bf16[272,128]{1,0:T(8,128)(2,1)S(1)} %get-tuple-element.27.refs_3_, ...), custom_call_target="tpu_custom_call" | custom-call | flops 603979776 | tf_op jit(solution)/shard_map/input_grad/pallas_call | solution.py:511
  42.2 0.0 copy-done.4
  42.2 1.7 %input_grad.4.refs_7_ = bf16[16,256,128]{2,1,0:T(8,128)(2,1)} custom-call(bf16[14,256,128]{2,1,0:T(8,128)(2,1)S(1)} %get-tuple-element.24.refs_0_, bf16[14,16,128]{2,1,0:T(8,128)(2,1)S(1)} %get-tuple-element.25.refs_1_, bf16[272,128]{1,0:T(8,128)(2,1)S(1)} %get-tuple-element.26.refs_2_, ...), custom_call_target="tpu_custom_call", output_to_operand_aliasing={{}: (5, {})} | custom-call | flops 452984832 | tf_op jit(solution)/shard_map/input_grad/pallas_call | solution.py:511
  43.8 0.0 collective-permute-done.3.refs_4_
  43.8 1.1 %input_grad.5 = bf16[16,256,128]{2,1,0:T(8,128)(2,1)} custom-call(bf16[14,256,128]{2,1,0:T(8,128)(2,1)S(1)} %get-tuple-element.24.refs_0_, bf16[14,16,128]{2,1,0:T(8,128)(2,1)S(1)} %get-tuple-element.25.refs_1_, bf16[272,128]{1,0:T(8,128)(2,1)S(1)} %get-tuple-element.26.refs_2_, ...), custom_call_target="tpu_custom_call", output_to_operand_aliasing={{}: (7, {})} | custom-call | flops 150994944 | tf_op jit(solution)/shard_map/input_grad/pallas_call | solution.py:511
  45.0 0.0 collective-permute-done.9.refs_1_
  45.0 0.0 copy-start.5
  45.0 0.6 %copy-done.5 = f32[7,16,128]{2,1,0:T(8,128)} copy-done((f32[7,16,128]{2,1,0:T(8,128)}, f32[7,16,128]{2,1,0:T(8,128)S(1)}, u32[]{:S(2)}) %copy-start.5) | copy-done | bytes 57368
  45.6 1.6 %scale_weight_grad.1 = (bf16[27,16,64]{2,1,0:T(8,128)(2,1)}, f32[1,16]{1,0:T(1,128)}) custom-call(f32[7,16,128]{2,1,0:T(8,128)} %copy-done.4, f32[7,16,128]{2,1,0:T(8,128)} %copy-done.5, s32[3,3,3]{2,1,0:T(4,128)} %refs_2_.1), custom_call_target="tpu_custom_call" | custom-call | tf_op jit(solution)/shard_map/scale_weight_grad/pallas_call | solution.py:558
  (13 shorter events, 0.2 us)
Async XLA Ops:
  0.6 8.5 %copy-start.1 = (bf16[1,16,256,128]{3,2,1,0:T(8,128)(2,1)S(1)}, bf16[1,16,256,128]{3,2,1,0:T(8,128)(2,1)}, u32[]{:S(2)}) copy-start(bf16[1,16,256,128]{3,2,1,0:T(8,128)(2,1)} %param.5) | copy-start | bytes 3145732
  1.6 8.3 %collective-permute-start.1 = (bf16[16,16,128]{2,1,0:T(8,128)(2,1)S(1)}, bf16[16,16,128]{2,1,0:T(8,128)(2,1)S(1)}, u32[]{:S(2)}, u32[]{:S(2)}) collective-permute-start(bf16[16,16,128]{2,1,0:T(8,128)(2,1)S(1)} %pad_maximum_fusion.2), channel_id=1, source_target_pairs={{4,8},{8,4},{5,9},{9,5},{6,10},{10,6},{7,11},{11,7},{20,24},{24,20... | collective-permute-start | bytes 196616 | tf_op jit(solution)/shard_map/ppermute | solution.py:28
  2.3 7.6 %collective-permute-start = (bf16[16,16,128]{2,1,0:T(8,128)(2,1)S(1)}, bf16[16,16,128]{2,1,0:T(8,128)(2,1)S(1)}, u32[]{:S(2)}, u32[]{:S(2)}) collective-permute-start(bf16[16,16,128]{2,1,0:T(8,128)(2,1)S(1)} %pad_maximum_fusion.1), channel_id=1, source_target_pairs={{0,4},{4,0},{8,12},{12,8},{1,5},{5,1},{9,13},{13,9},{2,6},{6,2},{1... | collective-permute-start | bytes 196616 | tf_op jit(solution)/shard_map/ppermute | solution.py:28
  9.1 0.7 %copy-start.6 = (f32[64]{0:T(128)S(1)}, f32[64]{0:T(128)}, u32[]{:S(2)}) copy-start(f32[64]{0:T(128)} %param.7) | copy-start | bytes 772
  9.9 7.7 %collective-permute-start.2 = (bf16[272,128]{1,0:T(8,128)(2,1)S(1)}, bf16[272,128]{1,0:T(8,128)(2,1)S(1)}, u32[]{:S(2)}, u32[]{:S(2)}) collective-permute-start(bf16[272,128]{1,0:T(8,128)(2,1)S(1)} %pad_maximum_fusion), channel_id=1, source_target_pairs={{0,16},{16,0},{1,17},{17,1},{2,18},{18,2},{3,19},{19,3},{4,20},{20... | collective-permute-start | bytes 208904 | tf_op jit(solution)/shard_map/ppermute | solution.py:28
  11.5 1.2 %copy-start.2 = (bf16[1,16,256,128]{3,2,1,0:T(8,128)(2,1)S(1)}, bf16[1,16,256,128]{3,2,1,0:T(8,128)(2,1)}, u32[]{:S(2)}) copy-start(bf16[1,16,256,128]{3,2,1,0:T(8,128)(2,1)} %param.8) | copy-start | bytes 3145732
  12.7 1.1 %copy-start.3 = (bf16[512,768]{1,0:T(8,128)(2,1)S(1)}, bf16[512,768]{1,0:T(8,128)(2,1)}, u32[]{:S(2)}) copy-start(bf16[512,768]{1,0:T(8,128)(2,1)} %get-tuple-element.19.w_ref) | copy-start | bytes 2359300
  19.6 1.6 %collective-permute-start.4 = (f32[4,7,16,128]{3,2,1,0:T(8,128)S(1)}, f32[4,7,16,128]{3,2,1,0:T(8,128)S(1)}, u32[]{:S(2)}, u32[]{:S(2)}) collective-permute-start(f32[4,7,16,128]{3,2,1,0:T(8,128)S(1)} %get-tuple-element.30.refs_5_.refs_6_.refs_8_), channel_id=1, source_target_pairs={{0,4},{4,0},{8,12},{12,8},{1,5},{5,1},{9,13},{13,9},{2,6},{6,2},{1... | collective-permute-start | bytes 688136 | tf_op jit(solution)/shard_map/ppermute | solution.py:28
  21.2 19.1 %copy-start = (bf16[512,768]{1,0:T(8,128)(2,1)S(1)}, bf16[512,768]{1,0:T(8,128)(2,1)}, u32[]{:S(2)}) copy-start(bf16[512,768]{1,0:T(8,128)(2,1)} %get-tuple-element.29.refs_4_.refs_6_) | copy-start | bytes 2359300
  21.2 5.3 %collective-permute-start.5 = (f32[2,7,16,128]{3,2,1,0:T(8,128)S(1)}, f32[2,7,16,128]{3,2,1,0:T(8,128)S(1)}, u32[]{:S(2)}, u32[]{:S(2)}) collective-permute-start(f32[2,7,16,128]{3,2,1,0:T(8,128)S(1)} %dynamic-slice_bitcast_fusion), channel_id=1, source_target_pairs={{0,1},{1,0},{2,3},{3,2},{4,5},{5,4},{6,7},{7,6},{8,9},{9,8},{10,11... | collective-permute-start | bytes 344072 | tf_op jit(solution)/shard_map/ppermute | solution.py:32
  26.5 5.1 %collective-permute-start.6 = (f32[1,7,16,128]{3,2,1,0:T(8,128)S(1)}, f32[1,7,16,128]{3,2,1,0:T(8,128)S(1)}, u32[]{:S(2)}, u32[]{:S(2)}) collective-permute-start(f32[1,7,16,128]{3,2,1,0:T(8,128)S(1)} %constant_dynamic-slice_fusion), channel_id=1, source_target_pairs={{0,2},{1,3},{2,0},{3,1},{4,6},{5,7},{6,4},{7,5},{8,10},{9,11},{10,... | collective-permute-start | bytes 172040 | tf_op jit(solution)/shard_map/ppermute | solution.py:32
  31.6 4.2 %collective-permute-start.7 = (f32[7,16,128]{2,1,0:T(8,128)S(1)}, f32[7,16,128]{2,1,0:T(8,128)S(1)}, u32[]{:S(2)}, u32[]{:S(2)}) collective-permute-start(f32[7,16,128]{2,1,0:T(8,128)S(1)} %add_bitcast_fusion), channel_id=1, source_target_pairs={{0,8},{4,12},{8,0},{12,4},{1,9},{5,13},{9,1},{13,5},{2,10},{6,14},... | collective-permute-start | bytes 172040 | tf_op jit(solution)/shard_map/ppermute | solution.py:32
  35.9 4.2 %collective-permute-start.8 = (f32[7,16,128]{2,1,0:T(8,128)S(1)}, f32[7,16,128]{2,1,0:T(8,128)S(1)}, u32[]{:S(2)}, u32[]{:S(2)}) collective-permute-start(f32[7,16,128]{2,1,0:T(8,128)S(1)} %add.73), channel_id=1, source_target_pairs={{0,16},{16,0},{1,17},{17,1},{2,18},{18,2},{3,19},{19,3},{4,20},{20... | collective-permute-start | bytes 172040 | tf_op jit(solution)/shard_map/ppermute | solution.py:32
  36.5 7.3 %collective-permute-start.3 = (bf16[272,128]{1,0:T(8,128)(2,1)S(1)}, bf16[272,128]{1,0:T(8,128)(2,1)S(1)}, u32[]{:S(2)}, u32[]{:S(2)}) collective-permute-start(bf16[272,128]{1,0:T(8,128)(2,1)S(1)} %get-tuple-element.28), channel_id=1, source_target_pairs={{0,16},{16,0},{1,17},{17,1},{2,18},{18,2},{3,19},{19,3},{4,20},{20... | collective-permute-start | bytes 208904 | tf_op jit(solution)/shard_map/ppermute | solution.py:28
  40.2 2.0 %copy-start.4 = (f32[7,16,128]{2,1,0:T(8,128)}, f32[7,16,128]{2,1,0:T(8,128)S(1)}, u32[]{:S(2)}) copy-start(f32[7,16,128]{2,1,0:T(8,128)S(1)} %add.74.refs_0_) | copy-start | bytes 172036
  40.2 4.8 %collective-permute-start.9 = (f32[7,16,128]{2,1,0:T(8,128)S(1)}, f32[7,16,128]{2,1,0:T(8,128)S(1)}, u32[]{:S(2)}, u32[]{:S(2)}) collective-permute-start(f32[7,16,128]{2,1,0:T(8,128)S(1)} %add.74.refs_0_), channel_id=1, source_target_pairs={{0,4},{4,0},{8,12},{12,8},{1,5},{5,1},{9,13},{13,9},{2,6},{6,2},{1... | collective-permute-start | bytes 172040 | tf_op jit(solution)/shard_map/ppermute | solution.py:28
  45.0 0.6 %copy-start.5 = (f32[7,16,128]{2,1,0:T(8,128)}, f32[7,16,128]{2,1,0:T(8,128)S(1)}, u32[]{:S(2)}) copy-start(f32[7,16,128]{2,1,0:T(8,128)S(1)} %collective-permute-done.9.refs_1_) | copy-start | bytes 172036

commit v3 on v2

--- a/solution.py
+++ b/solution.py
@@ -8,13 +8,13 @@
 from jax.sharding import PartitionSpec as P
 
 RIM = 8
+THIN = 2
 PAD = 16
 CHUNK = 64
 SLOTS = 14
 VMEM = pl.BlockSpec(memory_space=pltpu.VMEM)
 SMEM = pl.BlockSpec(memory_space=pltpu.SMEM)
 ANY = pl.BlockSpec(memory_space=pl.ANY)
-PARAMS = pltpu.CompilerParams(vmem_limit_bytes=32 * 2**20)
 BF16, F32 = jnp.bfloat16, jnp.float32
 
 
@@ -32,23 +32,60 @@
     return lax.ppermute(value, axis, [(i, i ^ step) for i in range(lax.axis_size(axis))])
 
 
-def weights_kernel(taps, ahead, back):
+def tap_block(taps, a, b):
+    low, mid, high = taps[a, b, 0], taps[a, b, 1], taps[a, b, 2]
+    return jnp.concatenate(
+        [jnp.concatenate([mid, low], axis=1), jnp.concatenate([high, mid], axis=1)], axis=0
+    )
+
+
+def clear_corners(out, width):
+    blank = jnp.zeros((width, 3 * width), BF16)
+    out[3 * width :, : 3 * width] = blank
+    out[:width, 3 * width :] = blank
+
+
+def bias_kernel(offsets, rim_in, bias_ref):
+    bias = offsets[...].reshape(1, bias_ref.shape[1] // 2)
+    bias_ref[...] = jnp.concatenate([bias, bias], axis=1)
+
+
+def build_front(taps, w_ref, narrow_ref):
+    width = 2 * taps.shape[3]
+    clear_corners(w_ref, width)
+    for a in range(3):
+        for b in range(3):
+            block = tap_block(taps, a, b)
+            for k in range(2):
+                row, col = (a + k) * width, (3 * k + b) * width
+                w_ref[row : row + width, col : col + width] = block
+            row, col = a * width, b * width
+            narrow_ref[row : row + width, col : col + width] = block
+
+
+def back_weights_kernel(inverse, taps, exponents, w_ref, scale_ref):
     half = taps.shape[3]
     width = 2 * half
-    for out in (ahead, back):
-        out[...] = jnp.zeros(out.shape, BF16)
+    clear_corners(w_ref, width)
     for a in range(3):
         for b in range(3):
-            low, mid, high = taps[a, b, 0], taps[a, b, 1], taps[a, b, 2]
-            block = jnp.concatenate(
-                [jnp.concatenate([mid, low], axis=1), jnp.concatenate([high, mid], axis=1)], axis=0
-            )
-            turned = block.T
+            turned = tap_block(taps, a, b).T
             for k in range(2):
-                row, col = (a + k) * width, (3 * k + b) * width
-                ahead[row : row + width, col : col + width] = block
                 row, col = (2 - a + k) * width, (3 * k + 2 - b) * width
-                back[row : row + width, col : col + width] = turned
+                w_ref[row : row + width, col : col + width] = turned
+    lower = lax.broadcasted_iota(jnp.int32, (8, width), 1) < half
+
+    def scale(t, c):
+        power = lax.shift_left(jnp.int32(1), exponents[t // 3, t % 3, c] + 2)
+        return power.astype(F32) * (0.25 * inverse)
+
+    for s in range(SLOTS):
+        t = 2 * (s - 9)
+        if s < 9:
+            low, high = scale(s, 1), scale(s, 2)
+        else:
+            low, high = scale(t, 0), scale(t + 1, 0) if t + 1 < 9 else inverse
+        scale_ref[s] = jnp.where(lower, low, high)
 
 
 def plane_taps(taps, slots, bodies, weights):
@@ -134,21 +171,25 @@
 
 
 def place_rims(y_near, y_far, f_rim, u_rim):
+    for ref in (f_rim, u_rim):
+        ref[...] = jnp.zeros(ref.shape, BF16)
+
     def place(left, right):
-        f_rim[:, :RIM, :] = left[:, :RIM, :]
-        f_rim[:, RIM:, :] = right[:, :RIM, :]
-        u_rim[:, :RIM, :] = left[:, RIM:, :]
-        u_rim[:, RIM:, :] = right[:, RIM:, :]
+        f_rim[:, RIM - THIN : RIM, :] = left[:, :THIN, :]
+        f_rim[:, RIM : RIM + THIN, :] = right[:, :THIN, :]
+        u_rim[:, RIM - THIN : RIM, :] = left[:, THIN:, :]
+        u_rim[:, RIM : RIM + THIN, :] = right[:, THIN:, :]
 
     oriented(y_near, y_far, lax.axis_index("gy") % 2, place)
 
 
 def inner_kernel(
-    f_ref, u_ref, y_near, y_far, w_ref, bias_ref,
-    act_hbm, grad_ref, rim_ref, acc_ref, sums_ref,
-    f_rim, u_rim, act, taps, wide, turned, sems,
+    f_ref, u_ref, y_near, y_far, kernel_ref, bias_ref,
+    act_hbm, grad_ref, rim_ref, acc_ref, sums_ref, narrow_ref,
+    f_rim, u_rim, act, taps, wide, turned, w_ref, sems,
 ):
     size_x, size_y, width = f_ref.shape
+    build_front(kernel_ref, w_ref, narrow_ref)
     inner = size_x - 2
     place_rims(y_near, y_far, f_rim, u_rim)
     bias = bias_ref[...]
@@ -213,7 +254,7 @@
 
     oriented(x_near, x_far, x_side, place)
     bias = bias_ref[...]
-    weights = w_ref[: 3 * width, : 3 * width]
+    weights = w_ref[...]
     tall = size_y + 2 * RIM
     bodies = [
         [around[0, :size_y], f_ref[0], f_ref[1]],
@@ -354,28 +395,19 @@
         copy.wait()
 
 
-def finish_kernel(inverse, own, other, exponents, grad_ref, bias_ref):
-    half = own.shape[2] // 2
+def finish_kernel(own, other, scale_ref, grad_ref, bias_ref):
+    share, half = grad_ref.shape[1:]
 
     def emit(first, second):
-        def scaled(block, a, b, c):
-            power = lax.shift_left(jnp.int32(1), exponents[a, b, c] + 2).astype(F32)
-            return (block * (power * (0.25 * inverse))).astype(BF16)
-
         for s in range(SLOTS):
-            block = (first if s < SLOTS // 2 else second)[s % (SLOTS // 2)]
+            block = (first if s < SLOTS // 2 else second)[s % (SLOTS // 2)] * scale_ref[s, :1]
             low, high = block[:, :half], pltpu.roll(block, half, 1)[:, :half]
-            if s < 9:
-                a, b = s // 3, s % 3
-                grad_ref[3 * s + 1] = scaled(low, a, b, 1)
-                grad_ref[3 * s + 2] = scaled(high, a, b, 2)
+            t = 2 * (s - 9)
+            grad_ref[3 * s + 1 if s < 9 else 3 * t] = low.astype(BF16)
+            if s < SLOTS - 1:
+                grad_ref[3 * s + 2 if s < 9 else 3 * t + 3] = high.astype(BF16)
             else:
-                t = 2 * (s - 9)
-                grad_ref[3 * t] = scaled(low, t // 3, t % 3, 0)
-                if t + 1 < 9:
-                    grad_ref[3 * t + 3] = scaled(high, (t + 1) // 3, (t + 1) % 3, 0)
-                else:
-                    bias_ref[...] = high[:1, : bias_ref.shape[1]] * inverse
+                bias_ref[...] = high[:1, :share]
 
     @pl.when(lax.axis_index("gy") % 2 == 0)
     def _():
@@ -388,6 +420,16 @@
 
 def shape(*dims, dtype=BF16):
     return jax.ShapeDtypeStruct(dims, dtype)
+
+
+def grant(mebibytes):
+    return pltpu.CompilerParams(vmem_limit_bytes=mebibytes * 2**20)
+
+
+def cost(microseconds):
+    return pl.CostEstimate(
+        flops=int(1.1e9 * microseconds), bytes_accessed=0, transcendentals=0
+    )
 
 
 def local(features, kernel, offsets, upstream, grad_exponents):
@@ -403,32 +445,47 @@
     def rim(start):
         return jnp.concatenate(
             [
-                lax.dynamic_slice_in_dim(cells, start, RIM, axis=1),
-                lax.dynamic_slice_in_dim(cotangent, start, RIM, axis=1),
+                lax.dynamic_slice_in_dim(cells, start, THIN, axis=1),
+                lax.dynamic_slice_in_dim(cotangent, start, THIN, axis=1),
             ],
             axis=1,
         )
 
-    last = size_y - RIM
-    y_near = swap(rim((1 - y_side) * last), "gy", 0)
-    y_far = swap(rim(y_side * last), "gy", 1)
-
-    forward_weights, backward_weights = pl.pallas_call(
-        weights_kernel,
-        out_shape=(shape(4 * width, 6 * width), shape(4 * width, 6 * width)),
-        in_specs=[VMEM],
+    last = size_y - THIN
+    rim_near, rim_far = rim((1 - y_side) * last), rim(y_side * last)
+    y_near = swap(rim_near, "gy", 0)
+    y_far = swap(rim_far, "gy", 1)
+
+    voxels = (
+        features.shape[0] * parts * size_x * lax.axis_size("gx") * size_y * lax.axis_size("gy") * 2
+    )
+    backward_weights, scales = pl.pallas_call(
+        lambda *refs: back_weights_kernel(1.0 / math.sqrt(voxels), *refs),
+        out_shape=(shape(4 * width, 6 * width), shape(SLOTS, 8, width, dtype=F32)),
+        in_specs=[VMEM, SMEM],
         out_specs=(VMEM, VMEM),
-        name="tap_matrices",
-    )(kernel)
-    bias = jnp.concatenate([offsets, offsets])[None, :]
+        compiler_params=grant(4),
+        cost_estimate=cost(2.0),
+        name="back_weights",
+    )(kernel, grad_exponents)
+    bias = pl.pallas_call(
+        bias_kernel,
+        out_shape=shape(1, width, dtype=F32),
+        in_specs=[VMEM, ANY],
+        out_specs=VMEM,
+        compiler_params=grant(2),
+        cost_estimate=cost(3.0),
+        name="bias",
+    )(offsets, rim_far)
 
     def plane(index):
-        near = lax.dynamic_slice_in_dim(y_near, index, 1, axis=0)[0, :RIM]
-        far = lax.dynamic_slice_in_dim(y_far, index, 1, axis=0)[0, :RIM]
+        near = lax.dynamic_slice_in_dim(y_near, index, 1, axis=0)[0, :THIN]
+        far = lax.dynamic_slice_in_dim(y_far, index, 1, axis=0)[0, :THIN]
         body = lax.dynamic_slice_in_dim(cells, index, 1, axis=0)[0]
         left = jnp.where(y_side == 0, far, near)
         right = jnp.where(y_side == 0, near, far)
-        return jnp.concatenate([body, left, right], axis=0)
+        blank = jnp.zeros((RIM - THIN, width), body.dtype)
+        return jnp.concatenate([body, blank, left, right, blank], axis=0)
 
     x_near = swap(plane((1 - x_side) * (size_x - 1)), "gx", 0)
     x_far = swap(plane(x_side * (size_x - 1)), "gx", 1)
@@ -438,7 +495,7 @@
         pltpu.VMEM((size_x, 2 * RIM, width), BF16),
         pltpu.VMEM((size_x, 2 * RIM, width), BF16),
     ]
-    activation, grad, grad_rim, acc, sums = pl.pallas_call(
+    activation, grad, grad_rim, acc, sums, forward_weights = pl.pallas_call(
         inner_kernel,
         out_shape=(
             shape(size_x, size_y, width),
@@ -446,22 +503,22 @@
             shape(inner, 2 * RIM, width),
             shape(3 * width, 3 * width, dtype=F32),
             shape(8, width, dtype=F32),
+            shape(3 * width, 3 * width),
         ),
         in_specs=[VMEM] * 6,
-        out_specs=(ANY, VMEM, VMEM, VMEM, VMEM),
+        out_specs=(ANY,) + (VMEM,) * 5,
         scratch_shapes=rims + [
             pltpu.VMEM((inner, size_y, width), BF16),
             pltpu.VMEM((3, inner, rows, width), F32),
             pltpu.VMEM((inner, rows, width), F32),
             pltpu.VMEM((size_x, width, size_y), BF16),
+            pltpu.VMEM((4 * width, 6 * width), BF16),
             pltpu.SemaphoreType.DMA((inner // 2,)),
         ],
-        compiler_params=PARAMS,
-        cost_estimate=pl.CostEstimate(
-            flops=2 * 18 * inner * size_y * width * width, bytes_accessed=0, transcendentals=0
-        ),
+        compiler_params=grant(24),
+        cost_estimate=cost(4.0),
         name="inner_planes",
-    )(cells, cotangent, y_near, y_far, forward_weights, bias)
+    )(cells, cotangent, y_near, y_far, kernel, bias)
 
     activation, first, final, near, far, keep, send = pl.pallas_call(
         edge_kernel,
@@ -485,7 +542,8 @@
             pltpu.SemaphoreType.DMA((2,)),
         ],
         input_output_aliases={10: 0},
-        compiler_params=PARAMS,
+        compiler_params=grant(12),
+        cost_estimate=cost(2.0),
         name="edge_planes",
     )(
         cells, cotangent, y_near, y_far, x_near, x_far, forward_weights, bias, acc, sums,
@@ -520,12 +578,8 @@
                 pltpu.SemaphoreType.DMA((planes,)),
             ],
             input_output_aliases=aliases,
-            compiler_params=PARAMS,
-            cost_estimate=pl.CostEstimate(
-                flops=2 * 9 * planes * size_y * width * width,
-                bytes_accessed=0,
-                transcendentals=0,
-            ),
+            compiler_params=grant(12),
+            cost_estimate=cost(2.5),
             name="input_grad",
         )(*operands)
 
@@ -552,16 +606,14 @@
     input_grad = back(starts[cut:], False, input_grad, send)
     input_grad = back([], True, input_grad, send)
 
-    voxels = (
-        features.shape[0] * parts * size_x * lax.axis_size("gx") * size_y * lax.axis_size("gy") * 2
-    )
     kernel_grad, bias_grad = pl.pallas_call(
-        lambda *refs: finish_kernel(1.0 / math.sqrt(voxels), *refs),
+        finish_kernel,
         out_shape=(shape(27, share, half), shape(1, share, dtype=F32)),
-        in_specs=[VMEM, VMEM, SMEM],
+        in_specs=[VMEM] * 3,
         out_specs=(VMEM, VMEM),
+        compiler_params=grant(4),
         name="scale_weight_grad",
-    )(total, other, grad_exponents)
+    )(total, other, scales)
     return (
         activation[None],
         input_grad[None],

time: 47.6 us -> 39.2 us (0.82)
  waiting for transfers between devices: 13.6 us -> 9.2 us
  Pallas kernels: 14.5 us -> 12.6 us
  local copies, waits for them, and re-layouts: 4.59 us -> 2.83 us
    ppermute x4, waiting for transfers between devices: 12.2 us -> 7.66 us  [exchange(): lax.ppermute(value, axis, [(i, i ^ step) for i in range(lax.axis_size(axi...]
    pallas_call x2 -> x3, Pallas kernels: 4.11 us -> 1.78 us  [the longest x1 0.98 us: local(): pl.pallas_call(lambda *refs: back_weights_kernel(1.0 / math.sqrt(voxels),...]
    unnamed x14, local copies, waits for them, and re-layouts: 3.63 us -> 1.83 us
    ppermute x6, starting transfers between devices: 8.24 us -> 7.35 us  [swap(): return lax.ppermute(value, axis, links)]
    ppermute x4, starting transfers between devices: 5.23 us -> 6.01 us  [exchange(): lax.ppermute(value, axis, [(i, i ^ step) for i in range(lax.axis_size(axi...]
  transfers between devices with their start and end apart: 10 -> 10, of which waited for: 5 -> 6; matrix products, arithmetic and copies ran while one was open for 0% -> 0% of each run, Pallas kernels for 23% -> 25%
where the time goes in v3:
time: 39.2 us; the launch traced here: 39 us
  starting transfers between devices  13.4 us (34%)
  Pallas kernels  12.6 us (32%)
  waiting for transfers between devices  9.2 us (23%)
  local copies, waits for them, and re-layouts  2.83 us (7%)
  between operations  0.9 us (2%)
    ppermute x4, waiting for transfers between devices, exchange(): lax.ppermute(value, axis, [(i, i ^ step) for i in range(lax.axis_size(axi...  7.66 us
    ppermute x6, starting transfers between devices, swap(): return lax.ppermute(value, axis, links)  7.35 us
    ppermute x4, starting transfers between devices, exchange(): lax.ppermute(value, axis, [(i, i ^ step) for i in range(lax.axis_size(axi...  6.01 us
    pallas_call x3, Pallas kernels, back(): pl.pallas_call(lambda *refs: back_kernel(pairs, edges, *refs), out_shape=...  4.72 us
    pallas_call x1, Pallas kernels, local(): pl.pallas_call(inner_kernel, out_shape=(shape(size_x, size_y, width), sha...  4.11 us
    pallas_call x1, Pallas kernels, local(): pl.pallas_call(edge_kernel, out_shape=(shape(size_x, size_y, width), shap...  1.95 us
    unnamed x14, local copies, waits for them, and re-layouts  1.83 us
    ppermute x6, waiting for transfers between devices, swap(): return lax.ppermute(value, axis, links)  1.54 us
  transfers between devices with their start and end apart: 10, of which 6 were waited for; matrix products, arithmetic and copies ran while one was open for 0% of the time, Pallas kernels for 25%

profile of v3, /device:TPU:0, one launch (start us, length us, event | category | flops | bytes accessed | tf_op | source)
XLA Modules:
  0.0 39.0 jit_solution(2281835446425869981)
XLA Ops:
  0.7 0.9 %dynamic-slice_bitcast_fusion.2 = (bf16[16,2,128]{2,1,0:T(2,128)(2,1)S(1)}, bf16[16,2,128]{2,1,0:T(2,128)(2,1)S(1)}, bf16[16,2,128]{2,1,0:T(2,128)(2,1)S(1)}, bf16[16,2,128]{2,1,0:T(2,128)(2,1)S(1)}) fusion(bf16[1,16,256,128]{3,2,1,0:T(8,128)(2,1)} %param.8, s32[]{:T(128)S(6)} %select_n.71, s32[]{:T(128)S(6)} %select_n.70, bf16[1,16,256,128]{3,2,1,0:T(8,128)(2,1)} %param.5), kind=kLoop, calls=%fused_computation.6 | loop fusion | bytes 65544 | tf_op jit(solution)/shard_map/dynamic_slice | solution.py:449
  1.5 0.7 %collective-permute-start.1 = (bf16[16,4,128]{2,1,0:T(4,128)(2,1)S(1)}, bf16[16,4,128]{2,1,0:T(4,128)(2,1)S(1)}, u32[]{:S(2)}, u32[]{:S(2)}) collective-permute-start(bf16[16,4,128]{2,1,0:T(4,128)(2,1)S(1)} %pad_maximum_fusion.1.rim_in), channel_id=1, source_target_pairs={{4,8},{8,4},{5,9},{9,5},{6,10},{10,6},{7,11},{11,7},{20,24},{24,20... | collective-permute-start | bytes 49160 | tf_op jit(solution)/shard_map/ppermute | solution.py:28
  2.2 4.4 %collective-permute-start = (bf16[16,4,128]{2,1,0:T(4,128)(2,1)S(1)}, bf16[16,4,128]{2,1,0:T(4,128)(2,1)S(1)}, u32[]{:S(2)}, u32[]{:S(2)}) collective-permute-start(bf16[16,4,128]{2,1,0:T(4,128)(2,1)S(1)} %pad_maximum_fusion), channel_id=1, source_target_pairs={{0,4},{4,0},{8,12},{12,8},{1,5},{5,1},{9,13},{13,9},{2,6},{6,2},{1... | collective-permute-start | bytes 49160 | tf_op jit(solution)/shard_map/ppermute | solution.py:28
  6.6 0.0 copy-start.4
  6.6 0.7 %copy-done.4 = f32[64]{0:T(128)S(1)} copy-done((f32[64]{0:T(128)S(1)}, f32[64]{0:T(128)}, u32[]{:S(2)}) %copy-start.4) | copy-done | bytes 280
  7.3 0.0 copy-start
  7.3 0.0 copy-start.1
  7.3 0.0 copy-start.2
  7.3 0.1 bias.1.bias_ref
  7.4 1.1 %copy-done = bf16[1,16,256,128]{3,2,1,0:T(8,128)(2,1)S(1)} copy-done((bf16[1,16,256,128]{3,2,1,0:T(8,128)(2,1)S(1)}, bf16[1,16,256,128]{3,2,1,0:T(8,128)(2,1)}, u32[]{:S(2)}) %copy-start) | copy-done | bytes 1048600
  8.5 0.0 collective-permute-done.1.y_far
  8.5 0.0 collective-permute-done.y_near
  8.6 0.1 concatenate.11
  8.7 1.5 %collective-permute-start.2 = (bf16[272,128]{1,0:T(8,128)(2,1)S(1)}, bf16[272,128]{1,0:T(8,128)(2,1)S(1)}, u32[]{:S(2)}, u32[]{:S(2)}) collective-permute-start(bf16[272,128]{1,0:T(8,128)(2,1)S(1)} %concatenate.11), channel_id=1, source_target_pairs={{0,16},{16,0},{1,17},{17,1},{2,18},{18,2},{3,19},{19,3},{4,20},{20... | collective-permute-start | bytes 208904 | tf_op jit(solution)/shard_map/ppermute | solution.py:28
  10.2 0.0 copy-done.1
  10.2 0.0 copy-done.2
  10.2 4.1 %inner_planes.1 = (bf16[16,256,128]{2,1,0:T(8,128)(2,1)}, bf16[14,256,128]{2,1,0:T(8,128)(2,1)S(1)}, bf16[14,16,128]{2,1,0:T(8,128)(2,1)S(1)}, f32[384,384]{1,0:...) custom-call(bf16[16,256,128]{2,1,0:T(8,128)(2,1)S(1)} %bitcast.33, bf16[16,256,128]{2,1,0:T(8,128)(2,1)S(1)} %bitcast.35, ...), custom_call_target="tpu_custom_call" | custom-call | flops 4400000000 | tf_op jit(solution)/shard_map/inner_planes/pallas_call | solution.py:498
  14.3 0.0 copy-start.5
  14.3 0.0 collective-permute-done.2.x_near
  14.4 1.9 %edge_planes.1 = (bf16[16,256,128]{2,1,0:T(8,128)(2,1)}, bf16[272,128]{1,0:T(8,128)(2,1)S(1)}, bf16[272,128]{1,0:T(8,128)(2,1)S(1)}, bf16[272,128]{1,0:T(8,128)(...) custom-call(bf16[16,256,128]{2,1,0:T(8,128)(2,1)S(1)} %bitcast.34, ...), custom_call_target="tpu_custom_call", output_to_operand_aliasing={{0}: (10, {})} | custom-call | flops 2200000000 | tf_op jit(solution)/shard_map/edge_planes/pallas_call | solution.py:523
  16.3 0.0 copy-done.5
  16.3 0.1 collective-permute-start.4
  16.4 1.5 %collective-permute-done.4 = f32[4,7,16,128]{3,2,1,0:T(8,128)S(1)} collective-permute-done((f32[4,7,16,128]{3,2,1,0:T(8,128)S(1)}, f32[4,7,16,128]{3,2,1,0:T(8,128)S(1)}, u32[]{:S(2)}, u32[]{:S(2)}) %collective-permute-start.4) | collective-permute-done | bytes 229408 | tf_op jit(solution)/shard_map/ppermute | solution.py:28
  18.0 1.6 %collective-permute-start.5 = (f32[2,7,16,128]{3,2,1,0:T(8,128)S(1)}, f32[2,7,16,128]{3,2,1,0:T(8,128)S(1)}, u32[]{:S(2)}, u32[]{:S(2)}) collective-permute-start(f32[2,7,16,128]{3,2,1,0:T(8,128)S(1)} %dynamic-slice_bitcast_fusion), channel_id=1, source_target_pairs={{0,1},{1,0},{2,3},{3,2},{4,5},{5,4},{6,7},{7,6},{8,9},{9,8},{10,11... | collective-permute-start | bytes 344072 | tf_op jit(solution)/shard_map/ppermute | solution.py:32
  19.6 3.6 %collective-permute-done.5 = f32[2,7,16,128]{3,2,1,0:T(8,128)S(1)} collective-permute-done((f32[2,7,16,128]{3,2,1,0:T(8,128)S(1)}, f32[2,7,16,128]{3,2,1,0:T(8,128)S(1)}, u32[]{:S(2)}, u32[]{:S(2)}) %collective-permute-start.5) | collective-permute-done | bytes 114720 | tf_op jit(solution)/shard_map/ppermute | solution.py:32
  23.2 0.0 copy-start.3
  23.3 0.0 copy-start.6
  23.3 2.6 %collective-permute-start.6 = (f32[1,7,16,128]{3,2,1,0:T(8,128)S(1)}, f32[1,7,16,128]{3,2,1,0:T(8,128)S(1)}, u32[]{:S(2)}, u32[]{:S(2)}) collective-permute-start(f32[1,7,16,128]{3,2,1,0:T(8,128)S(1)} %constant_dynamic-slice_fusion), channel_id=1, source_target_pairs={{0,2},{1,3},{2,0},{3,1},{4,6},{5,7},{6,4},{7,5},{8,10},{9,11},{10,... | collective-permute-start | bytes 172040 | tf_op jit(solution)/shard_map/ppermute | solution.py:32
  25.9 0.0 copy-done.3
  25.9 1.0 %back_weights.1 = (bf16[512,768]{1,0:T(8,128)(2,1)S(1)}, f32[14,8,128]{2,1,0:T(8,128)S(1)}) custom-call(bf16[3,3,3,64,64]{4,3,2,1,0:T(8,128)(2,1)S(1)} %copy-done.2, s32[3,3,3]{2,1,0:T(4,128)S(1)} %copy-done.3), custom_call_target="tpu_custom_call" | custom-call | flops 2200000000 | tf_op jit(solution)/shard_map/back_weights/pallas_call | solution.py:462
  26.9 0.6 %collective-permute-start.3 = (bf16[272,128]{1,0:T(8,128)(2,1)S(1)}, bf16[272,128]{1,0:T(8,128)(2,1)S(1)}, u32[]{:S(2)}, u32[]{:S(2)}) collective-permute-start(bf16[272,128]{1,0:T(8,128)(2,1)S(1)} %get-tuple-element.29), channel_id=1, source_target_pairs={{0,16},{16,0},{1,17},{17,1},{2,18},{18,2},{3,19},{19,3},{4,20},{20... | collective-permute-start | bytes 208904 | tf_op jit(solution)/shard_map/ppermute | solution.py:28
  27.5 0.9 %collective-permute-done.6 = f32[1,7,16,128]{3,2,1,0:T(8,128)S(1)} collective-permute-done((f32[1,7,16,128]{3,2,1,0:T(8,128)S(1)}, f32[1,7,16,128]{3,2,1,0:T(8,128)S(1)}, u32[]{:S(2)}, u32[]{:S(2)}) %collective-permute-start.6) | collective-permute-done | bytes 57376 | tf_op jit(solution)/shard_map/ppermute | solution.py:32
  28.4 1.1 %collective-permute-start.7 = (f32[7,16,128]{2,1,0:T(8,128)S(1)}, f32[7,16,128]{2,1,0:T(8,128)S(1)}, u32[]{:S(2)}, u32[]{:S(2)}) collective-permute-start(f32[7,16,128]{2,1,0:T(8,128)S(1)} %add_bitcast_fusion), channel_id=1, source_target_pairs={{0,8},{4,12},{8,0},{12,4},{1,9},{5,13},{9,1},{13,5},{2,10},{6,14},... | collective-permute-start | bytes 172040 | tf_op jit(solution)/shard_map/ppermute | solution.py:32
  29.5 0.0 copy-done.6
  29.5 1.9 %input_grad.3.refs_5_ = bf16[16,256,128]{2,1,0:T(8,128)(2,1)} custom-call(bf16[14,256,128]{2,1,0:T(8,128)(2,1)S(1)} %copy-done.6, bf16[14,16,128]{2,1,0:T(8,128)(2,1)S(1)} %get-tuple-element.26.refs_1_, bf16[272,128]{1,0:T(8,128)(2,1)S(1)} %get-tuple-element.27.refs_2_, bf16[272,128]{1,0:T(8,128)(2,1)S(1)} %get-tuple-element.28.refs_3_, ...), custom_call_target="tpu_custom_call" | custom-call | flops 2750000128 | tf_op jit(solution)/shard_map/input_grad/pallas_call | solution.py:569
  31.4 1.2 %collective-permute-done.7 = f32[7,16,128]{2,1,0:T(8,128)S(1)} collective-permute-done((f32[7,16,128]{2,1,0:T(8,128)S(1)}, f32[7,16,128]{2,1,0:T(8,128)S(1)}, u32[]{:S(2)}, u32[]{:S(2)}) %collective-permute-start.7) | collective-permute-done | bytes 57376 | tf_op jit(solution)/shard_map/ppermute | solution.py:32
  32.7 0.7 %collective-permute-start.8 = (f32[7,16,128]{2,1,0:T(8,128)S(1)}, f32[7,16,128]{2,1,0:T(8,128)S(1)}, u32[]{:S(2)}, u32[]{:S(2)}) collective-permute-start(f32[7,16,128]{2,1,0:T(8,128)S(1)} %add.73), channel_id=1, source_target_pairs={{0,16},{16,0},{1,17},{17,1},{2,18},{18,2},{3,19},{19,3},{4,20},{20... | collective-permute-start | bytes 172040 | tf_op jit(solution)/shard_map/ppermute | solution.py:32
  33.3 1.7 %input_grad.4.refs_7_ = bf16[16,256,128]{2,1,0:T(8,128)(2,1)} custom-call(bf16[14,256,128]{2,1,0:T(8,128)(2,1)S(1)} %copy-done.6, bf16[14,16,128]{2,1,0:T(8,128)(2,1)S(1)} %get-tuple-element.26.refs_1_, bf16[272,128]{1,0:T(8,128)(2,1)S(1)} %get-tuple-element.27.refs_2_, ...), custom_call_target="tpu_custom_call", output_to_operand_aliasing={{}: (5, {})} | custom-call | flops 2750000128 | tf_op jit(solution)/shard_map/input_grad/pallas_call | solution.py:569
  35.0 1.9 %collective-permute-done.8 = f32[7,16,128]{2,1,0:T(8,128)S(1)} collective-permute-done((f32[7,16,128]{2,1,0:T(8,128)S(1)}, f32[7,16,128]{2,1,0:T(8,128)S(1)}, u32[]{:S(2)}, u32[]{:S(2)}) %collective-permute-start.8) | collective-permute-done | bytes 57376 | tf_op jit(solution)/shard_map/ppermute | solution.py:32
  36.9 0.1 collective-permute-start.9
  37.0 0.0 collective-permute-done.3.refs_4_
  37.0 1.1 %input_grad.5 = bf16[16,256,128]{2,1,0:T(8,128)(2,1)} custom-call(bf16[14,256,128]{2,1,0:T(8,128)(2,1)S(1)} %copy-done.6, bf16[14,16,128]{2,1,0:T(8,128)(2,1)S(1)} %get-tuple-element.26.refs_1_, bf16[272,128]{1,0:T(8,128)(2,1)S(1)} %get-tuple-element.27.refs_2_, bf16[272,128]{1,0:T(8,128)(2,1)S(1)} %get-tuple-element.28.refs_3_, ...), custom_call_target="tpu_custom_call", output_to_operand_aliasing={{}: (7, {})} | custom-call | flops 2750000128 | tf_op jit(solution)/shard_map/input_grad/pallas_call | solution.py:569
  38.2 0.1 collective-permute-done.9.other
  38.3 0.7 %scale_weight_grad.1 = (bf16[27,16,64]{2,1,0:T(8,128)(2,1)}, f32[1,16]{1,0:T(1,128)}) custom-call(f32[7,16,128]{2,1,0:T(8,128)S(1)} %add.74.own, f32[7,16,128]{2,1,0:T(8,128)S(1)} %collective-permute-done.9.other, f32[14,8,128]{2,1,0:T(8,128)S(1)} %get-tuple-element.33.scale_ref), custom_call_target="tpu_custom_call" | custom-call | tf_op jit(solution)/shard_map/scale_weight_grad/pallas_call | solution.py:609
  (15 shorter events, 0.2 us)
Async XLA Ops:
  1.5 7.0 %collective-permute-start.1 = (bf16[16,4,128]{2,1,0:T(4,128)(2,1)S(1)}, bf16[16,4,128]{2,1,0:T(4,128)(2,1)S(1)}, u32[]{:S(2)}, u32[]{:S(2)}) collective-permute-start(bf16[16,4,128]{2,1,0:T(4,128)(2,1)S(1)} %pad_maximum_fusion.1.rim_in), channel_id=1, source_target_pairs={{4,8},{8,4},{5,9},{9,5},{6,10},{10,6},{7,11},{11,7},{20,24},{24,20... | collective-permute-start | bytes 49160 | tf_op jit(solution)/shard_map/ppermute | solution.py:28
  2.2 6.3 %collective-permute-start = (bf16[16,4,128]{2,1,0:T(4,128)(2,1)S(1)}, bf16[16,4,128]{2,1,0:T(4,128)(2,1)S(1)}, u32[]{:S(2)}, u32[]{:S(2)}) collective-permute-start(bf16[16,4,128]{2,1,0:T(4,128)(2,1)S(1)} %pad_maximum_fusion), channel_id=1, source_target_pairs={{0,4},{4,0},{8,12},{12,8},{1,5},{5,1},{9,13},{13,9},{2,6},{6,2},{1... | collective-permute-start | bytes 49160 | tf_op jit(solution)/shard_map/ppermute | solution.py:28
  6.6 0.7 %copy-start.4 = (f32[64]{0:T(128)S(1)}, f32[64]{0:T(128)}, u32[]{:S(2)}) copy-start(f32[64]{0:T(128)} %offsets.1) | copy-start | bytes 772
  7.3 1.2 %copy-start = (bf16[1,16,256,128]{3,2,1,0:T(8,128)(2,1)S(1)}, bf16[1,16,256,128]{3,2,1,0:T(8,128)(2,1)}, u32[]{:S(2)}) copy-start(bf16[1,16,256,128]{3,2,1,0:T(8,128)(2,1)} %param.5) | copy-start | bytes 3145732
  7.3 2.9 %copy-start.1 = (bf16[1,16,256,128]{3,2,1,0:T(8,128)(2,1)S(1)}, bf16[1,16,256,128]{3,2,1,0:T(8,128)(2,1)}, u32[]{:S(2)}) copy-start(bf16[1,16,256,128]{3,2,1,0:T(8,128)(2,1)} %param.8) | copy-start | bytes 3145732
  7.3 2.9 %copy-start.2 = (bf16[3,3,3,64,64]{4,3,2,1,0:T(8,128)(2,1)S(1)}, bf16[3,3,3,64,64]{4,3,2,1,0:T(8,128)(2,1)}, u32[]{:S(2)}) copy-start(bf16[3,3,3,64,64]{4,3,2,1,0:T(8,128)(2,1)} %refs_0_.1) | copy-start | bytes 663556
  8.7 5.7 %collective-permute-start.2 = (bf16[272,128]{1,0:T(8,128)(2,1)S(1)}, bf16[272,128]{1,0:T(8,128)(2,1)S(1)}, u32[]{:S(2)}, u32[]{:S(2)}) collective-permute-start(bf16[272,128]{1,0:T(8,128)(2,1)S(1)} %concatenate.11), channel_id=1, source_target_pairs={{0,16},{16,0},{1,17},{17,1},{2,18},{18,2},{3,19},{19,3},{4,20},{20... | collective-permute-start | bytes 208904 | tf_op jit(solution)/shard_map/ppermute | solution.py:28
  14.3 2.0 %copy-start.5 = (bf16[14,256,128]{2,1,0:T(8,128)(2,1)}, bf16[14,256,128]{2,1,0:T(8,128)(2,1)S(1)}, u32[]{:S(2)}) copy-start(bf16[14,256,128]{2,1,0:T(8,128)(2,1)S(1)} %get-tuple-element.25.refs_0_) | copy-start | bytes 2752516
  16.3 1.6 %collective-permute-start.4 = (f32[4,7,16,128]{3,2,1,0:T(8,128)S(1)}, f32[4,7,16,128]{3,2,1,0:T(8,128)S(1)}, u32[]{:S(2)}, u32[]{:S(2)}) collective-permute-start(f32[4,7,16,128]{3,2,1,0:T(8,128)S(1)} %get-tuple-element.31.refs_5_.refs_6_.refs_8_), channel_id=1, source_target_pairs={{0,4},{4,0},{8,12},{12,8},{1,5},{5,1},{9,13},{13,9},{2,6},{6,2},{1... | collective-permute-start | bytes 688136 | tf_op jit(solution)/shard_map/ppermute | solution.py:28
  18.0 5.3 %collective-permute-start.5 = (f32[2,7,16,128]{3,2,1,0:T(8,128)S(1)}, f32[2,7,16,128]{3,2,1,0:T(8,128)S(1)}, u32[]{:S(2)}, u32[]{:S(2)}) collective-permute-start(f32[2,7,16,128]{3,2,1,0:T(8,128)S(1)} %dynamic-slice_bitcast_fusion), channel_id=1, source_target_pairs={{0,1},{1,0},{2,3},{3,2},{4,5},{5,4},{6,7},{7,6},{8,9},{9,8},{10,11... | collective-permute-start | bytes 344072 | tf_op jit(solution)/shard_map/ppermute | solution.py:32
  23.2 2.7 %copy-start.3 = (s32[3,3,3]{2,1,0:T(4,128)S(1)}, s32[3,3,3]{2,1,0:T(4,128)}, u32[]{:S(2)}) copy-start(s32[3,3,3]{2,1,0:T(4,128)} %refs_1_.1) | copy-start | bytes 328
  23.3 6.2 %copy-start.6 = (bf16[14,256,128]{2,1,0:T(8,128)(2,1)S(1)}, bf16[14,256,128]{2,1,0:T(8,128)(2,1)}, u32[]{:S(2)}) copy-start(bf16[14,256,128]{2,1,0:T(8,128)(2,1)} %copy-done.5) | copy-start | bytes 2752516
  23.3 5.1 %collective-permute-start.6 = (f32[1,7,16,128]{3,2,1,0:T(8,128)S(1)}, f32[1,7,16,128]{3,2,1,0:T(8,128)S(1)}, u32[]{:S(2)}, u32[]{:S(2)}) collective-permute-start(f32[1,7,16,128]{3,2,1,0:T(8,128)S(1)} %constant_dynamic-slice_fusion), channel_id=1, source_target_pairs={{0,2},{1,3},{2,0},{3,1},{4,6},{5,7},{6,4},{7,5},{8,10},{9,11},{10,... | collective-permute-start | bytes 172040 | tf_op jit(solution)/shard_map/ppermute | solution.py:32
  26.9 10.1 %collective-permute-start.3 = (bf16[272,128]{1,0:T(8,128)(2,1)S(1)}, bf16[272,128]{1,0:T(8,128)(2,1)S(1)}, u32[]{:S(2)}, u32[]{:S(2)}) collective-permute-start(bf16[272,128]{1,0:T(8,128)(2,1)S(1)} %get-tuple-element.29), channel_id=1, source_target_pairs={{0,16},{16,0},{1,17},{17,1},{2,18},{18,2},{3,19},{19,3},{4,20},{20... | collective-permute-start | bytes 208904 | tf_op jit(solution)/shard_map/ppermute | solution.py:28
  28.4 4.2 %collective-permute-start.7 = (f32[7,16,128]{2,1,0:T(8,128)S(1)}, f32[7,16,128]{2,1,0:T(8,128)S(1)}, u32[]{:S(2)}, u32[]{:S(2)}) collective-permute-start(f32[7,16,128]{2,1,0:T(8,128)S(1)} %add_bitcast_fusion), channel_id=1, source_target_pairs={{0,8},{4,12},{8,0},{12,4},{1,9},{5,13},{9,1},{13,5},{2,10},{6,14},... | collective-permute-start | bytes 172040 | tf_op jit(solution)/shard_map/ppermute | solution.py:32
  32.7 4.2 %collective-permute-start.8 = (f32[7,16,128]{2,1,0:T(8,128)S(1)}, f32[7,16,128]{2,1,0:T(8,128)S(1)}, u32[]{:S(2)}, u32[]{:S(2)}) collective-permute-start(f32[7,16,128]{2,1,0:T(8,128)S(1)} %add.73), channel_id=1, source_target_pairs={{0,16},{16,0},{1,17},{17,1},{2,18},{18,2},{3,19},{19,3},{4,20},{20... | collective-permute-start | bytes 172040 | tf_op jit(solution)/shard_map/ppermute | solution.py:32
  36.9 1.3 %collective-permute-start.9 = (f32[7,16,128]{2,1,0:T(8,128)S(1)}, f32[7,16,128]{2,1,0:T(8,128)S(1)}, u32[]{:S(2)}, u32[]{:S(2)}) collective-permute-start(f32[7,16,128]{2,1,0:T(8,128)S(1)} %add.74.own), channel_id=1, source_target_pairs={{0,4},{4,0},{8,12},{12,8},{1,5},{5,1},{9,13},{13,9},{2,6},{6,2},{1... | collective-permute-start | bytes 172040 | tf_op jit(solution)/shard_map/ppermute | solution.py:28

commit v4 on v3

--- a/solution.py
+++ b/solution.py
@@ -21,15 +21,28 @@
 def swap(value, axis, first):
     count = lax.axis_size(axis)
     links = []
-    for low in range(first, count - 1, 2):
-        links += [(low, low + 1), (low + 1, low)]
-    if not links:
-        return jnp.zeros_like(value)
+    for low in range(first, count, 2):
+        high = (low + 1) % count
+        links += [(low, high), (high, low)]
     return lax.ppermute(value, axis, links)
 
 
 def exchange(value, axis, step):
-    return lax.ppermute(value, axis, [(i, i ^ step) for i in range(lax.axis_size(axis))])
+    axes = ("gx", "gy", "dp")
+    sizes = [lax.axis_size(name) for name in axes]
+    stride = {name: math.prod(sizes[i + 1 :]) for i, name in enumerate(axes)}
+    flip = (step * stride[axis]) ^ stride["gy"]
+    return lax.ppermute(value, axes, [(i, i ^ flip) for i in range(math.prod(sizes))])
+
+
+def half_kept():
+    side = lax.axis_index("gy") % 2
+    for axis, first in (("gx", 1), ("gy", 2), ("dp", 1)):
+        step = first
+        while step < lax.axis_size(axis):
+            side = side + lax.axis_index(axis) // step
+            step *= 2
+    return side % 2
 
 
 def tap_block(taps, a, b):
@@ -43,11 +56,6 @@
     blank = jnp.zeros((width, 3 * width), BF16)
     out[3 * width :, : 3 * width] = blank
     out[:width, 3 * width :] = blank
-
-
-def bias_kernel(offsets, rim_in, bias_ref):
-    bias = offsets[...].reshape(1, bias_ref.shape[1] // 2)
-    bias_ref[...] = jnp.concatenate([bias, bias], axis=1)
 
 
 def build_front(taps, w_ref, narrow_ref):
@@ -170,53 +178,166 @@
         place(near, far)
 
 
-def place_rims(y_near, y_far, f_rim, u_rim):
+def beside(axis, near, far, place, clear_low, clear_high):
+    index = lax.axis_index(axis)
+    oriented(near, far, index % 2, place)
+    pl.when(index == 0)(clear_low)
+    pl.when(index == lax.axis_size(axis) - 1)(clear_high)
+
+
+def place_rims(y_near, y_far, f_rim, u_rim, gap):
+    low = slice(gap, gap + THIN)
+    high = slice(2 * RIM - gap - THIN, 2 * RIM - gap)
+
+    def place(left, right):
+        f_rim[:, low, :] = left[:, :THIN, :]
+        u_rim[:, low, :] = left[:, THIN:, :]
+        f_rim[:, high, :] = right[:, :THIN, :]
+        u_rim[:, high, :] = right[:, THIN:, :]
+
+    def clear(rows):
+        blank = jnp.zeros((f_rim.shape[0], THIN, f_rim.shape[2]), BF16)
+        f_rim[:, rows, :] = blank
+        u_rim[:, rows, :] = blank
+
     for ref in (f_rim, u_rim):
         ref[...] = jnp.zeros(ref.shape, BF16)
-
-    def place(left, right):
-        f_rim[:, RIM - THIN : RIM, :] = left[:, :THIN, :]
-        f_rim[:, RIM : RIM + THIN, :] = right[:, :THIN, :]
-        u_rim[:, RIM - THIN : RIM, :] = left[:, THIN:, :]
-        u_rim[:, RIM : RIM + THIN, :] = right[:, THIN:, :]
-
-    oriented(y_near, y_far, lax.axis_index("gy") % 2, place)
-
-
-def inner_kernel(
-    f_ref, u_ref, y_near, y_far, kernel_ref, bias_ref,
-    act_hbm, grad_ref, rim_ref, acc_ref, sums_ref, narrow_ref,
-    f_rim, u_rim, act, taps, wide, turned, w_ref, sems,
+    beside("gy", y_near, y_far, place, lambda: clear(low), lambda: clear(high))
+
+
+def place_planes(x_near, x_far, around):
+    def place(below, above):
+        around[0] = below[...]
+        around[1] = above[...]
+
+    def clear(k):
+        around[k] = jnp.zeros(around.shape[1:], BF16)
+
+    beside("gx", x_near, x_far, place, lambda: clear(0), lambda: clear(1))
+
+
+def rims_kernel(ends, near_ref, far_ref):
+    rows = ends.shape[1] // 2
+
+    def hand(tail, head):
+        tail[...] = ends[:, rows:, :]
+        head[...] = ends[:, :rows, :]
+
+    oriented(far_ref, near_ref, lax.axis_index("gy") % 2, hand)
+
+
+def planes_kernel(f_ref, y_near, y_far, near_ref, far_ref=None):
+    size_x, size_y, width = f_ref.shape
+    low = slice(size_y + RIM - THIN, size_y + RIM)
+    high = slice(size_y + RIM, size_y + RIM + THIN)
+
+    def fill(out, x):
+        out[:size_y] = f_ref[x]
+        out[size_y:] = jnp.zeros((2 * RIM, width), BF16)
+
+        def place(left, right):
+            out[low] = left[x, :THIN]
+            out[high] = right[x, :THIN]
+
+        def clear(rows):
+            out[rows] = jnp.zeros((THIN, width), BF16)
+
+        beside("gy", y_near, y_far, place, lambda: clear(low), lambda: clear(high))
+
+    def hand(last, first):
+        if last is not None:
+            fill(last, size_x - 1)
+        if first is not None:
+            fill(first, 0)
+
+    oriented(far_ref, near_ref, lax.axis_index("gx") % 2, hand)
+
+
+def front_kernel(
+    f_ref, kernel_ref, offsets, pre_ref, turned, narrow_ref, bias_ref, w_ref, taps
 ):
     size_x, size_y, width = f_ref.shape
+    inner = size_x - 2
     build_front(kernel_ref, w_ref, narrow_ref)
-    inner = size_x - 2
-    place_rims(y_near, y_far, f_rim, u_rim)
-    bias = bias_ref[...]
-    rim_taps(
-        taps,
-        range(inner),
-        [[f_rim[x + j] for j in range(3)] for x in range(inner)],
-        w_ref[: 3 * width, : 3 * width],
-    )
-    sums = jnp.zeros((8, width), F32)
-    stores = []
-    pairs = range(0, inner, 2)
-
-    def multiply(p):
+    bias = offsets[...].reshape(1, width // 2)
+    bias = jnp.concatenate([bias, bias], axis=1)
+    bias_ref[...] = bias
+    blank = jnp.zeros((3, inner, RIM, width), F32)
+    taps[:, :, PAD - RIM : PAD, :] = blank
+    taps[:, :, PAD + size_y : PAD + size_y + RIM, :] = blank
+    for p in range(0, inner, 2):
         plane_taps(taps, (p, p + 1), [f_ref[p + j] for j in range(4)], w_ref[...])
         for x in range(0 if p == 0 else p + 2, p + 4):
             turned[x] = f_ref[x].T
-
-    multiply(0)
-    for p in pairs:
-        if p + 2 < inner:
-            multiply(p + 2)
         for q in (p, p + 1):
-            sums = activate(
-                taps, wide, q, bias, sums, u_ref.at[q + 1], u_rim.at[q + 1],
-                act.at[q], grad_ref.at[q], rim_ref.at[q],
+            for y in range(0, size_y, CHUNK):
+                pre_ref[q, y : y + CHUNK, :] = shifted_sum(taps, q, PAD + y, CHUNK) + bias
+
+
+def gradient(preact, cotangent):
+    sigma = 0.5 * jnp.tanh(0.5 * preact) + 0.5
+    rounded = (
+        cotangent.astype(F32) * sigma * (1.0 + preact * (1.0 - sigma))
+    ).astype(BF16)
+    return preact * sigma, rounded, rounded.astype(F32)
+
+
+def inner_kernel(
+    f_ref, u_ref, y_near, y_far, pre_ref, turned, w_ref, bias_ref,
+    act_hbm, grad_ref, rim_ref, acc_ref, sums_ref,
+    f_rim, u_rim, act, wide, sems,
+):
+    size_x, size_y, width = f_ref.shape
+    inner = size_x - 2
+    gap = RIM - 2 * THIN
+
+    place_rims(y_near, y_far, f_rim, u_rim, gap)
+    f_rim[:, gap + THIN : RIM, :] = f_ref[:, :THIN, :]
+    f_rim[:, RIM : RIM + THIN, :] = f_ref[:, size_y - THIN :, :]
+    bias = bias_ref[...]
+    rows = 2 * RIM
+    tall = [
+        jnp.concatenate([f_rim[x + j] for x in range(inner)], axis=0) for j in range(3)
+    ]
+    strips = jnp.dot(
+        jnp.concatenate(tall, axis=1), w_ref[...], preferred_element_type=F32
+    )
+    row = lax.broadcasted_iota(jnp.int32, (RIM, width), 0)
+    sums = jnp.zeros((8, width), F32)
+    stores = []
+    for p in range(0, inner, 2):
+        for q in (p, p + 1):
+            strip = [
+                strips[q * rows : (q + 1) * rows, b * width : (b + 1) * width] for b in range(3)
+            ]
+            for side in range(2):
+                part = [tap[side * RIM : (side + 1) * RIM] for tap in strip]
+                preact = (
+                    pltpu.roll(part[0], 1, 0) + part[1] + pltpu.roll(part[2], RIM - 1, 0) + bias
+                )
+                _, rounded, exact = gradient(
+                    preact, u_rim[q + 1, side * RIM : (side + 1) * RIM, :]
+                )
+                turn = THIN if side == 0 else RIM - THIN
+                exact = pltpu.roll(exact, turn, 0)
+                start = PAD - RIM if side == 0 else PAD + size_y
+                wide[q, start : start + RIM, :] = exact
+                rim_ref[q, side * RIM : (side + 1) * RIM, :] = exact.astype(BF16)
+            low = jnp.where(row == 0, pltpu.roll(strip[0][:RIM], RIM - gap - THIN + 1, 0), 0.0)
+            high = jnp.where(
+                row == RIM - 1, pltpu.roll(strip[2][RIM:], RIM - 1 - THIN, 0), 0.0
             )
+            for y in range(0, size_y, CHUNK):
+                preact = pre_ref[q, y : y + CHUNK, :]
+                if y == 0:
+                    preact = jnp.concatenate([preact[:RIM] + low, preact[RIM:]], axis=0)
+                if y + CHUNK == size_y:
+                    preact = jnp.concatenate([preact[:-RIM], preact[-RIM:] + high], axis=0)
+                value, rounded, exact = gradient(preact, u_ref[q + 1, y : y + CHUNK, :])
+                wide[q, PAD + y : PAD + y + CHUNK, :] = exact
+                act[q, y : y + CHUNK, :] = value.astype(BF16)
+                grad_ref[q, y : y + CHUNK, :] = rounded
+                sums = sums + jnp.sum(exact.reshape(CHUNK // 8, 8, width), axis=0)
         stores.append(
             pltpu.make_async_copy(
                 act.at[pl.ds(p, 2)], act_hbm.at[pl.ds(p + 1, 2)], sems.at[p // 2]
@@ -236,23 +357,62 @@
         copy.wait()
 
 
+def emit_half(acc, sums, out, which):
+    parts, count, share, width = out.shape
+    half = width // 2
+
+    def block(t):
+        a, b = t // 3, t % 3
+        return acc[a * width : (a + 1) * width, b * width : (b + 1) * width].T
+
+    def lower(rows):
+        return lax.broadcasted_iota(jnp.int32, (rows, width), 1) < half
+
+    def middle(t):
+        whole = block(t)
+        rolled = pltpu.roll(whole[half:], half, 1)
+        return whole[:half] + jnp.where(lower(half), rolled, 0.0)
+
+    def put(s, value):
+        for d in range(parts):
+            out[d, s] = value[d * share : (d + 1) * share]
+
+    @pl.when(which == 0)
+    def _():
+        for s in range(count):
+            put(s, middle(s))
+
+    @pl.when(which == 1)
+    def _():
+        for t in range(count, 9):
+            put(t - count, middle(t))
+        for t in range(0, 9, 2):
+            low = block(t)[half:]
+            if t + 1 < 9:
+                high = pltpu.roll(block(t + 1)[half:], half, 1)
+                put(9 + t // 2 - count, jnp.where(lower(half), low, high))
+                continue
+            both = jnp.sum(sums, axis=0, keepdims=True)
+            both = jnp.broadcast_to(both + pltpu.roll(both, half, 1), (share, width))
+            for d in range(parts):
+                turned = pltpu.roll(both, (half - d * share) % width, 1)
+                mine = low[d * share : (d + 1) * share]
+                out[d, count - 1] = jnp.where(lower(share), mine, turned)
+
+
+def keep_kernel(acc, sums, keep_ref):
+    emit_half(acc, sums[...], keep_ref, half_kept())
+
+
 def edge_kernel(
     f_ref, u_ref, y_near, y_far, x_near, x_far, w_ref, bias_ref, acc_ref, sums_ref, act_in,
-    act_hbm, first_ref, last_ref, near_ref, far_ref, keep_ref, send_ref,
-    f_rim, u_rim, around, act, taps, wide, acc, sems,
+    act_hbm, first_ref, last_ref, near_ref, far_ref, acc, bias_sums, send_ref,
+    f_rim, u_rim, around, act, taps, wide, sems,
 ):
     size_x, size_y, width = f_ref.shape
-    half = width // 2
-    parts, _, share, _ = keep_ref.shape
-    y_side = lax.axis_index("gy") % 2
     x_side = lax.axis_index("gx") % 2
-    place_rims(y_near, y_far, f_rim, u_rim)
-
-    def place(below, above):
-        around[0] = below[...]
-        around[1] = above[...]
-
-    oriented(x_near, x_far, x_side, place)
+    place_rims(y_near, y_far, f_rim, u_rim, RIM - THIN)
+    place_planes(x_near, x_far, around)
     bias = bias_ref[...]
     weights = w_ref[...]
     tall = size_y + 2 * RIM
@@ -292,44 +452,8 @@
 
     oriented(far_ref, near_ref, x_side, lambda low, high: hand(low, high))
 
-    lane = lax.broadcasted_iota(jnp.int32, (half, width), 1)
-    lower = lane < half
-    slots, tails = [], []
-    for a in range(3):
-        for b in range(3):
-            block = acc[a * width : (a + 1) * width, b * width : (b + 1) * width].T
-            top, bottom = block[:half], block[half:]
-            rolled = pltpu.roll(bottom, half, 1)
-            slots.append(top + jnp.where(lower, rolled, 0.0))
-            tails.append((bottom, rolled))
-    for t in range(0, 8, 2):
-        slots.append(jnp.where(lower, tails[t][0], tails[t + 1][1]))
-    both = jnp.sum(sums, axis=0, keepdims=True)
-    both = jnp.broadcast_to(both + pltpu.roll(both, half, 1), (share, width))
-    spare = [
-        jnp.where(
-            lower[:share],
-            tails[8][0][d * share : (d + 1) * share],
-            pltpu.roll(both, (half - d * share) % width, 1),
-        )
-        for d in range(parts)
-    ]
-
-    def emit(first, second):
-        for s in range(SLOTS):
-            out = first if s < SLOTS // 2 else second
-            for d in range(parts):
-                part = spare[d] if s == SLOTS - 1 else slots[s][d * share : (d + 1) * share]
-                out[d, s % (SLOTS // 2)] = part
-
-    @pl.when(y_side == 0)
-    def _():
-        emit(keep_ref, send_ref)
-
-    @pl.when(y_side == 1)
-    def _():
-        emit(send_ref, keep_ref)
-
+    bias_sums[...] = sums
+    emit_half(acc, sums, send_ref, 1 - half_kept())
     for copy in stores:
         copy.wait()
 
@@ -361,24 +485,20 @@
         return rim_ref[x - 1]
 
     if edges:
-
-        def place(below, above):
-            around[0] = below[...]
-            around[1] = above[...]
-
-        oriented(x_near, x_far, lax.axis_index("gx") % 2, place)
+        place_planes(x_near, x_far, around)
     narrow = w_ref[: 3 * width, : 3 * width]
-    planes = [0, size_x - 1] if edges else [x for first in pairs for x in (first, first + 1)]
+    planes = [x for first in pairs for x in (first, first + 1)]
+    planes += [0, size_x - 1] if edges else []
     rim_taps(taps, range(len(planes)), [[rim(x + j) for j in (-1, 0, 1)] for x in planes], narrow)
     stores = []
 
     def multiply(k):
         x = planes[k]
-        if edges:
-            for i in range(2):
+        if planes[k + 1] == x + 1:
+            plane_taps(taps, (k, k + 1), [body(x + j) for j in (-1, 0, 1, 2)], w_ref[...])
+        else:
+            for i in (k, k + 1):
                 plane_taps(taps, (i,), [body(planes[i] + j) for j in (-1, 0, 1)], narrow)
-        else:
-            plane_taps(taps, (k, k + 1), [body(x + j) for j in (-1, 0, 1, 2)], w_ref[...])
 
     multiply(0)
     for k in range(0, len(planes), 2):
@@ -395,6 +515,23 @@
         copy.wait()
 
 
+def split_kernel(step, mine, received, keep_ref, send_ref):
+    total = mine[...] + received[...].astype(F32)
+    bit = (lax.axis_index("dp") // step) % 2
+
+    def place(first, second):
+        for k in range(keep_ref.shape[0]):
+            keep_ref[k] = total[2 * k + first]
+            send_ref[k] = total[2 * k + second].astype(BF16)
+
+    pl.when(bit == 0)(lambda: place(0, 1))
+    pl.when(bit == 1)(lambda: place(1, 0))
+
+
+def add_kernel(mine, received, total_ref):
+    total_ref[...] = mine[...] + received[...].astype(F32)
+
+
 def finish_kernel(own, other, scale_ref, grad_ref, bias_ref):
     share, half = grad_ref.shape[1:]
 
@@ -409,11 +546,13 @@
             else:
                 bias_ref[...] = high[:1, :share]
 
-    @pl.when(lax.axis_index("gy") % 2 == 0)
+    kept = half_kept()
+
+    @pl.when(kept == 0)
     def _():
         emit(own, other)
 
-    @pl.when(lax.axis_index("gy") % 2 == 1)
+    @pl.when(kept == 1)
     def _():
         emit(other, own)
 
@@ -439,63 +578,75 @@
     tall, rows = size_y + 2 * RIM, size_y + 2 * PAD
     parts = lax.axis_size("dp")
     share = half // parts
-    y_side = lax.axis_index("gy") % 2
-    x_side = lax.axis_index("gx") % 2
-
-    def rim(start):
-        return jnp.concatenate(
-            [
-                lax.dynamic_slice_in_dim(cells, start, THIN, axis=1),
-                lax.dynamic_slice_in_dim(cotangent, start, THIN, axis=1),
-            ],
-            axis=1,
-        )
-
-    last = size_y - THIN
-    rim_near, rim_far = rim((1 - y_side) * last), rim(y_side * last)
+    sources = (cells, cotangent)
+    ends = jnp.concatenate(
+        [source[:, :THIN] for source in sources] + [source[:, size_y - THIN :] for source in sources],
+        axis=1,
+    )
+    rim_near, rim_far = pl.pallas_call(
+        rims_kernel,
+        out_shape=(shape(size_x, 2 * THIN, width),) * 2,
+        in_specs=[VMEM],
+        out_specs=(VMEM, VMEM),
+        compiler_params=grant(1),
+        cost_estimate=cost(3.0),
+        name="pack_rims",
+    )(ends)
     y_near = swap(rim_near, "gy", 0)
     y_far = swap(rim_far, "gy", 1)
 
     voxels = (
         features.shape[0] * parts * size_x * lax.axis_size("gx") * size_y * lax.axis_size("gy") * 2
     )
-    backward_weights, scales = pl.pallas_call(
-        lambda *refs: back_weights_kernel(1.0 / math.sqrt(voxels), *refs),
-        out_shape=(shape(4 * width, 6 * width), shape(SLOTS, 8, width, dtype=F32)),
-        in_specs=[VMEM, SMEM],
-        out_specs=(VMEM, VMEM),
-        compiler_params=grant(4),
+    def back_weights(taps):
+        return pl.pallas_call(
+            lambda *refs: back_weights_kernel(1.0 / math.sqrt(voxels), *refs),
+            out_shape=(shape(4 * width, 6 * width), shape(SLOTS, 8, width, dtype=F32)),
+            in_specs=[VMEM, SMEM],
+            out_specs=(VMEM, VMEM),
+            compiler_params=grant(4),
+            cost_estimate=cost(1.0),
+            name="back_weights",
+        )(taps, grad_exponents)
+
+    inner = size_x - 2
+    preact, turned, forward_weights, bias = pl.pallas_call(
+        front_kernel,
+        out_shape=(
+            shape(inner, size_y, width, dtype=F32),
+            shape(size_x, width, size_y),
+            shape(3 * width, 3 * width),
+            shape(1, width, dtype=F32),
+        ),
+        in_specs=[VMEM] * 3,
+        out_specs=(VMEM,) * 4,
+        scratch_shapes=[
+            pltpu.VMEM((4 * width, 6 * width), BF16),
+            pltpu.VMEM((3, inner, rows, width), F32),
+        ],
+        compiler_params=grant(16),
         cost_estimate=cost(2.0),
-        name="back_weights",
-    )(kernel, grad_exponents)
-    bias = pl.pallas_call(
-        bias_kernel,
-        out_shape=shape(1, width, dtype=F32),
-        in_specs=[VMEM, ANY],
-        out_specs=VMEM,
-        compiler_params=grant(2),
-        cost_estimate=cost(3.0),
-        name="bias",
-    )(offsets, rim_far)
-
-    def plane(index):
-        near = lax.dynamic_slice_in_dim(y_near, index, 1, axis=0)[0, :THIN]
-        far = lax.dynamic_slice_in_dim(y_far, index, 1, axis=0)[0, :THIN]
-        body = lax.dynamic_slice_in_dim(cells, index, 1, axis=0)[0]
-        left = jnp.where(y_side == 0, far, near)
-        right = jnp.where(y_side == 0, near, far)
-        blank = jnp.zeros((RIM - THIN, width), body.dtype)
-        return jnp.concatenate([body, blank, left, right, blank], axis=0)
-
-    x_near = swap(plane((1 - x_side) * (size_x - 1)), "gx", 0)
-    x_far = swap(plane(x_side * (size_x - 1)), "gx", 1)
-
-    inner = size_x - 2
+        name="front_planes",
+    )(cells, kernel, offsets)
+
+    many = lax.axis_size("gx") > 2
+    plane_sends = pl.pallas_call(
+        planes_kernel,
+        out_shape=(shape(tall, width),) * (1 + many),
+        in_specs=[VMEM] * 3,
+        out_specs=(VMEM,) * (1 + many),
+        compiler_params=grant(1),
+        cost_estimate=cost(0.1),
+        name="pack_planes",
+    )(cells, y_near, y_far)
+    x_near = swap(plane_sends[0], "gx", 0)
+    x_far = swap(plane_sends[1], "gx", 1) if many else x_near
+
     rims = [
         pltpu.VMEM((size_x, 2 * RIM, width), BF16),
         pltpu.VMEM((size_x, 2 * RIM, width), BF16),
     ]
-    activation, grad, grad_rim, acc, sums, forward_weights = pl.pallas_call(
+    activation, grad, grad_rim, acc, sums = pl.pallas_call(
         inner_kernel,
         out_shape=(
             shape(size_x, size_y, width),
@@ -503,24 +654,20 @@
             shape(inner, 2 * RIM, width),
             shape(3 * width, 3 * width, dtype=F32),
             shape(8, width, dtype=F32),
-            shape(3 * width, 3 * width),
         ),
-        in_specs=[VMEM] * 6,
-        out_specs=(ANY,) + (VMEM,) * 5,
+        in_specs=[VMEM] * 8,
+        out_specs=(ANY,) + (VMEM,) * 4,
         scratch_shapes=rims + [
             pltpu.VMEM((inner, size_y, width), BF16),
-            pltpu.VMEM((3, inner, rows, width), F32),
             pltpu.VMEM((inner, rows, width), F32),
-            pltpu.VMEM((size_x, width, size_y), BF16),
-            pltpu.VMEM((4 * width, 6 * width), BF16),
             pltpu.SemaphoreType.DMA((inner // 2,)),
         ],
-        compiler_params=grant(24),
-        cost_estimate=cost(4.0),
+        compiler_params=grant(12),
+        cost_estimate=cost(3.0),
         name="inner_planes",
-    )(cells, cotangent, y_near, y_far, kernel, bias)
-
-    activation, first, final, near, far, keep, send = pl.pallas_call(
+    )(cells, cotangent, y_near, y_far, preact, turned, forward_weights, bias)
+
+    activation, first, final, near, far, acc, sums, send = pl.pallas_call(
         edge_kernel,
         out_shape=(
             shape(size_x, size_y, width),
@@ -528,17 +675,17 @@
             shape(tall, width),
             shape(tall, width),
             shape(tall, width),
-            shape(parts, SLOTS // 2, share, width, dtype=F32),
+            shape(3 * width, 3 * width, dtype=F32),
+            shape(8, width, dtype=F32),
             shape(parts, SLOTS // 2, share, width, dtype=F32),
         ),
         in_specs=[VMEM] * 10 + [ANY],
-        out_specs=(ANY,) + (VMEM,) * 6,
+        out_specs=(ANY,) + (VMEM,) * 7,
         scratch_shapes=rims + [
             pltpu.VMEM((2, tall, width), BF16),
             pltpu.VMEM((2, size_y, width), BF16),
             pltpu.VMEM((3, 2, rows, width), F32),
             pltpu.VMEM((2, rows, width), F32),
-            pltpu.VMEM((3 * width, 3 * width), F32),
             pltpu.SemaphoreType.DMA((2,)),
         ],
         input_output_aliases={10: 0},
@@ -550,10 +697,7 @@
         activation,
     )
 
-    back_near = swap(near, "gx", 0)
-    back_far = swap(far, "gx", 1)
-
-    def back(pairs, edges, previous, after):
+    def back(pairs, edges, previous, after, back_near=None):
         operands = [grad, grad_rim, first, final]
         operands += [back_near, back_far] if edges else []
         operands += [backward_weights]
@@ -565,7 +709,7 @@
             specs.append(ANY)
         operands.append(after)
         specs.append(ANY)
-        planes = 2 if edges else 2 * len(pairs)
+        planes = 2 * len(pairs) + 2 * edges
         return pl.pallas_call(
             lambda *refs: back_kernel(pairs, edges, *refs),
             out_shape=shape(size_x, size_y, width),
@@ -583,28 +727,67 @@
             name="input_grad",
         )(*operands)
 
-    total = keep + swap(send, "gy", 0)
-    me = lax.axis_index("dp")
-    step = 1
-    while step < parts:
-        paired = total.reshape(total.shape[0] // 2, 2, SLOTS // 2, share, width)
-        bit = (me // step) % 2
-        mine = lax.dynamic_index_in_dim(paired, bit, 1, keepdims=False)
-        theirs = lax.dynamic_index_in_dim(paired, 1 - bit, 1, keepdims=False)
-        total = mine + exchange(theirs, "dp", step)
-        step *= 2
-    total = total[0]
-    rounds = [("gy", 1 << i) for i in range(1, lax.axis_size("gy").bit_length() - 1)]
-    rounds += [("gx", 1 << i) for i in range(lax.axis_size("gx").bit_length() - 1)]
-    for axis, step in rounds:
-        total = total + exchange(total, axis, step)
-    other = swap(total, "gy", 0)
-
     starts = list(range(1, size_x - 1, 2))
     cut = (len(starts) + 1) // 2
-    input_grad = back(starts[:cut], False, None, send)
-    input_grad = back(starts[cut:], False, input_grad, send)
-    input_grad = back([], True, input_grad, send)
+    def add(mine, received):
+        return pl.pallas_call(
+            add_kernel,
+            out_shape=shape(*mine.shape, dtype=F32),
+            in_specs=[VMEM, VMEM],
+            out_specs=VMEM,
+            compiler_params=grant(2),
+            cost_estimate=cost(0.1),
+            name="add_sums",
+        )(mine, received)
+
+    def split(mine, received, step):
+        dims = (mine.shape[0] // 2,) + mine.shape[1:]
+        return pl.pallas_call(
+            lambda *refs: split_kernel(step, *refs),
+            out_shape=(shape(*dims, dtype=F32), shape(*dims)),
+            in_specs=[VMEM, VMEM],
+            out_specs=(VMEM, VMEM),
+            compiler_params=grant(2),
+            cost_estimate=cost(0.1),
+            name="split_sums",
+        )(mine, received)
+
+    rounds = [("dp", 1 << i) for i in range(parts.bit_length() - 1)]
+    rounds += [("gy", 1 << i) for i in range(1, lax.axis_size("gy").bit_length() - 1)]
+    rounds += [("gx", 1 << i) for i in range(lax.axis_size("gx").bit_length() - 1)]
+    received = swap(send, "gy", 0)
+    total = pl.pallas_call(
+        keep_kernel,
+        out_shape=shape(parts, SLOTS // 2, share, width, dtype=F32),
+        in_specs=[VMEM, VMEM],
+        out_specs=VMEM,
+        compiler_params=grant(4),
+        cost_estimate=cost(0.7),
+        name="kept_half",
+    )(acc, sums)
+    input_grad = None
+    for index, (axis, step) in enumerate(rounds):
+        if axis == "dp":
+            total, send = split(total, received, step)
+        else:
+            total = send = add(total, received)
+        if index == 0:
+            later, send = lax.optimization_barrier((kernel, send))
+            backward_weights, scales = back_weights(later)
+        received = exchange(send, axis, step)
+        if index == 0:
+            received, backward_weights = lax.optimization_barrier((received, backward_weights))
+            near, far, backward_weights = lax.optimization_barrier((near, far, backward_weights))
+            back_near = swap(near, "gx", 0)
+            back_far = swap(far, "gx", 1) if many else back_near
+        if index == len(rounds) - 2:
+            input_grad = back(starts[:cut], False, None, send)
+            received, input_grad = lax.optimization_barrier((received, input_grad))
+        if index == len(rounds) - 1:
+            input_grad = back(starts[cut:], True, input_grad, send, back_near)
+            received, input_grad = lax.optimization_barrier((received, input_grad))
+    total = add(total, received).reshape(SLOTS // 2, share, width)
+    other = swap(total, "gy", 0)
 
     kernel_grad, bias_grad = pl.pallas_call(
         finish_kernel,

time: 39.2 us -> 33.6 us (0.86)
  waiting for transfers between devices: 9.2 us -> 6.55 us
  local copies, waits for them, and re-layouts: 2.83 us -> 0.87 us
  starting transfers between devices: 13.4 us -> 11.9 us
  Pallas kernels: 12.6 us -> 13.2 us
    ppermute x4, waiting for transfers between devices: 7.66 us -> 4.27 us  [exchange(): lax.ppermute(value, axes, [(i, i ^ flip) for i in range(math.prod(sizes))])]
    pallas_call x2 -> x10, Pallas kernels: 1.05 us -> 3.56 us  [the longest x1 2.12 us: local(): pl.pallas_call(front_kernel, out_shape=(shape(inner, size_y, width, dtype...]
    unnamed x14 -> x10, local copies, waits for them, and re-layouts: 1.83 us -> 0.03 us
    ppermute x6, starting transfers between devices: 7.35 us -> 6.25 us  [swap(): return lax.ppermute(value, axis, links)]
    pallas_call x1, Pallas kernels: 4.11 us -> 3.02 us  [local(): pl.pallas_call(inner_kernel, out_shape=(shape(size_x, size_y, width), sha...]
    dynamic_slice x3 -> x0, local copies, waits for them, and re-layouts: 0.88 us -> none  [the longest x1 0.86 us: rim(): lax.dynamic_slice_in_dim(cotangent, start, THIN, axis=1)]
    slice x0 -> x1, local copies, waits for them, and re-layouts: none -> 0.84 us  [local(): source[:, :THIN]]
    pallas_call x3 -> x2, Pallas kernels: 4.72 us -> 3.94 us  [back(): pl.pallas_call(lambda *refs: back_kernel(pairs, edges, *refs), out_shape=...]
  transfers between devices with their start and end apart: 10 -> 10, of which waited for: 6 -> 6; matrix products, arithmetic and copies ran while one was open for 0% -> 0% of each run, Pallas kernels for 25% -> 31%
where the time goes in v4:
time: 33.6 us; the launch traced here: 33.4 us
  Pallas kernels  13.2 us (39%)
  starting transfers between devices  11.9 us (35%)
  waiting for transfers between devices  6.55 us (19%)
  local copies, waits for them, and re-layouts  0.87 us (3%)
  between operations  0.8 us (2%)
    ppermute x6, starting transfers between devices, swap(): return lax.ppermute(value, axis, links)  6.25 us
    ppermute x4, starting transfers between devices, exchange(): lax.ppermute(value, axes, [(i, i ^ flip) for i in range(math.prod(sizes))])  5.68 us
    ppermute x4, waiting for transfers between devices, exchange(): lax.ppermute(value, axes, [(i, i ^ flip) for i in range(math.prod(sizes))])  4.27 us
    pallas_call x2, Pallas kernels, back(): pl.pallas_call(lambda *refs: back_kernel(pairs, edges, *refs), out_shape=...  3.94 us
    pallas_call x1, Pallas kernels, local(): pl.pallas_call(inner_kernel, out_shape=(shape(size_x, size_y, width), sha...  3.02 us
    ppermute x6, waiting for transfers between devices, swap(): return lax.ppermute(value, axis, links)  2.28 us
    pallas_call x1, Pallas kernels, local(): pl.pallas_call(front_kernel, out_shape=(shape(inner, size_y, width, dtype...  2.12 us
    pallas_call x1, Pallas kernels, local(): pl.pallas_call(edge_kernel, out_shape=(shape(size_x, size_y, width), shap...  1.93 us
  transfers between devices with their start and end apart: 10, of which 6 were waited for; matrix products, arithmetic and copies ran while one was open for 0% of the time, Pallas kernels for 31%

profile of v4, /device:TPU:0, one launch (start us, length us, event | category | flops | bytes accessed | tf_op | source)
XLA Modules:
  0.0 33.4 jit_solution(8041781591822987940)
XLA Ops:
  0.6 0.8 %fusion = (bf16[16,2,128]{2,1,0:T(2,128)(2,1)S(1)}, bf16[16,2,128]{2,1,0:T(2,128)(2,1)S(1)}, bf16[16,2,128]{2,1,0:T(2,128)(2,1)S(1)}, bf16[16,2,128]{2,1,0:T(2,128)(2,1)S(1)}) fusion(bf16[16,256,128]{2,1,0:T(8,128)(2,1)} %bitcast.9, bf16[16,256,128]{2,1,0:T(8,128)(2,1)} %bitcast.16), kind=kLoop, calls=%fused_computation.1 | loop fusion | bytes 65536 | tf_op jit(solution)/shard_map/slice | solution.py:583
  1.5 0.0 copy-start
  1.5 0.0 copy-start.2
  1.6 0.0 copy-start.4
  1.6 0.5 %collective-permute-start = (bf16[16,4,128]{2,1,0:T(4,128)(2,1)S(1)}, bf16[16,4,128]{2,1,0:T(4,128)(2,1)S(1)}, u32[]{:S(2)}, u32[]{:S(2)}) collective-permute-start(bf16[16,4,128]{2,1,0:T(4,128)(2,1)S(1)} %get-tuple-element.40), channel_id=1, source_target_pairs={{0,4},{4,0},{8,12},{12,8},{1,5},{5,1},{9,13},{13,9},{2,6},{6,2},{1... | collective-permute-start | bytes 49160 | tf_op jit(solution)/shard_map/ppermute | solution.py:27
  2.1 0.0 copy-start.1
  2.1 2.6 %collective-permute-start.1 = (bf16[16,4,128]{2,1,0:T(4,128)(2,1)S(1)}, bf16[16,4,128]{2,1,0:T(4,128)(2,1)S(1)}, u32[]{:S(2)}, u32[]{:S(2)}) collective-permute-start(bf16[16,4,128]{2,1,0:T(4,128)(2,1)S(1)} %get-tuple-element.41), channel_id=1, source_target_pairs={{4,8},{8,4},{12,0},{0,12},{5,9},{9,5},{13,1},{1,13},{6,10},{10,6},... | collective-permute-start | bytes 49160 | tf_op jit(solution)/shard_map/ppermute | solution.py:27
  4.8 0.0 copy-done
  4.8 0.0 copy-done.2
  4.8 0.0 copy-done.4
  4.8 2.1 %front_planes.1 = (f32[14,256,128]{2,1,0:T(8,128)S(1)}, bf16[16,128,256]{2,1,0:T(8,128)(2,1)S(1)}, bf16[384,384]{1,0:T(8,128)(2,1)S(1)}, f32[1,128]{1,0:T(1,128)S(1)}) custom-call(bf16[16,256,128]{2,1,0:T(8,128)(2,1)S(1)} %bitcast.10, bf16[3,3,3,64,64]{4,3,2,1,0:T(8,128)(2,1)S(1)} %copy-done.2, f32[64]{0:T(128)S(1)} %copy-done.4), custom_call_target="tpu_custom_call" | custom-call | flops 2200000000 | tf_op jit(solution)/shard_map/front_planes/pallas_call | solution.py:613
  6.9 0.0 collective-permute-done.y_near
  6.9 0.0 collective-permute-done.1.y_far
  7.0 1.6 %collective-permute-start.2 = (bf16[272,128]{1,0:T(8,128)(2,1)S(1)}, bf16[272,128]{1,0:T(8,128)(2,1)S(1)}, u32[]{:S(2)}, u32[]{:S(2)}) collective-permute-start(bf16[272,128]{1,0:T(8,128)(2,1)S(1)} %pack_planes.1), channel_id=1, source_target_pairs={{0,16},{16,0},{1,17},{17,1},{2,18},{18,2},{3,19},{19,3},{4,20},{20... | collective-permute-start | bytes 208904 | tf_op jit(solution)/shard_map/ppermute | solution.py:27
  8.5 0.0 copy-done.1
  8.5 3.0 %inner_planes.1 = (bf16[16,256,128]{2,1,0:T(8,128)(2,1)}, bf16[14,256,128]{2,1,0:T(8,128)(2,1)S(1)}, bf16[14,16,128]{2,1,0:T(8,128)(2,1)S(1)}, f32[384,384]{1,0:T(8,128)S(1)}, f32[8,128]{1,0:T(8,128)S(1)}) custom-call(bf16[16,256,128]{2,1,0:T(8,128)(2,1)S(1)} %bitcast.12, bf16[16,256,128]{2,1,0:T(8,128)(2,1)S(1)} %bitcast.17, ...), custom_call_target="tpu_custom_call" | custom-call | flops 3300000000 | tf_op jit(solution)/shard_map/inner_planes/pallas_call | solution.py:649
  11.6 0.0 collective-permute-done.2.x_near.x_far
  11.6 1.9 %edge_planes.1 = (bf16[16,256,128]{2,1,0:T(8,128)(2,1)}, bf16[272,128]{1,0:T(8,128)(2,1)S(1)}, bf16[272,128]{1,0:T(8,128)(2,1)S(1)}, bf16[272,128]{1,0:T(8,128)(...) custom-call(bf16[16,256,128]{2,1,0:T(8,128)(2,1)S(1)} %bitcast.13, ...), custom_call_target="tpu_custom_call", output_to_operand_aliasing={{0}: (10, {})} | custom-call | flops 2200000000 | tf_op jit(solution)/shard_map/edge_planes/pallas_call | solution.py:670
  13.5 0.0 copy-start.3
  13.5 0.1 collective-permute-start.3
  13.6 0.3 kept_half.1.refs_0_
  13.9 1.2 %collective-permute-done.3.refs_1_ = f32[4,7,16,128]{3,2,1,0:T(8,128)S(1)} collective-permute-done((f32[4,7,16,128]{3,2,1,0:T(8,128)S(1)}, f32[4,7,16,128]{3,2,1,0:T(8,128)S(1)}, u32[]{:S(2)}, u32[]{:S(2)}) %collective-permute-start.3) | collective-permute-done | bytes 229408 | tf_op jit(solution)/shard_map/ppermute | solution.py:27
  15.1 1.4 %collective-permute-start.4 = (bf16[2,7,16,128]{3,2,1,0:T(8,128)(2,1)S(1)}, bf16[2,7,16,128]{3,2,1,0:T(8,128)(2,1)S(1)}, u32[]{:S(2)}, u32[]{:S(2)}) collective-permute-start(bf16[2,7,16,128]{3,2,1,0:T(8,128)(2,1)S(1)} %get-tuple-element.55), channel_id=1, source_target_pairs={{0,5},{1,4},{2,7},{3,6},{4,1},{5,0},{6,3},{7,2},{8,13},{9,12},{10,... | collective-permute-start | bytes 172040 | tf_op jit(solution)/shard_map/ppermute | solution.py:35
  16.5 0.0 copy-done.3
  16.5 1.0 %back_weights.1 = (bf16[512,768]{1,0:T(8,128)(2,1)S(1)}, f32[14,8,128]{2,1,0:T(8,128)S(1)}) custom-call(bf16[3,3,3,64,64]{4,3,2,1,0:T(8,128)(2,1)S(1)} %copy-done.2, s32[3,3,3]{2,1,0:T(4,128)S(1)} %copy-done.3), custom_call_target="tpu_custom_call" | custom-call | flops 1100000000 | tf_op jit(solution)/shard_map/back_weights/pallas_call | solution.py:602
  17.5 1.6 %collective-permute-done.4.refs_1_ = bf16[2,7,16,128]{3,2,1,0:T(8,128)(2,1)S(1)} collective-permute-done((bf16[2,7,16,128]{3,2,1,0:T(8,128)(2,1)S(1)}, bf16[2,7,16,128]{3,2,1,0:T(8,128)(2,1)S(1)}, u32[]{:S(2)}, u32[]{:S(2)}) %collective-permute-start.4) | collective-permute-done | bytes 57376 | tf_op jit(solution)/shard_map/ppermute | solution.py:35
  19.1 2.4 %collective-permute-start.5 = (bf16[1,7,16,128]{3,2,1,0:T(8,128)(2,1)S(1)}, bf16[1,7,16,128]{3,2,1,0:T(8,128)(2,1)S(1)}, u32[]{:S(2)}, u32[]{:S(2)}) collective-permute-start(bf16[1,7,16,128]{3,2,1,0:T(8,128)(2,1)S(1)} %get-tuple-element.60), channel_id=1, source_target_pairs={{0,6},{1,7},{2,4},{3,5},{4,2},{5,3},{6,0},{7,1},{8,14},{9,15},{10,... | collective-permute-start | bytes 86024 | tf_op jit(solution)/shard_map/ppermute | solution.py:35
  21.5 1.3 %collective-permute-start.8 = (bf16[272,128]{1,0:T(8,128)(2,1)S(1)}, bf16[272,128]{1,0:T(8,128)(2,1)S(1)}, u32[]{:S(2)}, u32[]{:S(2)}) collective-permute-start(bf16[272,128]{1,0:T(8,128)(2,1)S(1)} %get-tuple-element.69), channel_id=1, source_target_pairs={{0,16},{16,0},{1,17},{17,1},{2,18},{18,2},{3,19},{19,3},{4,20},{20... | collective-permute-start | bytes 208904 | tf_op jit(solution)/shard_map/ppermute | solution.py:27
  22.8 0.6 %collective-permute-done.5.received = bf16[1,7,16,128]{3,2,1,0:T(8,128)(2,1)S(1)} collective-permute-done((bf16[1,7,16,128]{3,2,1,0:T(8,128)(2,1)S(1)}, bf16[1,7,16,128]{3,2,1,0:T(8,128)(2,1)S(1)}, u32[]{:S(2)}, u32[]{:S(2)}) %collective-permute-start.5) | collective-permute-done | bytes 28704 | tf_op jit(solution)/shard_map/ppermute | solution.py:35
  23.4 0.9 %collective-permute-start.6 = (f32[1,7,16,128]{3,2,1,0:T(8,128)S(1)}, f32[1,7,16,128]{3,2,1,0:T(8,128)S(1)}, u32[]{:S(2)}, u32[]{:S(2)}) collective-permute-start(f32[1,7,16,128]{3,2,1,0:T(8,128)S(1)} %add_sums.3.refs_5_.mine), channel_id=1, source_target_pairs={{0,12},{1,13},{2,14},{3,15},{4,8},{5,9},{6,10},{7,11},{8,4},{9,5},... | collective-permute-start | bytes 172040 | tf_op jit(solution)/shard_map/ppermute | solution.py:35
  24.3 1.9 %input_grad.2.refs_7_ = bf16[16,256,128]{2,1,0:T(8,128)(2,1)} custom-call(bf16[14,256,128]{2,1,0:T(8,128)(2,1)S(1)} %get-tuple-element.61.refs_0_, bf16[14,16,128]{2,1,0:T(8,128)(2,1)S(1)} %get-tuple-element.62.refs_1_, bf16[272,128]{1,0:T(8,128)(2,1)S(1)} %get-tuple-element.63.refs_2_, bf16[272,128]{1,0:T(8,128)(2,1)S(1)} %get-tuple-element.64.refs_3_, ...), custom_call_target="tpu_custom_call" | custom-call | flops 2750000128 | tf_op jit(solution)/shard_map/input_grad/pallas_call | solution.py:713
  26.2 1.2 %collective-permute-done.6.received = f32[1,7,16,128]{3,2,1,0:T(8,128)S(1)} collective-permute-done((f32[1,7,16,128]{3,2,1,0:T(8,128)S(1)}, f32[1,7,16,128]{3,2,1,0:T(8,128)S(1)}, u32[]{:S(2)}, u32[]{:S(2)}) %collective-permute-start.6) | collective-permute-done | bytes 57376 | tf_op jit(solution)/shard_map/ppermute | solution.py:35
  27.4 1.0 %collective-permute-start.7 = (f32[1,7,16,128]{3,2,1,0:T(8,128)S(1)}, f32[1,7,16,128]{3,2,1,0:T(8,128)S(1)}, u32[]{:S(2)}, u32[]{:S(2)}) collective-permute-start(f32[1,7,16,128]{3,2,1,0:T(8,128)S(1)} %add_sums.4.refs_8_.mine), channel_id=1, source_target_pairs={{0,20},{1,21},{2,22},{3,23},{4,16},{5,17},{6,18},{7,19},{8,28},{9,... | collective-permute-start | bytes 172040 | tf_op jit(solution)/shard_map/ppermute | solution.py:35
  28.4 0.0 collective-permute-done.8.refs_4_.refs_5_
  28.4 2.0 %input_grad.3 = bf16[16,256,128]{2,1,0:T(8,128)(2,1)} custom-call(bf16[14,256,128]{2,1,0:T(8,128)(2,1)S(1)} %get-tuple-element.61.refs_0_, bf16[14,16,128]{2,1,0:T(8,128)(2,1)S(1)} %get-tuple-element.62.refs_1_, bf16[272,128]{1,0:T(8,128)(2,1)S(1)} %get-tuple-element.63.refs_2_, ...), custom_call_target="tpu_custom_call", output_to_operand_aliasing={{}: (7, {})} | custom-call | flops 2750000128 | tf_op jit(solution)/shard_map/input_grad/pallas_call | solution.py:713
  30.4 0.9 %collective-permute-done.7.received = f32[1,7,16,128]{3,2,1,0:T(8,128)S(1)} collective-permute-done((f32[1,7,16,128]{3,2,1,0:T(8,128)S(1)}, f32[1,7,16,128]{3,2,1,0:T(8,128)S(1)}, u32[]{:S(2)}, u32[]{:S(2)}) %collective-permute-start.7) | collective-permute-done | bytes 57376 | tf_op jit(solution)/shard_map/ppermute | solution.py:35
  31.4 0.2 collective-permute-start.9
  31.6 1.1 %collective-permute-done.9.other = f32[7,16,128]{2,1,0:T(8,128)S(1)} collective-permute-done((f32[7,16,128]{2,1,0:T(8,128)S(1)}, f32[7,16,128]{2,1,0:T(8,128)S(1)}, u32[]{:S(2)}, u32[]{:S(2)}) %collective-permute-start.9) | collective-permute-done | bytes 57376 | tf_op jit(solution)/shard_map/ppermute | solution.py:27
  32.7 0.7 %scale_weight_grad.1 = (bf16[27,16,64]{2,1,0:T(8,128)(2,1)}, f32[1,16]{1,0:T(1,128)}) custom-call(f32[7,16,128]{2,1,0:T(8,128)S(1)} %bitcast.15, f32[7,16,128]{2,1,0:T(8,128)S(1)} %collective-permute-done.9.other, f32[14,8,128]{2,1,0:T(8,128)S(1)} %get-tuple-element.73.scale_ref), custom_call_target="tpu_custom_call" | custom-call | tf_op jit(solution)/shard_map/scale_weight_grad/pallas_call | solution.py:792
  (8 shorter events, 0.2 us)
Async XLA Ops:
  1.5 3.2 %copy-start = (bf16[1,16,256,128]{3,2,1,0:T(8,128)(2,1)S(1)}, bf16[1,16,256,128]{3,2,1,0:T(8,128)(2,1)}, u32[]{:S(2)}) copy-start(bf16[1,16,256,128]{3,2,1,0:T(8,128)(2,1)} %param.5) | copy-start | bytes 3145732
  1.5 3.2 %copy-start.2 = (bf16[3,3,3,64,64]{4,3,2,1,0:T(8,128)(2,1)S(1)}, bf16[3,3,3,64,64]{4,3,2,1,0:T(8,128)(2,1)}, u32[]{:S(2)}) copy-start(bf16[3,3,3,64,64]{4,3,2,1,0:T(8,128)(2,1)} %refs_0_) | copy-start | bytes 663556
  1.6 3.2 %copy-start.4 = (f32[64]{0:T(128)S(1)}, f32[64]{0:T(128)}, u32[]{:S(2)}) copy-start(f32[64]{0:T(128)} %offsets.1) | copy-start | bytes 772
  1.6 5.3 %collective-permute-start = (bf16[16,4,128]{2,1,0:T(4,128)(2,1)S(1)}, bf16[16,4,128]{2,1,0:T(4,128)(2,1)S(1)}, u32[]{:S(2)}, u32[]{:S(2)}) collective-permute-start(bf16[16,4,128]{2,1,0:T(4,128)(2,1)S(1)} %get-tuple-element.40), channel_id=1, source_target_pairs={{0,4},{4,0},{8,12},{12,8},{1,5},{5,1},{9,13},{13,9},{2,6},{6,2},{1... | collective-permute-start | bytes 49160 | tf_op jit(solution)/shard_map/ppermute | solution.py:27
  2.1 6.4 %copy-start.1 = (bf16[1,16,256,128]{3,2,1,0:T(8,128)(2,1)S(1)}, bf16[1,16,256,128]{3,2,1,0:T(8,128)(2,1)}, u32[]{:S(2)}) copy-start(bf16[1,16,256,128]{3,2,1,0:T(8,128)(2,1)} %param.8) | copy-start | bytes 3145732
  2.1 4.8 %collective-permute-start.1 = (bf16[16,4,128]{2,1,0:T(4,128)(2,1)S(1)}, bf16[16,4,128]{2,1,0:T(4,128)(2,1)S(1)}, u32[]{:S(2)}, u32[]{:S(2)}) collective-permute-start(bf16[16,4,128]{2,1,0:T(4,128)(2,1)S(1)} %get-tuple-element.41), channel_id=1, source_target_pairs={{4,8},{8,4},{12,0},{0,12},{5,9},{9,5},{13,1},{1,13},{6,10},{10,6},... | collective-permute-start | bytes 49160 | tf_op jit(solution)/shard_map/ppermute | solution.py:27
  7.0 4.6 %collective-permute-start.2 = (bf16[272,128]{1,0:T(8,128)(2,1)S(1)}, bf16[272,128]{1,0:T(8,128)(2,1)S(1)}, u32[]{:S(2)}, u32[]{:S(2)}) collective-permute-start(bf16[272,128]{1,0:T(8,128)(2,1)S(1)} %pack_planes.1), channel_id=1, source_target_pairs={{0,16},{16,0},{1,17},{17,1},{2,18},{18,2},{3,19},{19,3},{4,20},{20... | collective-permute-start | bytes 208904 | tf_op jit(solution)/shard_map/ppermute | solution.py:27
  13.5 3.0 %copy-start.3 = (s32[3,3,3]{2,1,0:T(4,128)S(1)}, s32[3,3,3]{2,1,0:T(4,128)}, u32[]{:S(2)}) copy-start(s32[3,3,3]{2,1,0:T(4,128)} %refs_1_.1) | copy-start | bytes 328
  13.5 1.6 %collective-permute-start.3 = (f32[4,7,16,128]{3,2,1,0:T(8,128)S(1)}, f32[4,7,16,128]{3,2,1,0:T(8,128)S(1)}, u32[]{:S(2)}, u32[]{:S(2)}) collective-permute-start(f32[4,7,16,128]{3,2,1,0:T(8,128)S(1)} %get-tuple-element.52), channel_id=1, source_target_pairs={{0,4},{4,0},{8,12},{12,8},{1,5},{5,1},{9,13},{13,9},{2,6},{6,2},{1... | collective-permute-start | bytes 688136 | tf_op jit(solution)/shard_map/ppermute | solution.py:27
  15.1 4.0 %collective-permute-start.4 = (bf16[2,7,16,128]{3,2,1,0:T(8,128)(2,1)S(1)}, bf16[2,7,16,128]{3,2,1,0:T(8,128)(2,1)S(1)}, u32[]{:S(2)}, u32[]{:S(2)}) collective-permute-start(bf16[2,7,16,128]{3,2,1,0:T(8,128)(2,1)S(1)} %get-tuple-element.55), channel_id=1, source_target_pairs={{0,5},{1,4},{2,7},{3,6},{4,1},{5,0},{6,3},{7,2},{8,13},{9,12},{10,... | collective-permute-start | bytes 172040 | tf_op jit(solution)/shard_map/ppermute | solution.py:35
  19.1 4.3 %collective-permute-start.5 = (bf16[1,7,16,128]{3,2,1,0:T(8,128)(2,1)S(1)}, bf16[1,7,16,128]{3,2,1,0:T(8,128)(2,1)S(1)}, u32[]{:S(2)}, u32[]{:S(2)}) collective-permute-start(bf16[1,7,16,128]{3,2,1,0:T(8,128)(2,1)S(1)} %get-tuple-element.60), channel_id=1, source_target_pairs={{0,6},{1,7},{2,4},{3,5},{4,2},{5,3},{6,0},{7,1},{8,14},{9,15},{10,... | collective-permute-start | bytes 86024 | tf_op jit(solution)/shard_map/ppermute | solution.py:35
  21.5 6.9 %collective-permute-start.8 = (bf16[272,128]{1,0:T(8,128)(2,1)S(1)}, bf16[272,128]{1,0:T(8,128)(2,1)S(1)}, u32[]{:S(2)}, u32[]{:S(2)}) collective-permute-start(bf16[272,128]{1,0:T(8,128)(2,1)S(1)} %get-tuple-element.69), channel_id=1, source_target_pairs={{0,16},{16,0},{1,17},{17,1},{2,18},{18,2},{3,19},{19,3},{4,20},{20... | collective-permute-start | bytes 208904 | tf_op jit(solution)/shard_map/ppermute | solution.py:27
  23.4 4.0 %collective-permute-start.6 = (f32[1,7,16,128]{3,2,1,0:T(8,128)S(1)}, f32[1,7,16,128]{3,2,1,0:T(8,128)S(1)}, u32[]{:S(2)}, u32[]{:S(2)}) collective-permute-start(f32[1,7,16,128]{3,2,1,0:T(8,128)S(1)} %add_sums.3.refs_5_.mine), channel_id=1, source_target_pairs={{0,12},{1,13},{2,14},{3,15},{4,8},{5,9},{6,10},{7,11},{8,4},{9,5},... | collective-permute-start | bytes 172040 | tf_op jit(solution)/shard_map/ppermute | solution.py:35
  27.4 4.0 %collective-permute-start.7 = (f32[1,7,16,128]{3,2,1,0:T(8,128)S(1)}, f32[1,7,16,128]{3,2,1,0:T(8,128)S(1)}, u32[]{:S(2)}, u32[]{:S(2)}) collective-permute-start(f32[1,7,16,128]{3,2,1,0:T(8,128)S(1)} %add_sums.4.refs_8_.mine), channel_id=1, source_target_pairs={{0,20},{1,21},{2,22},{3,23},{4,16},{5,17},{6,18},{7,19},{8,28},{9,... | collective-permute-start | bytes 172040 | tf_op jit(solution)/shard_map/ppermute | solution.py:35
  31.4 1.3 %collective-permute-start.9 = (f32[7,16,128]{2,1,0:T(8,128)S(1)}, f32[7,16,128]{2,1,0:T(8,128)S(1)}, u32[]{:S(2)}, u32[]{:S(2)}) collective-permute-start(f32[7,16,128]{2,1,0:T(8,128)S(1)} %bitcast.14), channel_id=1, source_target_pairs={{0,4},{4,0},{8,12},{12,8},{1,5},{5,1},{9,13},{13,9},{2,6},{6,2},{1... | collective-permute-start | bytes 172040 | tf_op jit(solution)/shard_map/ppermute | solution.py:27

commit v5 on v4

--- a/solution.py
+++ b/solution.py
@@ -284,8 +284,8 @@
 
 def inner_kernel(
     f_ref, u_ref, y_near, y_far, pre_ref, turned, w_ref, bias_ref,
-    act_hbm, grad_ref, rim_ref, acc_ref, sums_ref,
-    f_rim, u_rim, act, wide, sems,
+    act, grad_ref, rim_ref, acc_ref, sums_ref,
+    f_rim, u_rim, wide,
 ):
     size_x, size_y, width = f_ref.shape
     inner = size_x - 2
@@ -304,7 +304,6 @@
     )
     row = lax.broadcasted_iota(jnp.int32, (RIM, width), 0)
     sums = jnp.zeros((8, width), F32)
-    stores = []
     for p in range(0, inner, 2):
         for q in (p, p + 1):
             strip = [
@@ -338,12 +337,6 @@
                 act[q, y : y + CHUNK, :] = value.astype(BF16)
                 grad_ref[q, y : y + CHUNK, :] = rounded
                 sums = sums + jnp.sum(exact.reshape(CHUNK // 8, 8, width), axis=0)
-        stores.append(
-            pltpu.make_async_copy(
-                act.at[pl.ds(p, 2)], act_hbm.at[pl.ds(p + 1, 2)], sems.at[p // 2]
-            )
-        )
-        stores[-1].start()
         term = outer(
             [[turned[q + j] for j in range(3)] for q in (p, p + 1)],
             [shifted_grads(wide, q) for q in (p, p + 1)],
@@ -353,12 +346,11 @@
         else:
             acc_ref[...] += term
     sums_ref[...] = sums
-    for copy in stores:
-        copy.wait()
-
-
-def emit_half(acc, sums, out, which):
-    parts, count, share, width = out.shape
+
+
+def emit_half(acc, sums, which, away, stay):
+    outs = [out for out in (away, stay) if out is not None]
+    blocks, count, share, width = outs[0].shape
     half = width // 2
 
     def block(t):
@@ -373,42 +365,53 @@
         rolled = pltpu.roll(whole[half:], half, 1)
         return whole[:half] + jnp.where(lower(half), rolled, 0.0)
 
-    def put(s, value):
-        for d in range(parts):
-            out[d, s] = value[d * share : (d + 1) * share]
-
-    @pl.when(which == 0)
-    def _():
-        for s in range(count):
-            put(s, middle(s))
-
-    @pl.when(which == 1)
-    def _():
-        for t in range(count, 9):
-            put(t - count, middle(t))
-        for t in range(0, 9, 2):
-            low = block(t)[half:]
-            if t + 1 < 9:
-                high = pltpu.roll(block(t + 1)[half:], half, 1)
-                put(9 + t // 2 - count, jnp.where(lower(half), low, high))
-                continue
-            both = jnp.sum(sums, axis=0, keepdims=True)
-            both = jnp.broadcast_to(both + pltpu.roll(both, half, 1), (share, width))
-            for d in range(parts):
-                turned = pltpu.roll(both, (half - d * share) % width, 1)
-                mine = low[d * share : (d + 1) * share]
-                out[d, count - 1] = jnp.where(lower(share), mine, turned)
-
-
-def keep_kernel(acc, sums, keep_ref):
-    emit_half(acc, sums[...], keep_ref, half_kept())
+    def low_pair(t):
+        low = block(t)[half:]
+        if t + 1 < 9:
+            return jnp.where(lower(half), low, pltpu.roll(block(t + 1)[half:], half, 1))
+        both = jnp.sum(sums, axis=0, keepdims=True)
+        both = jnp.broadcast_to(both + pltpu.roll(both, half, 1), (share, width))
+        turned = [
+            pltpu.roll(both, (half - d * share) % width, 1) for d in range(2 * blocks)
+        ]
+        return jnp.where(lower(half), low, jnp.concatenate(turned, axis=0))
+
+    def write(bit):
+        def put(s, value):
+            for k in range(blocks):
+                for out, d in ((away, 2 * k + 1 - bit), (stay, 2 * k + bit)):
+                    if out is not None:
+                        out[k, s] = value[d * share : (d + 1) * share]
+
+        @pl.when(which == 0)
+        def _():
+            for s in range(count):
+                put(s, middle(s))
+
+        @pl.when(which == 1)
+        def _():
+            for t in range(count, 9):
+                put(t - count, middle(t))
+            for t in range(0, 9, 2):
+                put(9 + t // 2 - count, low_pair(t))
+
+    place = lax.axis_index("dp") % 2
+    pl.when(place == 0)(lambda: write(0))
+    pl.when(place == 1)(lambda: write(1))
+
+
+def rest_kernel(acc, sums, send_stay, keep_away, keep_stay):
+    kept = half_kept()
+    emit_half(acc, sums[...], 1 - kept, None, send_stay)
+    emit_half(acc, sums[...], kept, keep_away, keep_stay)
 
 
 def edge_kernel(
-    f_ref, u_ref, y_near, y_far, x_near, x_far, w_ref, bias_ref, acc_ref, sums_ref, act_in,
-    act_hbm, first_ref, last_ref, near_ref, far_ref, acc, bias_sums, send_ref,
-    f_rim, u_rim, around, act, taps, wide, sems,
+    f_ref, u_ref, y_near, y_far, x_near, x_far, w_ref, bias_ref, acc_ref, sums_ref,
+    act, first_ref, last_ref, acc, bias_sums, send_ref, near_ref, *refs
 ):
+    far_ref = refs[0] if len(refs) > 5 else None
+    f_rim, u_rim, around, taps, wide = refs[-5:]
     size_x, size_y, width = f_ref.shape
     x_side = lax.axis_index("gx") % 2
     place_rims(y_near, y_far, f_rim, u_rim, RIM - THIN)
@@ -436,32 +439,42 @@
             taps, wide, p, bias, sums, u_ref.at[x], u_rim.at[x], act.at[p],
             outs[p].at[pl.ds(0, size_y)], outs[p].at[pl.ds(size_y, 2 * RIM)],
         )
-    stores = [
-        pltpu.make_async_copy(act.at[p], act_hbm.at[places[p]], sems.at[p]) for p in range(2)
-    ]
-    for copy in stores:
-        copy.start()
     acc[...] = acc_ref[...] + outer(
         [[plane.T for plane in bodies[p]] for p in range(2)],
         [shifted_grads(wide, p) for p in range(2)],
     )
 
-    def hand(second, first):
-        first[...] = first_ref[...]
-        second[...] = last_ref[...]
-
-    oriented(far_ref, near_ref, x_side, lambda low, high: hand(low, high))
+    def hand(last, first):
+        if last is not None:
+            last[...] = last_ref[...]
+        if first is not None:
+            first[...] = first_ref[...]
+
+    oriented(far_ref, near_ref, x_side, hand)
 
     bias_sums[...] = sums
-    emit_half(acc, sums, send_ref, 1 - half_kept())
-    for copy in stores:
-        copy.wait()
-
-
-def back_kernel(pairs, edges, grad_ref, rim_ref, first_ref, last_ref, *refs):
+    emit_half(acc, sums, 1 - half_kept(), send_ref, None)
+
+
+def store_activation(act_inner, act_edges, act_hbm, sems):
+    size_x = act_hbm.shape[0]
+    copies = [
+        pltpu.make_async_copy(act_edges.at[0], act_hbm.at[0], sems.at[0]),
+        pltpu.make_async_copy(act_edges.at[1], act_hbm.at[size_x - 1], sems.at[1]),
+        pltpu.make_async_copy(act_inner, act_hbm.at[pl.ds(1, size_x - 2)], sems.at[2]),
+    ]
+    for copy in copies:
+        copy.start()
+    return copies
+
+
+def back_kernel(pairs, edges, stored, grad_ref, rim_ref, first_ref, last_ref, *refs):
     x_near, x_far = refs[:2] if edges else (None, None)
     w_ref = refs[2 * edges]
-    out_hbm, out, taps, around, sems = refs[-5:]
+    out_hbm, *act_hbm, out, taps, around, sems = refs[-5 - stored :]
+    copies = []
+    if stored:
+        copies = store_activation(*refs[1:3], act_hbm[0], sems.at[pl.ds(out.shape[0], 3)])
     size_y, width = grad_ref.shape[1:]
     size_x = grad_ref.shape[0] + 2
     tall = size_y + 2 * RIM
@@ -511,12 +524,13 @@
                 pltpu.make_async_copy(out.at[i], out_hbm.at[planes[i]], sems.at[i])
             )
             stores[-1].start()
-    for copy in stores:
+    for copy in stores + copies:
         copy.wait()
 
 
-def split_kernel(step, mine, received, keep_ref, send_ref):
-    total = mine[...] + received[...].astype(F32)
+def split_kernel(step, *refs):
+    *terms, keep_ref, send_ref = refs
+    total = sum_refs(terms)
     bit = (lax.axis_index("dp") // step) % 2
 
     def place(first, second):
@@ -528,8 +542,16 @@
     pl.when(bit == 1)(lambda: place(1, 0))
 
 
-def add_kernel(mine, received, total_ref):
-    total_ref[...] = mine[...] + received[...].astype(F32)
+def sum_refs(terms):
+    total = terms[0][...].astype(F32)
+    for term in terms[1:]:
+        total = total + term[...].astype(F32)
+    return total
+
+
+def add_kernel(*refs):
+    *terms, total_ref = refs
+    total_ref[...] = sum_refs(terms).astype(total_ref.dtype)
 
 
 def finish_kernel(own, other, scale_ref, grad_ref, bias_ref):
@@ -646,61 +668,52 @@
         pltpu.VMEM((size_x, 2 * RIM, width), BF16),
         pltpu.VMEM((size_x, 2 * RIM, width), BF16),
     ]
-    activation, grad, grad_rim, acc, sums = pl.pallas_call(
+    act_inner, grad, grad_rim, acc, sums = pl.pallas_call(
         inner_kernel,
         out_shape=(
-            shape(size_x, size_y, width),
+            shape(inner, size_y, width),
             shape(inner, size_y, width),
             shape(inner, 2 * RIM, width),
             shape(3 * width, 3 * width, dtype=F32),
             shape(8, width, dtype=F32),
         ),
         in_specs=[VMEM] * 8,
-        out_specs=(ANY,) + (VMEM,) * 4,
-        scratch_shapes=rims + [
-            pltpu.VMEM((inner, size_y, width), BF16),
-            pltpu.VMEM((inner, rows, width), F32),
-            pltpu.SemaphoreType.DMA((inner // 2,)),
-        ],
+        out_specs=(VMEM,) * 5,
+        scratch_shapes=rims + [pltpu.VMEM((inner, rows, width), F32)],
         compiler_params=grant(12),
         cost_estimate=cost(3.0),
         name="inner_planes",
     )(cells, cotangent, y_near, y_far, preact, turned, forward_weights, bias)
 
-    activation, first, final, near, far, acc, sums, send = pl.pallas_call(
+    blocks = (parts // 2, SLOTS // 2, share, width)
+    act_edges, first, final, acc, sums, send, *edges = pl.pallas_call(
         edge_kernel,
         out_shape=(
-            shape(size_x, size_y, width),
-            shape(tall, width),
-            shape(tall, width),
+            shape(2, size_y, width),
             shape(tall, width),
             shape(tall, width),
             shape(3 * width, 3 * width, dtype=F32),
             shape(8, width, dtype=F32),
-            shape(parts, SLOTS // 2, share, width, dtype=F32),
-        ),
-        in_specs=[VMEM] * 10 + [ANY],
-        out_specs=(ANY,) + (VMEM,) * 7,
+            shape(*blocks, dtype=F32),
+        )
+        + (shape(tall, width),) * (1 + many),
+        in_specs=[VMEM] * 10,
+        out_specs=(VMEM,) * (7 + many),
         scratch_shapes=rims + [
             pltpu.VMEM((2, tall, width), BF16),
-            pltpu.VMEM((2, size_y, width), BF16),
             pltpu.VMEM((3, 2, rows, width), F32),
             pltpu.VMEM((2, rows, width), F32),
-            pltpu.SemaphoreType.DMA((2,)),
         ],
-        input_output_aliases={10: 0},
         compiler_params=grant(12),
         cost_estimate=cost(2.0),
         name="edge_planes",
     )(
         cells, cotangent, y_near, y_far, x_near, x_far, forward_weights, bias, acc, sums,
-        activation,
-    )
-
-    def back(pairs, edges, previous, after, back_near=None):
-        operands = [grad, grad_rim, first, final]
-        operands += [back_near, back_far] if edges else []
-        operands += [backward_weights]
+    )
+
+    def back(pairs, previous, after, beyond=(), acts=()):
+        edges, stored = len(beyond) > 0, len(acts) > 0
+        operands = [grad, grad_rim, first, final, *beyond, backward_weights, *acts]
         specs = [VMEM] * len(operands)
         aliases = {}
         if previous is not None:
@@ -710,83 +723,93 @@
         operands.append(after)
         specs.append(ANY)
         planes = 2 * len(pairs) + 2 * edges
-        return pl.pallas_call(
-            lambda *refs: back_kernel(pairs, edges, *refs),
-            out_shape=shape(size_x, size_y, width),
+        results = pl.pallas_call(
+            lambda *refs: back_kernel(pairs, edges, stored, *refs),
+            out_shape=(shape(size_x, size_y, width),) * (1 + stored),
             in_specs=specs,
-            out_specs=ANY,
+            out_specs=(ANY,) * (1 + stored),
             scratch_shapes=[
                 pltpu.VMEM((planes, size_y, width), BF16),
                 pltpu.VMEM((3, planes, rows, width), F32),
                 pltpu.VMEM((2, tall, width), BF16),
-                pltpu.SemaphoreType.DMA((planes,)),
+                pltpu.SemaphoreType.DMA((planes + 3 * stored,)),
             ],
             input_output_aliases=aliases,
             compiler_params=grant(12),
-            cost_estimate=cost(2.5),
+            cost_estimate=cost(2.5 if planes > 4 else 1.0),
             name="input_grad",
         )(*operands)
+        return results if stored else results[0]
 
     starts = list(range(1, size_x - 1, 2))
-    cut = (len(starts) + 1) // 2
-    def add(mine, received):
+    cut = len(starts) - 2
+    def add(terms, dtype):
         return pl.pallas_call(
             add_kernel,
-            out_shape=shape(*mine.shape, dtype=F32),
-            in_specs=[VMEM, VMEM],
+            out_shape=shape(*terms[0].shape, dtype=dtype),
+            in_specs=[VMEM] * len(terms),
             out_specs=VMEM,
             compiler_params=grant(2),
             cost_estimate=cost(0.1),
             name="add_sums",
-        )(mine, received)
-
-    def split(mine, received, step):
-        dims = (mine.shape[0] // 2,) + mine.shape[1:]
+        )(*terms)
+
+    def split(terms, step):
+        dims = (terms[0].shape[0] // 2,) + terms[0].shape[1:]
         return pl.pallas_call(
             lambda *refs: split_kernel(step, *refs),
             out_shape=(shape(*dims, dtype=F32), shape(*dims)),
-            in_specs=[VMEM, VMEM],
+            in_specs=[VMEM] * len(terms),
             out_specs=(VMEM, VMEM),
             compiler_params=grant(2),
             cost_estimate=cost(0.1),
             name="split_sums",
-        )(mine, received)
+        )(*terms)
 
     rounds = [("dp", 1 << i) for i in range(parts.bit_length() - 1)]
     rounds += [("gy", 1 << i) for i in range(1, lax.axis_size("gy").bit_length() - 1)]
     rounds += [("gx", 1 << i) for i in range(lax.axis_size("gx").bit_length() - 1)]
-    received = swap(send, "gy", 0)
-    total = pl.pallas_call(
-        keep_kernel,
-        out_shape=shape(parts, SLOTS // 2, share, width, dtype=F32),
+    away = swap(send, "gy", 0)
+    send_stay, keep_away, keep_stay = pl.pallas_call(
+        rest_kernel,
+        out_shape=(shape(*blocks, dtype=F32),) * 3,
         in_specs=[VMEM, VMEM],
-        out_specs=VMEM,
+        out_specs=(VMEM,) * 3,
         compiler_params=grant(4),
         cost_estimate=cost(0.7),
-        name="kept_half",
+        name="rest_of_sums",
     )(acc, sums)
+    terms = [keep_stay, swap(send_stay, "gy", 0)]
     input_grad = None
     for index, (axis, step) in enumerate(rounds):
-        if axis == "dp":
-            total, send = split(total, received, step)
+        if index == 0:
+            send = add([keep_away, away], BF16)
+        elif axis == "dp":
+            total, send = split(terms, step)
+            terms = [total]
         else:
-            total = send = add(total, received)
+            send = add(terms, BF16)
+            terms = [send]
         if index == 0:
             later, send = lax.optimization_barrier((kernel, send))
             backward_weights, scales = back_weights(later)
         received = exchange(send, axis, step)
         if index == 0:
-            received, backward_weights = lax.optimization_barrier((received, backward_weights))
-            near, far, backward_weights = lax.optimization_barrier((near, far, backward_weights))
-            back_near = swap(near, "gx", 0)
-            back_far = swap(far, "gx", 1) if many else back_near
+            input_grad = back(starts[:2], None, send)
+            received, input_grad = lax.optimization_barrier((received, input_grad))
+            *edges, backward_weights = lax.optimization_barrier((*edges, backward_weights))
+            back_near = swap(edges[0], "gx", 0)
+            back_far = swap(edges[1], "gx", 1) if many else back_near
         if index == len(rounds) - 2:
-            input_grad = back(starts[:cut], False, None, send)
+            input_grad, activation = back(
+                starts[2:cut], input_grad, send, acts=(act_inner, act_edges)
+            )
             received, input_grad = lax.optimization_barrier((received, input_grad))
         if index == len(rounds) - 1:
-            input_grad = back(starts[cut:], True, input_grad, send, back_near)
+            input_grad = back(starts[cut:], input_grad, send, beyond=(back_near, back_far))
             received, input_grad = lax.optimization_barrier((received, input_grad))
-    total = add(total, received).reshape(SLOTS // 2, share, width)
+        terms.append(received)
+    total = add(terms, F32).reshape(SLOTS // 2, share, width)
     other = swap(total, "gy", 0)
 
     kernel_grad, bias_grad = pl.pallas_call(

time: 33.6 us -> 31.4 us (0.935)
  waiting for transfers between devices: 6.55 us -> 3.18 us
  starting transfers between devices: 11.9 us -> 12.7 us
  Pallas kernels: 13.2 us -> 13.6 us
    ppermute x4, waiting for transfers between devices: 4.27 us -> 1.83 us  [exchange(): lax.ppermute(value, axes, [(i, i ^ flip) for i in range(math.prod(sizes))])]
    ppermute x6 -> x7, waiting for transfers between devices: 2.28 us -> 1.35 us  [swap(): return lax.ppermute(value, axis, links)]
    ppermute x6 -> x7, starting transfers between devices: 6.25 us -> 6.84 us  [swap(): return lax.ppermute(value, axis, links)]
    pallas_call x8 -> x10, Pallas kernels: 9.22 us -> 9.7 us  [the longest x3 4.74 us: back(): pl.pallas_call(lambda *refs: back_kernel(pairs, edges, stored, *refs), ou...]
  transfers between devices with their start and end apart: 10 -> 11, of which waited for: 6 -> 7; matrix products, arithmetic and copies ran while one was open for 0% -> 0% of each run, Pallas kernels for 31% -> 36%
where the time goes in v5:
time: 31.4 us; the launch traced here: 31.3 us
  Pallas kernels  13.6 us (43%)
  starting transfers between devices  12.7 us (40%)
  waiting for transfers between devices  3.18 us (10%)
  local copies, waits for them, and re-layouts  0.87 us (3%)
  between operations  0.8 us (3%)
    ppermute x7, starting transfers between devices, swap(): return lax.ppermute(value, axis, links)  6.84 us
    ppermute x4, starting transfers between devices, exchange(): lax.ppermute(value, axes, [(i, i ^ flip) for i in range(math.prod(sizes))])  5.87 us
    pallas_call x3, Pallas kernels, back(): pl.pallas_call(lambda *refs: back_kernel(pairs, edges, stored, *refs), ou...  4.74 us
    pallas_call x1, Pallas kernels, local(): pl.pallas_call(inner_kernel, out_shape=(shape(inner, size_y, width), shap...  2.67 us
    pallas_call x1, Pallas kernels, local(): pl.pallas_call(front_kernel, out_shape=(shape(inner, size_y, width, dtype...  2.12 us
    ppermute x4, waiting for transfers between devices, exchange(): lax.ppermute(value, axes, [(i, i ^ flip) for i in range(math.prod(sizes))])  1.83 us
    pallas_call x1, Pallas kernels, local(): pl.pallas_call(edge_kernel, out_shape=(shape(2, size_y, width), shape(tal...  1.41 us
    ppermute x7, waiting for transfers between devices, swap(): return lax.ppermute(value, axis, links)  1.35 us
  transfers between devices with their start and end apart: 11, of which 7 were waited for; matrix products, arithmetic and copies ran while one was open for 0% of the time, Pallas kernels for 36%

profile of v5, /device:TPU:0, one launch (start us, length us, event | category | flops | bytes accessed | tf_op | source)
XLA Modules:
  0.0 31.3 jit_solution(11862357125789011226)
XLA Ops:
  0.6 0.8 %fusion = (bf16[16,2,128]{2,1,0:T(2,128)(2,1)S(1)}, bf16[16,2,128]{2,1,0:T(2,128)(2,1)S(1)}, bf16[16,2,128]{2,1,0:T(2,128)(2,1)S(1)}, bf16[16,2,128]{2,1,0:T(2,128)(2,1)S(1)}) fusion(bf16[16,256,128]{2,1,0:T(8,128)(2,1)} %bitcast.9, bf16[16,256,128]{2,1,0:T(8,128)(2,1)} %bitcast.16), kind=kLoop, calls=%fused_computation.1 | loop fusion | bytes 65536 | tf_op jit(solution)/shard_map/slice | solution.py:605
  1.5 0.0 copy-start
  1.5 0.0 copy-start.2
  1.6 0.0 copy-start.4
  1.6 0.5 %collective-permute-start = (bf16[16,4,128]{2,1,0:T(4,128)(2,1)S(1)}, bf16[16,4,128]{2,1,0:T(4,128)(2,1)S(1)}, u32[]{:S(2)}, u32[]{:S(2)}) collective-permute-start(bf16[16,4,128]{2,1,0:T(4,128)(2,1)S(1)} %get-tuple-element.43), channel_id=1, source_target_pairs={{0,4},{4,0},{8,12},{12,8},{1,5},{5,1},{9,13},{13,9},{2,6},{6,2},{1... | collective-permute-start | bytes 49160 | tf_op jit(solution)/shard_map/ppermute | solution.py:27
  2.1 0.0 copy-start.1
  2.1 2.6 %collective-permute-start.1 = (bf16[16,4,128]{2,1,0:T(4,128)(2,1)S(1)}, bf16[16,4,128]{2,1,0:T(4,128)(2,1)S(1)}, u32[]{:S(2)}, u32[]{:S(2)}) collective-permute-start(bf16[16,4,128]{2,1,0:T(4,128)(2,1)S(1)} %get-tuple-element.44), channel_id=1, source_target_pairs={{4,8},{8,4},{12,0},{0,12},{5,9},{9,5},{13,1},{1,13},{6,10},{10,6},... | collective-permute-start | bytes 49160 | tf_op jit(solution)/shard_map/ppermute | solution.py:27
  4.8 0.0 copy-done
  4.8 0.0 copy-done.2
  4.8 0.0 copy-done.4
  4.8 2.1 %front_planes.1 = (f32[14,256,128]{2,1,0:T(8,128)S(1)}, bf16[16,128,256]{2,1,0:T(8,128)(2,1)S(1)}, bf16[384,384]{1,0:T(8,128)(2,1)S(1)}, f32[1,128]{1,0:T(1,128)S(1)}) custom-call(bf16[16,256,128]{2,1,0:T(8,128)(2,1)S(1)} %bitcast.10, bf16[3,3,3,64,64]{4,3,2,1,0:T(8,128)(2,1)S(1)} %copy-done.2, f32[64]{0:T(128)S(1)} %copy-done.4), custom_call_target="tpu_custom_call" | custom-call | flops 2200000000 | tf_op jit(solution)/shard_map/front_planes/pallas_call | solution.py:635
  6.9 0.0 collective-permute-done.y_near
  6.9 0.0 collective-permute-done.1.y_far
  7.0 1.6 %collective-permute-start.2 = (bf16[272,128]{1,0:T(8,128)(2,1)S(1)}, bf16[272,128]{1,0:T(8,128)(2,1)S(1)}, u32[]{:S(2)}, u32[]{:S(2)}) collective-permute-start(bf16[272,128]{1,0:T(8,128)(2,1)S(1)} %pack_planes.1), channel_id=1, source_target_pairs={{0,16},{16,0},{1,17},{17,1},{2,18},{18,2},{3,19},{19,3},{4,20},{20... | collective-permute-start | bytes 208904 | tf_op jit(solution)/shard_map/ppermute | solution.py:27
  8.5 0.0 copy-done.1
  8.5 2.7 %inner_planes.1 = (bf16[14,256,128]{2,1,0:T(8,128)(2,1)S(1)}, bf16[14,256,128]{2,1,0:T(8,128)(2,1)S(1)}, bf16[14,16,128]{2,1,0:T(8,128)(2,1)S(1)}, f32[384,384]{1,0:T(8,128)S(1)}, f32[8,128]{1,0:T(8,128)S(1)}) custom-call(bf16[16,256,128]{2,1,0:T(8,128)(2,1)S(1)} %bitcast.12, bf16[16,256,128]{2,1,0:T(8,128)(2,1)S(1)} %bitcast.17, ...), custom_call_target="tpu_custom_call" | custom-call | flops 3300000000 | tf_op jit(solution)/shard_map/inner_planes/pallas_call | solution.py:671
  11.2 0.1 collective-permute-done.2.x_near.x_far
  11.4 1.4 %edge_planes.1 = (bf16[2,256,128]{2,1,0:T(8,128)(2,1)S(1)}, bf16[272,128]{1,0:T(8,128)(2,1)S(1)}, bf16[272,128]{1,0:T(8,128)(2,1)S(1)}, f32[384,384]{1,0:T(8,128...) custom-call(bf16[16,256,128]{2,1,0:T(8,128)(2,1)S(1)} %bitcast.13, ...), custom_call_target="tpu_custom_call" | custom-call | flops 2200000000 | tf_op jit(solution)/shard_map/edge_planes/pallas_call | solution.py:689
  12.8 0.0 copy-start.3
  12.8 0.1 collective-permute-start.3
  12.9 0.8 %rest_of_sums.1 = (f32[2,7,16,128]{3,2,1,0:T(8,128)S(1)}, f32[2,7,16,128]{3,2,1,0:T(8,128)S(1)}, f32[2,7,16,128]{3,2,1,0:T(8,128)S(1)}) custom-call(f32[384,384]{1,0:T(8,128)S(1)} %get-tuple-element.56.acc, f32[8,128]{1,0:T(8,128)S(1)} %get-tuple-element.57.sums), custom_call_target="tpu_custom_call" | custom-call | flops 770000000 | tf_op jit(solution)/shard_map/rest_of_sums/pallas_call | solution.py:773
  13.7 0.4 %collective-permute-start.5 = (f32[2,7,16,128]{3,2,1,0:T(8,128)S(1)}, f32[2,7,16,128]{3,2,1,0:T(8,128)S(1)}, u32[]{:S(2)}, u32[]{:S(2)}) collective-permute-start(f32[2,7,16,128]{3,2,1,0:T(8,128)S(1)} %get-tuple-element.68), channel_id=1, source_target_pairs={{0,4},{4,0},{8,12},{12,8},{1,5},{5,1},{9,13},{13,9},{2,6},{6,2},{1... | collective-permute-start | bytes 344072 | tf_op jit(solution)/shard_map/ppermute | solution.py:27
  14.1 0.1 collective-permute-done.3.refs_1_
  14.2 1.1 %collective-permute-start.4 = (bf16[2,7,16,128]{3,2,1,0:T(8,128)(2,1)S(1)}, bf16[2,7,16,128]{3,2,1,0:T(8,128)(2,1)S(1)}, u32[]{:S(2)}, u32[]{:S(2)}) collective-permute-start(bf16[2,7,16,128]{3,2,1,0:T(8,128)(2,1)S(1)} %add_sums.4.refs_5_), channel_id=1, source_target_pairs={{0,5},{1,4},{2,7},{3,6},{4,1},{5,0},{6,3},{7,2},{8,13},{9,12},{10,... | collective-permute-start | bytes 172040 | tf_op jit(solution)/shard_map/ppermute | solution.py:35
  15.3 0.0 copy-done.3
  15.3 1.0 %back_weights.1 = (bf16[512,768]{1,0:T(8,128)(2,1)S(1)}, f32[14,8,128]{2,1,0:T(8,128)S(1)}) custom-call(bf16[3,3,3,64,64]{4,3,2,1,0:T(8,128)(2,1)S(1)} %copy-done.2, s32[3,3,3]{2,1,0:T(4,128)S(1)} %copy-done.3), custom_call_target="tpu_custom_call" | custom-call | flops 1100000000 | tf_op jit(solution)/shard_map/back_weights/pallas_call | solution.py:624
  16.3 1.4 %input_grad.3.refs_7_ = bf16[16,256,128]{2,1,0:T(8,128)(2,1)} custom-call(bf16[14,256,128]{2,1,0:T(8,128)(2,1)S(1)} %get-tuple-element.49.refs_0_, bf16[14,16,128]{2,1,0:T(8,128)(2,1)S(1)} %get-tuple-element.50.refs_1_, bf16[272,128]{1,0:T(8,128)(2,1)S(1)} %get-tuple-element.53.refs_2_, bf16[272,128]{1,0:T(8,128)(2,1)S(1)} %get-tuple-element.54.refs_3_, ...), custom_call_target="tpu_custom_call" | custom-call | flops 1100000000 | tf_op jit(solution)/shard_map/input_grad/pallas_call | solution.py:726
  17.7 0.5 %collective-permute-done.4.refs_2_ = bf16[2,7,16,128]{3,2,1,0:T(8,128)(2,1)S(1)} collective-permute-done((bf16[2,7,16,128]{3,2,1,0:T(8,128)(2,1)S(1)}, bf16[2,7,16,128]{3,2,1,0:T(8,128)(2,1)S(1)}, u32[]{:S(2)}, u32[]{:S(2)}) %collective-permute-start.4) | collective-permute-done | bytes 57376 | tf_op jit(solution)/shard_map/ppermute | solution.py:35
  18.1 0.0 collective-permute-done.5.refs_1_
  18.2 2.4 %collective-permute-start.6 = (bf16[1,7,16,128]{3,2,1,0:T(8,128)(2,1)S(1)}, bf16[1,7,16,128]{3,2,1,0:T(8,128)(2,1)S(1)}, u32[]{:S(2)}, u32[]{:S(2)}) collective-permute-start(bf16[1,7,16,128]{3,2,1,0:T(8,128)(2,1)S(1)} %get-tuple-element.71), channel_id=1, source_target_pairs={{0,6},{1,7},{2,4},{3,5},{4,2},{5,3},{6,0},{7,1},{8,14},{9,15},{10,... | collective-permute-start | bytes 86024 | tf_op jit(solution)/shard_map/ppermute | solution.py:35
  20.6 1.5 %collective-permute-start.9 = (bf16[272,128]{1,0:T(8,128)(2,1)S(1)}, bf16[272,128]{1,0:T(8,128)(2,1)S(1)}, u32[]{:S(2)}, u32[]{:S(2)}) collective-permute-start(bf16[272,128]{1,0:T(8,128)(2,1)S(1)} %get-tuple-element.75), channel_id=1, source_target_pairs={{0,16},{16,0},{1,17},{17,1},{2,18},{18,2},{3,19},{19,3},{4,20},{20... | collective-permute-start | bytes 208904 | tf_op jit(solution)/shard_map/ppermute | solution.py:27
  22.1 0.4 %collective-permute-done.6.refs_1_ = bf16[1,7,16,128]{3,2,1,0:T(8,128)(2,1)S(1)} collective-permute-done((bf16[1,7,16,128]{3,2,1,0:T(8,128)(2,1)S(1)}, bf16[1,7,16,128]{3,2,1,0:T(8,128)(2,1)S(1)}, u32[]{:S(2)}, u32[]{:S(2)}) %collective-permute-start.6) | collective-permute-done | bytes 28704 | tf_op jit(solution)/shard_map/ppermute | solution.py:35
  22.5 1.0 %collective-permute-start.7 = (bf16[1,7,16,128]{3,2,1,0:T(8,128)(2,1)S(1)}, bf16[1,7,16,128]{3,2,1,0:T(8,128)(2,1)S(1)}, u32[]{:S(2)}, u32[]{:S(2)}) collective-permute-start(bf16[1,7,16,128]{3,2,1,0:T(8,128)(2,1)S(1)} %add_sums.5.refs_8_.refs_0_), channel_id=1, source_target_pairs={{0,12},{1,13},{2,14},{3,15},{4,8},{5,9},{6,10},{7,11},{8,4},{9,5},... | collective-permute-start | bytes 86024 | tf_op jit(solution)/shard_map/ppermute | solution.py:35
  23.5 1.7 %input_grad.4 = (bf16[16,256,128]{2,1,0:T(8,128)(2,1)}, bf16[16,256,128]{2,1,0:T(8,128)(2,1)}) custom-call(bf16[14,256,128]{2,1,0:T(8,128)(2,1)S(1)} %get-tuple-element.49.refs_0_, bf16[14,16,128]{2,1,0:T(8,128)(2,1)S(1)} %get-tuple-element.50.refs_1_, bf16[272,128]{1,0:T(8,128)(2,1)S(1)} %get-tuple-element.53.refs_2_, ...), custom_call_target="tpu_custom_call", output_to_operand_aliasing={{0}: (7, {})} | custom-call | flops 2750000128 | tf_op jit(solution)/shard_map/input_grad/pallas_call | solution.py:726
  25.1 0.7 %collective-permute-done.7.refs_1_ = bf16[1,7,16,128]{3,2,1,0:T(8,128)(2,1)S(1)} collective-permute-done((bf16[1,7,16,128]{3,2,1,0:T(8,128)(2,1)S(1)}, bf16[1,7,16,128]{3,2,1,0:T(8,128)(2,1)S(1)}, u32[]{:S(2)}, u32[]{:S(2)}) %collective-permute-start.7) | collective-permute-done | bytes 28704 | tf_op jit(solution)/shard_map/ppermute | solution.py:35
  25.8 1.3 %collective-permute-start.8 = (bf16[1,7,16,128]{3,2,1,0:T(8,128)(2,1)S(1)}, bf16[1,7,16,128]{3,2,1,0:T(8,128)(2,1)S(1)}, u32[]{:S(2)}, u32[]{:S(2)}) collective-permute-start(bf16[1,7,16,128]{3,2,1,0:T(8,128)(2,1)S(1)} %add_sums.6.refs_8_.refs_0_), channel_id=1, source_target_pairs={{0,20},{1,21},{2,22},{3,23},{4,16},{5,17},{6,18},{7,19},{8,28},{9,... | collective-permute-start | bytes 86024 | tf_op jit(solution)/shard_map/ppermute | solution.py:35
  27.2 0.0 collective-permute-done.9.refs_4_.refs_5_
  27.2 1.7 %input_grad.5 = bf16[16,256,128]{2,1,0:T(8,128)(2,1)} custom-call(bf16[14,256,128]{2,1,0:T(8,128)(2,1)S(1)} %get-tuple-element.49.refs_0_, bf16[14,16,128]{2,1,0:T(8,128)(2,1)S(1)} %get-tuple-element.50.refs_1_, bf16[272,128]{1,0:T(8,128)(2,1)S(1)} %get-tuple-element.53.refs_2_, ...), custom_call_target="tpu_custom_call", output_to_operand_aliasing={{}: (7, {})} | custom-call | flops 2750000128 | tf_op jit(solution)/shard_map/input_grad/pallas_call | solution.py:726
  28.9 0.3 %collective-permute-done.8.refs_1_ = bf16[1,7,16,128]{3,2,1,0:T(8,128)(2,1)S(1)} collective-permute-done((bf16[1,7,16,128]{3,2,1,0:T(8,128)(2,1)S(1)}, bf16[1,7,16,128]{3,2,1,0:T(8,128)(2,1)S(1)}, u32[]{:S(2)}, u32[]{:S(2)}) %collective-permute-start.8) | collective-permute-done | bytes 28704 | tf_op jit(solution)/shard_map/ppermute | solution.py:35
  29.2 0.2 collective-permute-start.10
  29.4 1.1 %collective-permute-done.10.other = f32[7,16,128]{2,1,0:T(8,128)S(1)} collective-permute-done((f32[7,16,128]{2,1,0:T(8,128)S(1)}, f32[7,16,128]{2,1,0:T(8,128)S(1)}, u32[]{:S(2)}, u32[]{:S(2)}) %collective-permute-start.10) | collective-permute-done | bytes 57376 | tf_op jit(solution)/shard_map/ppermute | solution.py:27
  30.5 0.7 %scale_weight_grad.1 = (bf16[27,16,64]{2,1,0:T(8,128)(2,1)}, f32[1,16]{1,0:T(1,128)}) custom-call(f32[7,16,128]{2,1,0:T(8,128)S(1)} %bitcast.15, f32[7,16,128]{2,1,0:T(8,128)S(1)} %collective-permute-done.10.other, f32[14,8,128]{2,1,0:T(8,128)S(1)} %get-tuple-element.79.scale_ref), custom_call_target="tpu_custom_call" | custom-call | tf_op jit(solution)/shard_map/scale_weight_grad/pallas_call | solution.py:815
  (8 shorter events, 0.2 us)
Async XLA Ops:
  1.5 3.2 %copy-start = (bf16[1,16,256,128]{3,2,1,0:T(8,128)(2,1)S(1)}, bf16[1,16,256,128]{3,2,1,0:T(8,128)(2,1)}, u32[]{:S(2)}) copy-start(bf16[1,16,256,128]{3,2,1,0:T(8,128)(2,1)} %param.5) | copy-start | bytes 3145732
  1.5 3.2 %copy-start.2 = (bf16[3,3,3,64,64]{4,3,2,1,0:T(8,128)(2,1)S(1)}, bf16[3,3,3,64,64]{4,3,2,1,0:T(8,128)(2,1)}, u32[]{:S(2)}) copy-start(bf16[3,3,3,64,64]{4,3,2,1,0:T(8,128)(2,1)} %refs_0_) | copy-start | bytes 663556
  1.6 3.2 %copy-start.4 = (f32[64]{0:T(128)S(1)}, f32[64]{0:T(128)}, u32[]{:S(2)}) copy-start(f32[64]{0:T(128)} %offsets.1) | copy-start | bytes 772
  1.6 5.3 %collective-permute-start = (bf16[16,4,128]{2,1,0:T(4,128)(2,1)S(1)}, bf16[16,4,128]{2,1,0:T(4,128)(2,1)S(1)}, u32[]{:S(2)}, u32[]{:S(2)}) collective-permute-start(bf16[16,4,128]{2,1,0:T(4,128)(2,1)S(1)} %get-tuple-element.43), channel_id=1, source_target_pairs={{0,4},{4,0},{8,12},{12,8},{1,5},{5,1},{9,13},{13,9},{2,6},{6,2},{1... | collective-permute-start | bytes 49160 | tf_op jit(solution)/shard_map/ppermute | solution.py:27
  2.1 6.4 %copy-start.1 = (bf16[1,16,256,128]{3,2,1,0:T(8,128)(2,1)S(1)}, bf16[1,16,256,128]{3,2,1,0:T(8,128)(2,1)}, u32[]{:S(2)}) copy-start(bf16[1,16,256,128]{3,2,1,0:T(8,128)(2,1)} %param.8) | copy-start | bytes 3145732
  2.1 4.8 %collective-permute-start.1 = (bf16[16,4,128]{2,1,0:T(4,128)(2,1)S(1)}, bf16[16,4,128]{2,1,0:T(4,128)(2,1)S(1)}, u32[]{:S(2)}, u32[]{:S(2)}) collective-permute-start(bf16[16,4,128]{2,1,0:T(4,128)(2,1)S(1)} %get-tuple-element.44), channel_id=1, source_target_pairs={{4,8},{8,4},{12,0},{0,12},{5,9},{9,5},{13,1},{1,13},{6,10},{10,6},... | collective-permute-start | bytes 49160 | tf_op jit(solution)/shard_map/ppermute | solution.py:27
  7.0 4.4 %collective-permute-start.2 = (bf16[272,128]{1,0:T(8,128)(2,1)S(1)}, bf16[272,128]{1,0:T(8,128)(2,1)S(1)}, u32[]{:S(2)}, u32[]{:S(2)}) collective-permute-start(bf16[272,128]{1,0:T(8,128)(2,1)S(1)} %pack_planes.1), channel_id=1, source_target_pairs={{0,16},{16,0},{1,17},{17,1},{2,18},{18,2},{3,19},{19,3},{4,20},{20... | collective-permute-start | bytes 208904 | tf_op jit(solution)/shard_map/ppermute | solution.py:27
  12.8 2.5 %copy-start.3 = (s32[3,3,3]{2,1,0:T(4,128)S(1)}, s32[3,3,3]{2,1,0:T(4,128)}, u32[]{:S(2)}) copy-start(s32[3,3,3]{2,1,0:T(4,128)} %refs_1_.1) | copy-start | bytes 328
  12.8 1.4 %collective-permute-start.3 = (f32[2,7,16,128]{3,2,1,0:T(8,128)S(1)}, f32[2,7,16,128]{3,2,1,0:T(8,128)S(1)}, u32[]{:S(2)}, u32[]{:S(2)}) collective-permute-start(f32[2,7,16,128]{3,2,1,0:T(8,128)S(1)} %get-tuple-element.59), channel_id=1, source_target_pairs={{0,4},{4,0},{8,12},{12,8},{1,5},{5,1},{9,13},{13,9},{2,6},{6,2},{1... | collective-permute-start | bytes 344072 | tf_op jit(solution)/shard_map/ppermute | solution.py:27
  13.7 4.4 %collective-permute-start.5 = (f32[2,7,16,128]{3,2,1,0:T(8,128)S(1)}, f32[2,7,16,128]{3,2,1,0:T(8,128)S(1)}, u32[]{:S(2)}, u32[]{:S(2)}) collective-permute-start(f32[2,7,16,128]{3,2,1,0:T(8,128)S(1)} %get-tuple-element.68), channel_id=1, source_target_pairs={{0,4},{4,0},{8,12},{12,8},{1,5},{5,1},{9,13},{13,9},{2,6},{6,2},{1... | collective-permute-start | bytes 344072 | tf_op jit(solution)/shard_map/ppermute | solution.py:27
  14.2 3.9 %collective-permute-start.4 = (bf16[2,7,16,128]{3,2,1,0:T(8,128)(2,1)S(1)}, bf16[2,7,16,128]{3,2,1,0:T(8,128)(2,1)S(1)}, u32[]{:S(2)}, u32[]{:S(2)}) collective-permute-start(bf16[2,7,16,128]{3,2,1,0:T(8,128)(2,1)S(1)} %add_sums.4.refs_5_), channel_id=1, source_target_pairs={{0,5},{1,4},{2,7},{3,6},{4,1},{5,0},{6,3},{7,2},{8,13},{9,12},{10,... | collective-permute-start | bytes 172040 | tf_op jit(solution)/shard_map/ppermute | solution.py:35
  18.2 4.3 %collective-permute-start.6 = (bf16[1,7,16,128]{3,2,1,0:T(8,128)(2,1)S(1)}, bf16[1,7,16,128]{3,2,1,0:T(8,128)(2,1)S(1)}, u32[]{:S(2)}, u32[]{:S(2)}) collective-permute-start(bf16[1,7,16,128]{3,2,1,0:T(8,128)(2,1)S(1)} %get-tuple-element.71), channel_id=1, source_target_pairs={{0,6},{1,7},{2,4},{3,5},{4,2},{5,3},{6,0},{7,1},{8,14},{9,15},{10,... | collective-permute-start | bytes 86024 | tf_op jit(solution)/shard_map/ppermute | solution.py:35
  20.6 6.5 %collective-permute-start.9 = (bf16[272,128]{1,0:T(8,128)(2,1)S(1)}, bf16[272,128]{1,0:T(8,128)(2,1)S(1)}, u32[]{:S(2)}, u32[]{:S(2)}) collective-permute-start(bf16[272,128]{1,0:T(8,128)(2,1)S(1)} %get-tuple-element.75), channel_id=1, source_target_pairs={{0,16},{16,0},{1,17},{17,1},{2,18},{18,2},{3,19},{19,3},{4,20},{20... | collective-permute-start | bytes 208904 | tf_op jit(solution)/shard_map/ppermute | solution.py:27
  22.5 3.4 %collective-permute-start.7 = (bf16[1,7,16,128]{3,2,1,0:T(8,128)(2,1)S(1)}, bf16[1,7,16,128]{3,2,1,0:T(8,128)(2,1)S(1)}, u32[]{:S(2)}, u32[]{:S(2)}) collective-permute-start(bf16[1,7,16,128]{3,2,1,0:T(8,128)(2,1)S(1)} %add_sums.5.refs_8_.refs_0_), channel_id=1, source_target_pairs={{0,12},{1,13},{2,14},{3,15},{4,8},{5,9},{6,10},{7,11},{8,4},{9,5},... | collective-permute-start | bytes 86024 | tf_op jit(solution)/shard_map/ppermute | solution.py:35
  25.8 3.4 %collective-permute-start.8 = (bf16[1,7,16,128]{3,2,1,0:T(8,128)(2,1)S(1)}, bf16[1,7,16,128]{3,2,1,0:T(8,128)(2,1)S(1)}, u32[]{:S(2)}, u32[]{:S(2)}) collective-permute-start(bf16[1,7,16,128]{3,2,1,0:T(8,128)(2,1)S(1)} %add_sums.6.refs_8_.refs_0_), channel_id=1, source_target_pairs={{0,20},{1,21},{2,22},{3,23},{4,16},{5,17},{6,18},{7,19},{8,28},{9,... | collective-permute-start | bytes 86024 | tf_op jit(solution)/shard_map/ppermute | solution.py:35
  29.2 1.3 %collective-permute-start.10 = (f32[7,16,128]{2,1,0:T(8,128)S(1)}, f32[7,16,128]{2,1,0:T(8,128)S(1)}, u32[]{:S(2)}, u32[]{:S(2)}) collective-permute-start(f32[7,16,128]{2,1,0:T(8,128)S(1)} %bitcast.14), channel_id=1, source_target_pairs={{0,4},{4,0},{8,12},{12,8},{1,5},{5,1},{9,13},{13,9},{2,6},{6,2},{1... | collective-permute-start | bytes 172040 | tf_op jit(solution)/shard_map/ppermute | solution.py:27

commit v6 on v5

--- a/solution.py
+++ b/solution.py
@@ -168,6 +168,15 @@
     )
 
 
+def outer_turned(bodies, grads):
+    return lax.dot_general(
+        jnp.concatenate(grads, axis=0),
+        jnp.concatenate([jnp.concatenate(three, axis=1) for three in bodies], axis=0),
+        (((0,), (0,)), ((), ())),
+        preferred_element_type=F32,
+    )
+
+
 def oriented(near, far, side, place):
     @pl.when(side == 0)
     def _():
@@ -285,7 +294,7 @@
 def inner_kernel(
     f_ref, u_ref, y_near, y_far, pre_ref, turned, w_ref, bias_ref,
     act, grad_ref, rim_ref, acc_ref, sums_ref,
-    f_rim, u_rim, wide,
+    f_rim, u_rim, wide, acc,
 ):
     size_x, size_y, width = f_ref.shape
     inner = size_x - 2
@@ -337,14 +346,22 @@
                 act[q, y : y + CHUNK, :] = value.astype(BF16)
                 grad_ref[q, y : y + CHUNK, :] = rounded
                 sums = sums + jnp.sum(exact.reshape(CHUNK // 8, 8, width), axis=0)
-        term = outer(
-            [[turned[q + j] for j in range(3)] for q in (p, p + 1)],
-            [shifted_grads(wide, q) for q in (p, p + 1)],
-        )
-        if p == 0:
-            acc_ref[...] = term
-        else:
-            acc_ref[...] += term
+        grads = [shifted_grads(wide, q) for q in (p, p + 1)]
+        if p < inner - 2:
+            term = outer([[turned[q + j] for j in range(3)] for q in (p, p + 1)], grads)
+            if p == 0:
+                acc[...] = term
+            else:
+                acc[...] += term
+        if p == inner - 4:
+            for a in range(3):
+                for b in range(3):
+                    here, there = slice(a * width, (a + 1) * width), slice(b * width, (b + 1) * width)
+                    acc_ref[there, here] = acc[here, there].T
+        if p == inner - 2:
+            acc_ref[...] += outer_turned(
+                [[f_ref[q + j] for j in range(3)] for q in (p, p + 1)], grads
+            )
     sums_ref[...] = sums
 
 
@@ -355,7 +372,7 @@
 
     def block(t):
         a, b = t // 3, t % 3
-        return acc[a * width : (a + 1) * width, b * width : (b + 1) * width].T
+        return acc[b * width : (b + 1) * width, a * width : (a + 1) * width]
 
     def lower(rows):
         return lax.broadcasted_iota(jnp.int32, (rows, width), 1) < half
@@ -439,10 +456,7 @@
             taps, wide, p, bias, sums, u_ref.at[x], u_rim.at[x], act.at[p],
             outs[p].at[pl.ds(0, size_y)], outs[p].at[pl.ds(size_y, 2 * RIM)],
         )
-    acc[...] = acc_ref[...] + outer(
-        [[plane.T for plane in bodies[p]] for p in range(2)],
-        [shifted_grads(wide, p) for p in range(2)],
-    )
+    acc[...] = acc_ref[...] + outer_turned(bodies, [shifted_grads(wide, p) for p in range(2)])
 
     def hand(last, first):
         if last is not None:
@@ -679,7 +693,10 @@
         ),
         in_specs=[VMEM] * 8,
         out_specs=(VMEM,) * 5,
-        scratch_shapes=rims + [pltpu.VMEM((inner, rows, width), F32)],
+        scratch_shapes=rims + [
+            pltpu.VMEM((inner, rows, width), F32),
+            pltpu.VMEM((3 * width, 3 * width), F32),
+        ],
         compiler_params=grant(12),
         cost_estimate=cost(3.0),
         name="inner_planes",

time: 31.4 us -> 31.1 us (level)
  Pallas kernels: 13.6 us -> 12.8 us
  starting transfers between devices: 12.7 us -> 13.2 us
    pallas_call x1, Pallas kernels: 0.83 us -> 0.31 us  [local(): pl.pallas_call(rest_kernel, out_shape=(shape(*blocks, dtype=F32),) * 3, i...]
    ppermute x7, waiting for transfers between devices: 1.35 us -> 1.72 us  [swap(): return lax.ppermute(value, axis, links)]
    pallas_call x1, Pallas kernels: 1.41 us -> 1.07 us  [local(): pl.pallas_call(edge_kernel, out_shape=(shape(2, size_y, width), shape(tal...]
    ppermute x4, waiting for transfers between devices: 1.83 us -> 1.52 us  [exchange(): lax.ppermute(value, axes, [(i, i ^ flip) for i in range(math.prod(sizes))])]
  transfers between devices with their start and end apart: 11 -> 11, of which waited for: 7 -> 7; matrix products, arithmetic and copies ran while one was open for 0% -> 0% of each run, Pallas kernels for 36% -> 35%
where the time goes in v6:
time: 31.1 us; the launch traced here: 30.9 us
  starting transfers between devices  13.2 us (42%)
  Pallas kernels  12.8 us (41%)
  waiting for transfers between devices  3.23 us (10%)
  local copies, waits for them, and re-layouts  0.87 us (3%)
  between operations  0.78 us (3%)
    ppermute x7, starting transfers between devices, swap(): return lax.ppermute(value, axis, links)  6.99 us
    ppermute x4, starting transfers between devices, exchange(): lax.ppermute(value, axes, [(i, i ^ flip) for i in range(math.prod(sizes))])  6.17 us
    pallas_call x3, Pallas kernels, back(): pl.pallas_call(lambda *refs: back_kernel(pairs, edges, stored, *refs), ou...  4.74 us
    pallas_call x1, Pallas kernels, local(): pl.pallas_call(inner_kernel, out_shape=(shape(inner, size_y, width), shap...  2.67 us
    pallas_call x1, Pallas kernels, local(): pl.pallas_call(front_kernel, out_shape=(shape(inner, size_y, width, dtype...  2.12 us
    ppermute x7, waiting for transfers between devices, swap(): return lax.ppermute(value, axis, links)  1.72 us
    ppermute x4, waiting for transfers between devices, exchange(): lax.ppermute(value, axes, [(i, i ^ flip) for i in range(math.prod(sizes))])  1.52 us
    pallas_call x1, Pallas kernels, local(): pl.pallas_call(edge_kernel, out_shape=(shape(2, size_y, width), shape(tal...  1.07 us
  transfers between devices with their start and end apart: 11, of which 7 were waited for; matrix products, arithmetic and copies ran while one was open for 0% of the time, Pallas kernels for 35%

profile of v6, /device:TPU:0, one launch (start us, length us, event | category | flops | bytes accessed | tf_op | source)
XLA Modules:
  0.0 30.9 jit_solution(12762386801368562147)
XLA Ops:
  0.6 0.8 %fusion = (bf16[16,2,128]{2,1,0:T(2,128)(2,1)S(1)}, bf16[16,2,128]{2,1,0:T(2,128)(2,1)S(1)}, bf16[16,2,128]{2,1,0:T(2,128)(2,1)S(1)}, bf16[16,2,128]{2,1,0:T(2,128)(2,1)S(1)}) fusion(bf16[16,256,128]{2,1,0:T(8,128)(2,1)} %bitcast.9, bf16[16,256,128]{2,1,0:T(8,128)(2,1)} %bitcast.16), kind=kLoop, calls=%fused_computation.1 | loop fusion | bytes 65536 | tf_op jit(solution)/shard_map/slice | solution.py:619
  1.5 0.0 copy-start
  1.5 0.0 copy-start.2
  1.6 0.0 copy-start.4
  1.6 0.5 %collective-permute-start = (bf16[16,4,128]{2,1,0:T(4,128)(2,1)S(1)}, bf16[16,4,128]{2,1,0:T(4,128)(2,1)S(1)}, u32[]{:S(2)}, u32[]{:S(2)}) collective-permute-start(bf16[16,4,128]{2,1,0:T(4,128)(2,1)S(1)} %get-tuple-element.43), channel_id=1, source_target_pairs={{0,4},{4,0},{8,12},{12,8},{1,5},{5,1},{9,13},{13,9},{2,6},{6,2},{1... | collective-permute-start | bytes 49160 | tf_op jit(solution)/shard_map/ppermute | solution.py:27
  2.1 0.0 copy-start.1
  2.1 2.6 %collective-permute-start.1 = (bf16[16,4,128]{2,1,0:T(4,128)(2,1)S(1)}, bf16[16,4,128]{2,1,0:T(4,128)(2,1)S(1)}, u32[]{:S(2)}, u32[]{:S(2)}) collective-permute-start(bf16[16,4,128]{2,1,0:T(4,128)(2,1)S(1)} %get-tuple-element.44), channel_id=1, source_target_pairs={{4,8},{8,4},{12,0},{0,12},{5,9},{9,5},{13,1},{1,13},{6,10},{10,6},... | collective-permute-start | bytes 49160 | tf_op jit(solution)/shard_map/ppermute | solution.py:27
  4.8 0.0 copy-done
  4.8 0.0 copy-done.2
  4.8 0.0 copy-done.4
  4.8 2.1 %front_planes.1 = (f32[14,256,128]{2,1,0:T(8,128)S(1)}, bf16[16,128,256]{2,1,0:T(8,128)(2,1)S(1)}, bf16[384,384]{1,0:T(8,128)(2,1)S(1)}, f32[1,128]{1,0:T(1,128)S(1)}) custom-call(bf16[16,256,128]{2,1,0:T(8,128)(2,1)S(1)} %bitcast.10, bf16[3,3,3,64,64]{4,3,2,1,0:T(8,128)(2,1)S(1)} %copy-done.2, f32[64]{0:T(128)S(1)} %copy-done.4), custom_call_target="tpu_custom_call" | custom-call | flops 2200000000 | tf_op jit(solution)/shard_map/front_planes/pallas_call | solution.py:649
  6.9 0.0 collective-permute-done.y_near
  6.9 0.0 collective-permute-done.1.y_far
  7.0 1.6 %collective-permute-start.2 = (bf16[272,128]{1,0:T(8,128)(2,1)S(1)}, bf16[272,128]{1,0:T(8,128)(2,1)S(1)}, u32[]{:S(2)}, u32[]{:S(2)}) collective-permute-start(bf16[272,128]{1,0:T(8,128)(2,1)S(1)} %pack_planes.1), channel_id=1, source_target_pairs={{0,16},{16,0},{1,17},{17,1},{2,18},{18,2},{3,19},{19,3},{4,20},{20... | collective-permute-start | bytes 208904 | tf_op jit(solution)/shard_map/ppermute | solution.py:27
  8.5 0.0 copy-done.1
  8.5 2.7 %inner_planes.1 = (bf16[14,256,128]{2,1,0:T(8,128)(2,1)S(1)}, bf16[14,256,128]{2,1,0:T(8,128)(2,1)S(1)}, bf16[14,16,128]{2,1,0:T(8,128)(2,1)S(1)}, f32[384,384]{1,0:T(8,128)S(1)}, f32[8,128]{1,0:T(8,128)S(1)}) custom-call(bf16[16,256,128]{2,1,0:T(8,128)(2,1)S(1)} %bitcast.12, bf16[16,256,128]{2,1,0:T(8,128)(2,1)S(1)} %bitcast.17, ...), custom_call_target="tpu_custom_call" | custom-call | flops 3300000000 | tf_op jit(solution)/shard_map/inner_planes/pallas_call | solution.py:685
  11.2 0.1 collective-permute-done.2.x_near.x_far
  11.4 1.1 %edge_planes.1 = (bf16[2,256,128]{2,1,0:T(8,128)(2,1)S(1)}, bf16[272,128]{1,0:T(8,128)(2,1)S(1)}, bf16[272,128]{1,0:T(8,128)(2,1)S(1)}, f32[384,384]{1,0:T(8,128...) custom-call(bf16[16,256,128]{2,1,0:T(8,128)(2,1)S(1)} %bitcast.13, ...), custom_call_target="tpu_custom_call" | custom-call | flops 2200000000 | tf_op jit(solution)/shard_map/edge_planes/pallas_call | solution.py:706
  12.4 0.0 copy-start.3
  12.4 0.1 collective-permute-start.3
  12.5 0.3 %rest_of_sums.1 = (f32[2,7,16,128]{3,2,1,0:T(8,128)S(1)}, f32[2,7,16,128]{3,2,1,0:T(8,128)S(1)}, f32[2,7,16,128]{3,2,1,0:T(8,128)S(1)}) custom-call(f32[384,384]{1,0:T(8,128)S(1)} %get-tuple-element.56.acc, f32[8,128]{1,0:T(8,128)S(1)} %get-tuple-element.57.sums), custom_call_target="tpu_custom_call" | custom-call | flops 770000000 | tf_op jit(solution)/shard_map/rest_of_sums/pallas_call | solution.py:790
  12.8 0.5 %collective-permute-start.5 = (f32[2,7,16,128]{3,2,1,0:T(8,128)S(1)}, f32[2,7,16,128]{3,2,1,0:T(8,128)S(1)}, u32[]{:S(2)}, u32[]{:S(2)}) collective-permute-start(f32[2,7,16,128]{3,2,1,0:T(8,128)S(1)} %get-tuple-element.68), channel_id=1, source_target_pairs={{0,4},{4,0},{8,12},{12,8},{1,5},{5,1},{9,13},{13,9},{2,6},{6,2},{1... | collective-permute-start | bytes 344072 | tf_op jit(solution)/shard_map/ppermute | solution.py:27
  13.3 0.5 %collective-permute-done.3.refs_1_ = f32[2,7,16,128]{3,2,1,0:T(8,128)S(1)} collective-permute-done((f32[2,7,16,128]{3,2,1,0:T(8,128)S(1)}, f32[2,7,16,128]{3,2,1,0:T(8,128)S(1)}, u32[]{:S(2)}, u32[]{:S(2)}) %collective-permute-start.3) | collective-permute-done | bytes 114720 | tf_op jit(solution)/shard_map/ppermute | solution.py:27
  13.8 1.4 %collective-permute-start.4 = (bf16[2,7,16,128]{3,2,1,0:T(8,128)(2,1)S(1)}, bf16[2,7,16,128]{3,2,1,0:T(8,128)(2,1)S(1)}, u32[]{:S(2)}, u32[]{:S(2)}) collective-permute-start(bf16[2,7,16,128]{3,2,1,0:T(8,128)(2,1)S(1)} %add_sums.4.refs_5_), channel_id=1, source_target_pairs={{0,5},{1,4},{2,7},{3,6},{4,1},{5,0},{6,3},{7,2},{8,13},{9,12},{10,... | collective-permute-start | bytes 172040 | tf_op jit(solution)/shard_map/ppermute | solution.py:35
  15.2 0.0 copy-done.3
  15.2 1.0 %back_weights.1 = (bf16[512,768]{1,0:T(8,128)(2,1)S(1)}, f32[14,8,128]{2,1,0:T(8,128)S(1)}) custom-call(bf16[3,3,3,64,64]{4,3,2,1,0:T(8,128)(2,1)S(1)} %copy-done.2, s32[3,3,3]{2,1,0:T(4,128)S(1)} %copy-done.3), custom_call_target="tpu_custom_call" | custom-call | flops 1100000000 | tf_op jit(solution)/shard_map/back_weights/pallas_call | solution.py:638
  16.2 1.4 %input_grad.3.refs_7_ = bf16[16,256,128]{2,1,0:T(8,128)(2,1)} custom-call(bf16[14,256,128]{2,1,0:T(8,128)(2,1)S(1)} %get-tuple-element.49.refs_0_, bf16[14,16,128]{2,1,0:T(8,128)(2,1)S(1)} %get-tuple-element.50.refs_1_, bf16[272,128]{1,0:T(8,128)(2,1)S(1)} %get-tuple-element.53.refs_2_, bf16[272,128]{1,0:T(8,128)(2,1)S(1)} %get-tuple-element.54.refs_3_, ...), custom_call_target="tpu_custom_call" | custom-call | flops 1100000000 | tf_op jit(solution)/shard_map/input_grad/pallas_call | solution.py:743
  17.6 0.2 collective-permute-done.4.refs_2_
  17.8 0.0 collective-permute-done.5.refs_1_
  17.8 2.4 %collective-permute-start.6 = (bf16[1,7,16,128]{3,2,1,0:T(8,128)(2,1)S(1)}, bf16[1,7,16,128]{3,2,1,0:T(8,128)(2,1)S(1)}, u32[]{:S(2)}, u32[]{:S(2)}) collective-permute-start(bf16[1,7,16,128]{3,2,1,0:T(8,128)(2,1)S(1)} %get-tuple-element.71), channel_id=1, source_target_pairs={{0,6},{1,7},{2,4},{3,5},{4,2},{5,3},{6,0},{7,1},{8,14},{9,15},{10,... | collective-permute-start | bytes 86024 | tf_op jit(solution)/shard_map/ppermute | solution.py:35
  20.3 1.5 %collective-permute-start.9 = (bf16[272,128]{1,0:T(8,128)(2,1)S(1)}, bf16[272,128]{1,0:T(8,128)(2,1)S(1)}, u32[]{:S(2)}, u32[]{:S(2)}) collective-permute-start(bf16[272,128]{1,0:T(8,128)(2,1)S(1)} %get-tuple-element.75), channel_id=1, source_target_pairs={{0,16},{16,0},{1,17},{17,1},{2,18},{18,2},{3,19},{19,3},{4,20},{20... | collective-permute-start | bytes 208904 | tf_op jit(solution)/shard_map/ppermute | solution.py:27
  21.7 0.3 %collective-permute-done.6.refs_1_ = bf16[1,7,16,128]{3,2,1,0:T(8,128)(2,1)S(1)} collective-permute-done((bf16[1,7,16,128]{3,2,1,0:T(8,128)(2,1)S(1)}, bf16[1,7,16,128]{3,2,1,0:T(8,128)(2,1)S(1)}, u32[]{:S(2)}, u32[]{:S(2)}) %collective-permute-start.6) | collective-permute-done | bytes 28704 | tf_op jit(solution)/shard_map/ppermute | solution.py:35
  22.1 1.0 %collective-permute-start.7 = (bf16[1,7,16,128]{3,2,1,0:T(8,128)(2,1)S(1)}, bf16[1,7,16,128]{3,2,1,0:T(8,128)(2,1)S(1)}, u32[]{:S(2)}, u32[]{:S(2)}) collective-permute-start(bf16[1,7,16,128]{3,2,1,0:T(8,128)(2,1)S(1)} %add_sums.5.refs_8_.refs_0_), channel_id=1, source_target_pairs={{0,12},{1,13},{2,14},{3,15},{4,8},{5,9},{6,10},{7,11},{8,4},{9,5},... | collective-permute-start | bytes 86024 | tf_op jit(solution)/shard_map/ppermute | solution.py:35
  23.1 1.7 %input_grad.4 = (bf16[16,256,128]{2,1,0:T(8,128)(2,1)}, bf16[16,256,128]{2,1,0:T(8,128)(2,1)}) custom-call(bf16[14,256,128]{2,1,0:T(8,128)(2,1)S(1)} %get-tuple-element.49.refs_0_, bf16[14,16,128]{2,1,0:T(8,128)(2,1)S(1)} %get-tuple-element.50.refs_1_, bf16[272,128]{1,0:T(8,128)(2,1)S(1)} %get-tuple-element.53.refs_2_, ...), custom_call_target="tpu_custom_call", output_to_operand_aliasing={{0}: (7, {})} | custom-call | flops 2750000128 | tf_op jit(solution)/shard_map/input_grad/pallas_call | solution.py:743
  24.8 0.7 %collective-permute-done.7.refs_1_ = bf16[1,7,16,128]{3,2,1,0:T(8,128)(2,1)S(1)} collective-permute-done((bf16[1,7,16,128]{3,2,1,0:T(8,128)(2,1)S(1)}, bf16[1,7,16,128]{3,2,1,0:T(8,128)(2,1)S(1)}, u32[]{:S(2)}, u32[]{:S(2)}) %collective-permute-start.7) | collective-permute-done | bytes 28704 | tf_op jit(solution)/shard_map/ppermute | solution.py:35
  25.5 1.3 %collective-permute-start.8 = (bf16[1,7,16,128]{3,2,1,0:T(8,128)(2,1)S(1)}, bf16[1,7,16,128]{3,2,1,0:T(8,128)(2,1)S(1)}, u32[]{:S(2)}, u32[]{:S(2)}) collective-permute-start(bf16[1,7,16,128]{3,2,1,0:T(8,128)(2,1)S(1)} %add_sums.6.refs_8_.refs_0_), channel_id=1, source_target_pairs={{0,20},{1,21},{2,22},{3,23},{4,16},{5,17},{6,18},{7,19},{8,28},{9,... | collective-permute-start | bytes 86024 | tf_op jit(solution)/shard_map/ppermute | solution.py:35
  26.8 0.0 collective-permute-done.9.refs_4_.refs_5_
  26.8 1.7 %input_grad.5 = bf16[16,256,128]{2,1,0:T(8,128)(2,1)} custom-call(bf16[14,256,128]{2,1,0:T(8,128)(2,1)S(1)} %get-tuple-element.49.refs_0_, bf16[14,16,128]{2,1,0:T(8,128)(2,1)S(1)} %get-tuple-element.50.refs_1_, bf16[272,128]{1,0:T(8,128)(2,1)S(1)} %get-tuple-element.53.refs_2_, ...), custom_call_target="tpu_custom_call", output_to_operand_aliasing={{}: (7, {})} | custom-call | flops 2750000128 | tf_op jit(solution)/shard_map/input_grad/pallas_call | solution.py:743
  28.5 0.3 %collective-permute-done.8.refs_1_ = bf16[1,7,16,128]{3,2,1,0:T(8,128)(2,1)S(1)} collective-permute-done((bf16[1,7,16,128]{3,2,1,0:T(8,128)(2,1)S(1)}, bf16[1,7,16,128]{3,2,1,0:T(8,128)(2,1)S(1)}, u32[]{:S(2)}, u32[]{:S(2)}) %collective-permute-start.8) | collective-permute-done | bytes 28704 | tf_op jit(solution)/shard_map/ppermute | solution.py:35
  28.8 0.2 collective-permute-start.10
  29.1 1.1 %collective-permute-done.10.other = f32[7,16,128]{2,1,0:T(8,128)S(1)} collective-permute-done((f32[7,16,128]{2,1,0:T(8,128)S(1)}, f32[7,16,128]{2,1,0:T(8,128)S(1)}, u32[]{:S(2)}, u32[]{:S(2)}) %collective-permute-start.10) | collective-permute-done | bytes 57376 | tf_op jit(solution)/shard_map/ppermute | solution.py:27
  30.1 0.7 %scale_weight_grad.1 = (bf16[27,16,64]{2,1,0:T(8,128)(2,1)}, f32[1,16]{1,0:T(1,128)}) custom-call(f32[7,16,128]{2,1,0:T(8,128)S(1)} %bitcast.15, f32[7,16,128]{2,1,0:T(8,128)S(1)} %collective-permute-done.10.other, f32[14,8,128]{2,1,0:T(8,128)S(1)} %get-tuple-element.79.scale_ref), custom_call_target="tpu_custom_call" | custom-call | tf_op jit(solution)/shard_map/scale_weight_grad/pallas_call | solution.py:832
  (8 shorter events, 0.2 us)
Async XLA Ops:
  1.5 3.2 %copy-start = (bf16[1,16,256,128]{3,2,1,0:T(8,128)(2,1)S(1)}, bf16[1,16,256,128]{3,2,1,0:T(8,128)(2,1)}, u32[]{:S(2)}) copy-start(bf16[1,16,256,128]{3,2,1,0:T(8,128)(2,1)} %param.5) | copy-start | bytes 3145732
  1.5 3.2 %copy-start.2 = (bf16[3,3,3,64,64]{4,3,2,1,0:T(8,128)(2,1)S(1)}, bf16[3,3,3,64,64]{4,3,2,1,0:T(8,128)(2,1)}, u32[]{:S(2)}) copy-start(bf16[3,3,3,64,64]{4,3,2,1,0:T(8,128)(2,1)} %refs_0_) | copy-start | bytes 663556
  1.6 3.2 %copy-start.4 = (f32[64]{0:T(128)S(1)}, f32[64]{0:T(128)}, u32[]{:S(2)}) copy-start(f32[64]{0:T(128)} %offsets.1) | copy-start | bytes 772
  1.6 5.3 %collective-permute-start = (bf16[16,4,128]{2,1,0:T(4,128)(2,1)S(1)}, bf16[16,4,128]{2,1,0:T(4,128)(2,1)S(1)}, u32[]{:S(2)}, u32[]{:S(2)}) collective-permute-start(bf16[16,4,128]{2,1,0:T(4,128)(2,1)S(1)} %get-tuple-element.43), channel_id=1, source_target_pairs={{0,4},{4,0},{8,12},{12,8},{1,5},{5,1},{9,13},{13,9},{2,6},{6,2},{1... | collective-permute-start | bytes 49160 | tf_op jit(solution)/shard_map/ppermute | solution.py:27
  2.1 6.4 %copy-start.1 = (bf16[1,16,256,128]{3,2,1,0:T(8,128)(2,1)S(1)}, bf16[1,16,256,128]{3,2,1,0:T(8,128)(2,1)}, u32[]{:S(2)}) copy-start(bf16[1,16,256,128]{3,2,1,0:T(8,128)(2,1)} %param.8) | copy-start | bytes 3145732
  2.1 4.8 %collective-permute-start.1 = (bf16[16,4,128]{2,1,0:T(4,128)(2,1)S(1)}, bf16[16,4,128]{2,1,0:T(4,128)(2,1)S(1)}, u32[]{:S(2)}, u32[]{:S(2)}) collective-permute-start(bf16[16,4,128]{2,1,0:T(4,128)(2,1)S(1)} %get-tuple-element.44), channel_id=1, source_target_pairs={{4,8},{8,4},{12,0},{0,12},{5,9},{9,5},{13,1},{1,13},{6,10},{10,6},... | collective-permute-start | bytes 49160 | tf_op jit(solution)/shard_map/ppermute | solution.py:27
  7.0 4.4 %collective-permute-start.2 = (bf16[272,128]{1,0:T(8,128)(2,1)S(1)}, bf16[272,128]{1,0:T(8,128)(2,1)S(1)}, u32[]{:S(2)}, u32[]{:S(2)}) collective-permute-start(bf16[272,128]{1,0:T(8,128)(2,1)S(1)} %pack_planes.1), channel_id=1, source_target_pairs={{0,16},{16,0},{1,17},{17,1},{2,18},{18,2},{3,19},{19,3},{4,20},{20... | collective-permute-start | bytes 208904 | tf_op jit(solution)/shard_map/ppermute | solution.py:27
  12.4 2.8 %copy-start.3 = (s32[3,3,3]{2,1,0:T(4,128)S(1)}, s32[3,3,3]{2,1,0:T(4,128)}, u32[]{:S(2)}) copy-start(s32[3,3,3]{2,1,0:T(4,128)} %refs_1_.1) | copy-start | bytes 328
  12.4 1.4 %collective-permute-start.3 = (f32[2,7,16,128]{3,2,1,0:T(8,128)S(1)}, f32[2,7,16,128]{3,2,1,0:T(8,128)S(1)}, u32[]{:S(2)}, u32[]{:S(2)}) collective-permute-start(f32[2,7,16,128]{3,2,1,0:T(8,128)S(1)} %get-tuple-element.59), channel_id=1, source_target_pairs={{0,4},{4,0},{8,12},{12,8},{1,5},{5,1},{9,13},{13,9},{2,6},{6,2},{1... | collective-permute-start | bytes 344072 | tf_op jit(solution)/shard_map/ppermute | solution.py:27
  12.8 5.0 %collective-permute-start.5 = (f32[2,7,16,128]{3,2,1,0:T(8,128)S(1)}, f32[2,7,16,128]{3,2,1,0:T(8,128)S(1)}, u32[]{:S(2)}, u32[]{:S(2)}) collective-permute-start(f32[2,7,16,128]{3,2,1,0:T(8,128)S(1)} %get-tuple-element.68), channel_id=1, source_target_pairs={{0,4},{4,0},{8,12},{12,8},{1,5},{5,1},{9,13},{13,9},{2,6},{6,2},{1... | collective-permute-start | bytes 344072 | tf_op jit(solution)/shard_map/ppermute | solution.py:27
  13.8 3.9 %collective-permute-start.4 = (bf16[2,7,16,128]{3,2,1,0:T(8,128)(2,1)S(1)}, bf16[2,7,16,128]{3,2,1,0:T(8,128)(2,1)S(1)}, u32[]{:S(2)}, u32[]{:S(2)}) collective-permute-start(bf16[2,7,16,128]{3,2,1,0:T(8,128)(2,1)S(1)} %add_sums.4.refs_5_), channel_id=1, source_target_pairs={{0,5},{1,4},{2,7},{3,6},{4,1},{5,0},{6,3},{7,2},{8,13},{9,12},{10,... | collective-permute-start | bytes 172040 | tf_op jit(solution)/shard_map/ppermute | solution.py:35
  17.8 4.3 %collective-permute-start.6 = (bf16[1,7,16,128]{3,2,1,0:T(8,128)(2,1)S(1)}, bf16[1,7,16,128]{3,2,1,0:T(8,128)(2,1)S(1)}, u32[]{:S(2)}, u32[]{:S(2)}) collective-permute-start(bf16[1,7,16,128]{3,2,1,0:T(8,128)(2,1)S(1)} %get-tuple-element.71), channel_id=1, source_target_pairs={{0,6},{1,7},{2,4},{3,5},{4,2},{5,3},{6,0},{7,1},{8,14},{9,15},{10,... | collective-permute-start | bytes 86024 | tf_op jit(solution)/shard_map/ppermute | solution.py:35
  20.3 6.6 %collective-permute-start.9 = (bf16[272,128]{1,0:T(8,128)(2,1)S(1)}, bf16[272,128]{1,0:T(8,128)(2,1)S(1)}, u32[]{:S(2)}, u32[]{:S(2)}) collective-permute-start(bf16[272,128]{1,0:T(8,128)(2,1)S(1)} %get-tuple-element.75), channel_id=1, source_target_pairs={{0,16},{16,0},{1,17},{17,1},{2,18},{18,2},{3,19},{19,3},{4,20},{20... | collective-permute-start | bytes 208904 | tf_op jit(solution)/shard_map/ppermute | solution.py:27
  22.1 3.4 %collective-permute-start.7 = (bf16[1,7,16,128]{3,2,1,0:T(8,128)(2,1)S(1)}, bf16[1,7,16,128]{3,2,1,0:T(8,128)(2,1)S(1)}, u32[]{:S(2)}, u32[]{:S(2)}) collective-permute-start(bf16[1,7,16,128]{3,2,1,0:T(8,128)(2,1)S(1)} %add_sums.5.refs_8_.refs_0_), channel_id=1, source_target_pairs={{0,12},{1,13},{2,14},{3,15},{4,8},{5,9},{6,10},{7,11},{8,4},{9,5},... | collective-permute-start | bytes 86024 | tf_op jit(solution)/shard_map/ppermute | solution.py:35
  25.5 3.4 %collective-permute-start.8 = (bf16[1,7,16,128]{3,2,1,0:T(8,128)(2,1)S(1)}, bf16[1,7,16,128]{3,2,1,0:T(8,128)(2,1)S(1)}, u32[]{:S(2)}, u32[]{:S(2)}) collective-permute-start(bf16[1,7,16,128]{3,2,1,0:T(8,128)(2,1)S(1)} %add_sums.6.refs_8_.refs_0_), channel_id=1, source_target_pairs={{0,20},{1,21},{2,22},{3,23},{4,16},{5,17},{6,18},{7,19},{8,28},{9,... | collective-permute-start | bytes 86024 | tf_op jit(solution)/shard_map/ppermute | solution.py:35
  28.8 1.3 %collective-permute-start.10 = (f32[7,16,128]{2,1,0:T(8,128)S(1)}, f32[7,16,128]{2,1,0:T(8,128)S(1)}, u32[]{:S(2)}, u32[]{:S(2)}) collective-permute-start(f32[7,16,128]{2,1,0:T(8,128)S(1)} %bitcast.14), channel_id=1, source_target_pairs={{0,4},{4,0},{8,12},{12,8},{1,5},{5,1},{9,13},{13,9},{2,6},{6,2},{1... | collective-permute-start | bytes 172040 | tf_op jit(solution)/shard_map/ppermute | solution.py:27

commit v7 on v6

--- a/solution.py
+++ b/solution.py
@@ -130,7 +130,7 @@
     )
 
 
-def activate(taps, wide, p, bias, sums, u_body, u_rim, act, grad_body, grad_rim):
+def activate(taps, wide, p, bias, u_body, u_rim, act, grad_body, grad_rim):
     size_y = taps.shape[2] - 2 * PAD
     spans = [(PAD - RIM, RIM)]
     spans += [(PAD + y, CHUNK) for y in range(0, size_y, CHUNK)]
@@ -147,10 +147,13 @@
         if body:
             act[y : y + rows, :] = (preact * sigma).astype(BF16)
             grad_body[y : y + rows, :] = rounded
-            sums = sums + jnp.sum(exact.reshape(rows // 8, 8, exact.shape[1]), axis=0)
         else:
             grad_rim[y : y + rows, :] = rounded
-    return sums
+
+
+def body_sum(wide, p):
+    size_y, width = wide.shape[1] - 2 * PAD, wide.shape[2]
+    return jnp.sum(wide[p, PAD : PAD + size_y, :].reshape(size_y // 8, 8, width), axis=0)
 
 
 def shifted_grads(wide, p):
@@ -345,8 +348,8 @@
                 wide[q, PAD + y : PAD + y + CHUNK, :] = exact
                 act[q, y : y + CHUNK, :] = value.astype(BF16)
                 grad_ref[q, y : y + CHUNK, :] = rounded
-                sums = sums + jnp.sum(exact.reshape(CHUNK // 8, 8, width), axis=0)
         grads = [shifted_grads(wide, q) for q in (p, p + 1)]
+        sums = sums + body_sum(wide, p) + body_sum(wide, p + 1)
         if p < inner - 2:
             term = outer([[turned[q + j] for j in range(3)] for q in (p, p + 1)], grads)
             if p == 0:
@@ -447,16 +450,16 @@
     rim_taps(taps, (0, 1), rims, weights)
     for p in range(2):
         plane_taps(taps, (p,), bodies[p], weights)
-    sums = sums_ref[...]
     outs = (first_ref, last_ref)
     places = (0, size_x - 1)
     for p in range(2):
         x = places[p]
-        sums = activate(
-            taps, wide, p, bias, sums, u_ref.at[x], u_rim.at[x], act.at[p],
+        activate(
+            taps, wide, p, bias, u_ref.at[x], u_rim.at[x], act.at[p],
             outs[p].at[pl.ds(0, size_y)], outs[p].at[pl.ds(size_y, 2 * RIM)],
         )
     acc[...] = acc_ref[...] + outer_turned(bodies, [shifted_grads(wide, p) for p in range(2)])
+    sums = sums_ref[...] + body_sum(wide, 0) + body_sum(wide, 1)
 
     def hand(last, first):
         if last is not None:

time: 31.1 us -> 31.1 us (level)
  transfers between devices with their start and end apart: 11 -> 11, of which waited for: 7 -> 7; matrix products, arithmetic and copies ran while one was open for 0% -> 0% of each run, Pallas kernels for 35% -> 34%
where the time goes in v7:
time: 31.1 us; the launch traced here: 30.9 us
  starting transfers between devices  13.2 us (42%)
  Pallas kernels  12.5 us (40%)
  waiting for transfers between devices  3.54 us (11%)
  local copies, waits for them, and re-layouts  0.87 us (3%)
  between operations  0.79 us (3%)
    ppermute x7, starting transfers between devices, swap(): return lax.ppermute(value, axis, links)  6.99 us
    ppermute x4, starting transfers between devices, exchange(): lax.ppermute(value, axes, [(i, i ^ flip) for i in range(math.prod(sizes))])  6.17 us
    pallas_call x3, Pallas kernels, back(): pl.pallas_call(lambda *refs: back_kernel(pairs, edges, stored, *refs), ou...  4.74 us
    pallas_call x1, Pallas kernels, local(): pl.pallas_call(inner_kernel, out_shape=(shape(inner, size_y, width), shap...  2.37 us
    pallas_call x1, Pallas kernels, local(): pl.pallas_call(front_kernel, out_shape=(shape(inner, size_y, width, dtype...  2.12 us
    ppermute x7, waiting for transfers between devices, swap(): return lax.ppermute(value, axis, links)  2.02 us
    ppermute x4, waiting for transfers between devices, exchange(): lax.ppermute(value, axes, [(i, i ^ flip) for i in range(math.prod(sizes))])  1.51 us
    pallas_call x1, Pallas kernels, local(): pl.pallas_call(edge_kernel, out_shape=(shape(2, size_y, width), shape(tal...  1.07 us
  transfers between devices with their start and end apart: 11, of which 7 were waited for; matrix products, arithmetic and copies ran while one was open for 0% of the time, Pallas kernels for 34%

profile of v7, /device:TPU:0, one launch (start us, length us, event | category | flops | bytes accessed | tf_op | source)
XLA Modules:
  0.0 30.9 jit_solution(6509062419081399952)
XLA Ops:
  0.6 0.8 %fusion = (bf16[16,2,128]{2,1,0:T(2,128)(2,1)S(1)}, bf16[16,2,128]{2,1,0:T(2,128)(2,1)S(1)}, bf16[16,2,128]{2,1,0:T(2,128)(2,1)S(1)}, bf16[16,2,128]{2,1,0:T(2,128)(2,1)S(1)}) fusion(bf16[16,256,128]{2,1,0:T(8,128)(2,1)} %bitcast.9, bf16[16,256,128]{2,1,0:T(8,128)(2,1)} %bitcast.16), kind=kLoop, calls=%fused_computation.1 | loop fusion | bytes 65536 | tf_op jit(solution)/shard_map/slice | solution.py:622
  1.5 0.0 copy-start
  1.5 0.0 copy-start.2
  1.6 0.0 copy-start.4
  1.6 0.5 %collective-permute-start = (bf16[16,4,128]{2,1,0:T(4,128)(2,1)S(1)}, bf16[16,4,128]{2,1,0:T(4,128)(2,1)S(1)}, u32[]{:S(2)}, u32[]{:S(2)}) collective-permute-start(bf16[16,4,128]{2,1,0:T(4,128)(2,1)S(1)} %get-tuple-element.43), channel_id=1, source_target_pairs={{0,4},{4,0},{8,12},{12,8},{1,5},{5,1},{9,13},{13,9},{2,6},{6,2},{1... | collective-permute-start | bytes 49160 | tf_op jit(solution)/shard_map/ppermute | solution.py:27
  2.1 0.0 copy-start.1
  2.1 2.6 %collective-permute-start.1 = (bf16[16,4,128]{2,1,0:T(4,128)(2,1)S(1)}, bf16[16,4,128]{2,1,0:T(4,128)(2,1)S(1)}, u32[]{:S(2)}, u32[]{:S(2)}) collective-permute-start(bf16[16,4,128]{2,1,0:T(4,128)(2,1)S(1)} %get-tuple-element.44), channel_id=1, source_target_pairs={{4,8},{8,4},{12,0},{0,12},{5,9},{9,5},{13,1},{1,13},{6,10},{10,6},... | collective-permute-start | bytes 49160 | tf_op jit(solution)/shard_map/ppermute | solution.py:27
  4.8 0.0 copy-done
  4.8 0.0 copy-done.2
  4.8 0.0 copy-done.4
  4.8 2.1 %front_planes.1 = (f32[14,256,128]{2,1,0:T(8,128)S(1)}, bf16[16,128,256]{2,1,0:T(8,128)(2,1)S(1)}, bf16[384,384]{1,0:T(8,128)(2,1)S(1)}, f32[1,128]{1,0:T(1,128)S(1)}) custom-call(bf16[16,256,128]{2,1,0:T(8,128)(2,1)S(1)} %bitcast.10, bf16[3,3,3,64,64]{4,3,2,1,0:T(8,128)(2,1)S(1)} %copy-done.2, f32[64]{0:T(128)S(1)} %copy-done.4), custom_call_target="tpu_custom_call" | custom-call | flops 2200000000 | tf_op jit(solution)/shard_map/front_planes/pallas_call | solution.py:652
  6.9 0.0 collective-permute-done.y_near
  6.9 0.0 collective-permute-done.1.y_far
  7.0 1.6 %collective-permute-start.2 = (bf16[272,128]{1,0:T(8,128)(2,1)S(1)}, bf16[272,128]{1,0:T(8,128)(2,1)S(1)}, u32[]{:S(2)}, u32[]{:S(2)}) collective-permute-start(bf16[272,128]{1,0:T(8,128)(2,1)S(1)} %pack_planes.1), channel_id=1, source_target_pairs={{0,16},{16,0},{1,17},{17,1},{2,18},{18,2},{3,19},{19,3},{4,20},{20... | collective-permute-start | bytes 208904 | tf_op jit(solution)/shard_map/ppermute | solution.py:27
  8.5 0.0 copy-done.1
  8.5 2.4 %inner_planes.1 = (bf16[14,256,128]{2,1,0:T(8,128)(2,1)S(1)}, bf16[14,256,128]{2,1,0:T(8,128)(2,1)S(1)}, bf16[14,16,128]{2,1,0:T(8,128)(2,1)S(1)}, f32[384,384]{1,0:T(8,128)S(1)}, f32[8,128]{1,0:T(8,128)S(1)}) custom-call(bf16[16,256,128]{2,1,0:T(8,128)(2,1)S(1)} %bitcast.12, bf16[16,256,128]{2,1,0:T(8,128)(2,1)S(1)} %bitcast.17, ...), custom_call_target="tpu_custom_call" | custom-call | flops 3300000000 | tf_op jit(solution)/shard_map/inner_planes/pallas_call | solution.py:688
  10.9 0.4 %collective-permute-done.2.x_near.x_far = bf16[272,128]{1,0:T(8,128)(2,1)S(1)} collective-permute-done((bf16[272,128]{1,0:T(8,128)(2,1)S(1)}, bf16[272,128]{1,0:T(8,128)(2,1)S(1)}, u32[]{:S(2)}, u32[]{:S(2)}) %collective-permute-start.2) | collective-permute-done | bytes 69664 | tf_op jit(solution)/shard_map/ppermute | solution.py:27
  11.4 1.1 %edge_planes.1 = (bf16[2,256,128]{2,1,0:T(8,128)(2,1)S(1)}, bf16[272,128]{1,0:T(8,128)(2,1)S(1)}, bf16[272,128]{1,0:T(8,128)(2,1)S(1)}, f32[384,384]{1,0:T(8,128...) custom-call(bf16[16,256,128]{2,1,0:T(8,128)(2,1)S(1)} %bitcast.13, ...), custom_call_target="tpu_custom_call" | custom-call | flops 2200000000 | tf_op jit(solution)/shard_map/edge_planes/pallas_call | solution.py:709
  12.4 0.0 copy-start.3
  12.4 0.1 collective-permute-start.3
  12.5 0.3 %rest_of_sums.1 = (f32[2,7,16,128]{3,2,1,0:T(8,128)S(1)}, f32[2,7,16,128]{3,2,1,0:T(8,128)S(1)}, f32[2,7,16,128]{3,2,1,0:T(8,128)S(1)}) custom-call(f32[384,384]{1,0:T(8,128)S(1)} %get-tuple-element.56.acc, f32[8,128]{1,0:T(8,128)S(1)} %get-tuple-element.57.sums), custom_call_target="tpu_custom_call" | custom-call | flops 770000000 | tf_op jit(solution)/shard_map/rest_of_sums/pallas_call | solution.py:793
  12.8 0.5 %collective-permute-start.5 = (f32[2,7,16,128]{3,2,1,0:T(8,128)S(1)}, f32[2,7,16,128]{3,2,1,0:T(8,128)S(1)}, u32[]{:S(2)}, u32[]{:S(2)}) collective-permute-start(f32[2,7,16,128]{3,2,1,0:T(8,128)S(1)} %get-tuple-element.68), channel_id=1, source_target_pairs={{0,4},{4,0},{8,12},{12,8},{1,5},{5,1},{9,13},{13,9},{2,6},{6,2},{1... | collective-permute-start | bytes 344072 | tf_op jit(solution)/shard_map/ppermute | solution.py:27
  13.3 0.5 %collective-permute-done.3.refs_1_ = f32[2,7,16,128]{3,2,1,0:T(8,128)S(1)} collective-permute-done((f32[2,7,16,128]{3,2,1,0:T(8,128)S(1)}, f32[2,7,16,128]{3,2,1,0:T(8,128)S(1)}, u32[]{:S(2)}, u32[]{:S(2)}) %collective-permute-start.3) | collective-permute-done | bytes 114720 | tf_op jit(solution)/shard_map/ppermute | solution.py:27
  13.8 1.4 %collective-permute-start.4 = (bf16[2,7,16,128]{3,2,1,0:T(8,128)(2,1)S(1)}, bf16[2,7,16,128]{3,2,1,0:T(8,128)(2,1)S(1)}, u32[]{:S(2)}, u32[]{:S(2)}) collective-permute-start(bf16[2,7,16,128]{3,2,1,0:T(8,128)(2,1)S(1)} %add_sums.4.refs_5_), channel_id=1, source_target_pairs={{0,5},{1,4},{2,7},{3,6},{4,1},{5,0},{6,3},{7,2},{8,13},{9,12},{10,... | collective-permute-start | bytes 172040 | tf_op jit(solution)/shard_map/ppermute | solution.py:35
  15.2 0.0 copy-done.3
  15.2 1.0 %back_weights.1 = (bf16[512,768]{1,0:T(8,128)(2,1)S(1)}, f32[14,8,128]{2,1,0:T(8,128)S(1)}) custom-call(bf16[3,3,3,64,64]{4,3,2,1,0:T(8,128)(2,1)S(1)} %copy-done.2, s32[3,3,3]{2,1,0:T(4,128)S(1)} %copy-done.3), custom_call_target="tpu_custom_call" | custom-call | flops 1100000000 | tf_op jit(solution)/shard_map/back_weights/pallas_call | solution.py:641
  16.2 1.4 %input_grad.3.refs_7_ = bf16[16,256,128]{2,1,0:T(8,128)(2,1)} custom-call(bf16[14,256,128]{2,1,0:T(8,128)(2,1)S(1)} %get-tuple-element.49.refs_0_, bf16[14,16,128]{2,1,0:T(8,128)(2,1)S(1)} %get-tuple-element.50.refs_1_, bf16[272,128]{1,0:T(8,128)(2,1)S(1)} %get-tuple-element.53.refs_2_, bf16[272,128]{1,0:T(8,128)(2,1)S(1)} %get-tuple-element.54.refs_3_, ...), custom_call_target="tpu_custom_call" | custom-call | flops 1100000000 | tf_op jit(solution)/shard_map/input_grad/pallas_call | solution.py:746
  17.6 0.2 collective-permute-done.4.refs_2_
  17.8 0.0 collective-permute-done.5.refs_1_
  17.8 2.4 %collective-permute-start.6 = (bf16[1,7,16,128]{3,2,1,0:T(8,128)(2,1)S(1)}, bf16[1,7,16,128]{3,2,1,0:T(8,128)(2,1)S(1)}, u32[]{:S(2)}, u32[]{:S(2)}) collective-permute-start(bf16[1,7,16,128]{3,2,1,0:T(8,128)(2,1)S(1)} %get-tuple-element.71), channel_id=1, source_target_pairs={{0,6},{1,7},{2,4},{3,5},{4,2},{5,3},{6,0},{7,1},{8,14},{9,15},{10,... | collective-permute-start | bytes 86024 | tf_op jit(solution)/shard_map/ppermute | solution.py:35
  20.2 1.5 %collective-permute-start.9 = (bf16[272,128]{1,0:T(8,128)(2,1)S(1)}, bf16[272,128]{1,0:T(8,128)(2,1)S(1)}, u32[]{:S(2)}, u32[]{:S(2)}) collective-permute-start(bf16[272,128]{1,0:T(8,128)(2,1)S(1)} %get-tuple-element.75), channel_id=1, source_target_pairs={{0,16},{16,0},{1,17},{17,1},{2,18},{18,2},{3,19},{19,3},{4,20},{20... | collective-permute-start | bytes 208904 | tf_op jit(solution)/shard_map/ppermute | solution.py:27
  21.7 0.3 %collective-permute-done.6.refs_1_ = bf16[1,7,16,128]{3,2,1,0:T(8,128)(2,1)S(1)} collective-permute-done((bf16[1,7,16,128]{3,2,1,0:T(8,128)(2,1)S(1)}, bf16[1,7,16,128]{3,2,1,0:T(8,128)(2,1)S(1)}, u32[]{:S(2)}, u32[]{:S(2)}) %collective-permute-start.6) | collective-permute-done | bytes 28704 | tf_op jit(solution)/shard_map/ppermute | solution.py:35
  22.1 1.0 %collective-permute-start.7 = (bf16[1,7,16,128]{3,2,1,0:T(8,128)(2,1)S(1)}, bf16[1,7,16,128]{3,2,1,0:T(8,128)(2,1)S(1)}, u32[]{:S(2)}, u32[]{:S(2)}) collective-permute-start(bf16[1,7,16,128]{3,2,1,0:T(8,128)(2,1)S(1)} %add_sums.5.refs_8_.refs_0_), channel_id=1, source_target_pairs={{0,12},{1,13},{2,14},{3,15},{4,8},{5,9},{6,10},{7,11},{8,4},{9,5},... | collective-permute-start | bytes 86024 | tf_op jit(solution)/shard_map/ppermute | solution.py:35
  23.1 1.7 %input_grad.4 = (bf16[16,256,128]{2,1,0:T(8,128)(2,1)}, bf16[16,256,128]{2,1,0:T(8,128)(2,1)}) custom-call(bf16[14,256,128]{2,1,0:T(8,128)(2,1)S(1)} %get-tuple-element.49.refs_0_, bf16[14,16,128]{2,1,0:T(8,128)(2,1)S(1)} %get-tuple-element.50.refs_1_, bf16[272,128]{1,0:T(8,128)(2,1)S(1)} %get-tuple-element.53.refs_2_, ...), custom_call_target="tpu_custom_call", output_to_operand_aliasing={{0}: (7, {})} | custom-call | flops 2750000128 | tf_op jit(solution)/shard_map/input_grad/pallas_call | solution.py:746
  24.8 0.7 %collective-permute-done.7.refs_1_ = bf16[1,7,16,128]{3,2,1,0:T(8,128)(2,1)S(1)} collective-permute-done((bf16[1,7,16,128]{3,2,1,0:T(8,128)(2,1)S(1)}, bf16[1,7,16,128]{3,2,1,0:T(8,128)(2,1)S(1)}, u32[]{:S(2)}, u32[]{:S(2)}) %collective-permute-start.7) | collective-permute-done | bytes 28704 | tf_op jit(solution)/shard_map/ppermute | solution.py:35
  25.5 1.3 %collective-permute-start.8 = (bf16[1,7,16,128]{3,2,1,0:T(8,128)(2,1)S(1)}, bf16[1,7,16,128]{3,2,1,0:T(8,128)(2,1)S(1)}, u32[]{:S(2)}, u32[]{:S(2)}) collective-permute-start(bf16[1,7,16,128]{3,2,1,0:T(8,128)(2,1)S(1)} %add_sums.6.refs_8_.refs_0_), channel_id=1, source_target_pairs={{0,20},{1,21},{2,22},{3,23},{4,16},{5,17},{6,18},{7,19},{8,28},{9,... | collective-permute-start | bytes 86024 | tf_op jit(solution)/shard_map/ppermute | solution.py:35
  26.8 0.0 collective-permute-done.9.refs_4_.refs_5_
  26.8 1.7 %input_grad.5 = bf16[16,256,128]{2,1,0:T(8,128)(2,1)} custom-call(bf16[14,256,128]{2,1,0:T(8,128)(2,1)S(1)} %get-tuple-element.49.refs_0_, bf16[14,16,128]{2,1,0:T(8,128)(2,1)S(1)} %get-tuple-element.50.refs_1_, bf16[272,128]{1,0:T(8,128)(2,1)S(1)} %get-tuple-element.53.refs_2_, ...), custom_call_target="tpu_custom_call", output_to_operand_aliasing={{}: (7, {})} | custom-call | flops 2750000128 | tf_op jit(solution)/shard_map/input_grad/pallas_call | solution.py:746
  28.5 0.3 %collective-permute-done.8.refs_1_ = bf16[1,7,16,128]{3,2,1,0:T(8,128)(2,1)S(1)} collective-permute-done((bf16[1,7,16,128]{3,2,1,0:T(8,128)(2,1)S(1)}, bf16[1,7,16,128]{3,2,1,0:T(8,128)(2,1)S(1)}, u32[]{:S(2)}, u32[]{:S(2)}) %collective-permute-start.8) | collective-permute-done | bytes 28704 | tf_op jit(solution)/shard_map/ppermute | solution.py:35
  28.8 0.2 collective-permute-start.10
  29.1 1.1 %collective-permute-done.10.other = f32[7,16,128]{2,1,0:T(8,128)S(1)} collective-permute-done((f32[7,16,128]{2,1,0:T(8,128)S(1)}, f32[7,16,128]{2,1,0:T(8,128)S(1)}, u32[]{:S(2)}, u32[]{:S(2)}) %collective-permute-start.10) | collective-permute-done | bytes 57376 | tf_op jit(solution)/shard_map/ppermute | solution.py:27
  30.1 0.7 %scale_weight_grad.1 = (bf16[27,16,64]{2,1,0:T(8,128)(2,1)}, f32[1,16]{1,0:T(1,128)}) custom-call(f32[7,16,128]{2,1,0:T(8,128)S(1)} %bitcast.15, f32[7,16,128]{2,1,0:T(8,128)S(1)} %collective-permute-done.10.other, f32[14,8,128]{2,1,0:T(8,128)S(1)} %get-tuple-element.79.scale_ref), custom_call_target="tpu_custom_call" | custom-call | tf_op jit(solution)/shard_map/scale_weight_grad/pallas_call | solution.py:835
  (8 shorter events, 0.2 us)
Async XLA Ops:
  1.5 3.2 %copy-start = (bf16[1,16,256,128]{3,2,1,0:T(8,128)(2,1)S(1)}, bf16[1,16,256,128]{3,2,1,0:T(8,128)(2,1)}, u32[]{:S(2)}) copy-start(bf16[1,16,256,128]{3,2,1,0:T(8,128)(2,1)} %param.5) | copy-start | bytes 3145732
  1.5 3.2 %copy-start.2 = (bf16[3,3,3,64,64]{4,3,2,1,0:T(8,128)(2,1)S(1)}, bf16[3,3,3,64,64]{4,3,2,1,0:T(8,128)(2,1)}, u32[]{:S(2)}) copy-start(bf16[3,3,3,64,64]{4,3,2,1,0:T(8,128)(2,1)} %refs_0_) | copy-start | bytes 663556
  1.6 3.2 %copy-start.4 = (f32[64]{0:T(128)S(1)}, f32[64]{0:T(128)}, u32[]{:S(2)}) copy-start(f32[64]{0:T(128)} %offsets.1) | copy-start | bytes 772
  1.6 5.3 %collective-permute-start = (bf16[16,4,128]{2,1,0:T(4,128)(2,1)S(1)}, bf16[16,4,128]{2,1,0:T(4,128)(2,1)S(1)}, u32[]{:S(2)}, u32[]{:S(2)}) collective-permute-start(bf16[16,4,128]{2,1,0:T(4,128)(2,1)S(1)} %get-tuple-element.43), channel_id=1, source_target_pairs={{0,4},{4,0},{8,12},{12,8},{1,5},{5,1},{9,13},{13,9},{2,6},{6,2},{1... | collective-permute-start | bytes 49160 | tf_op jit(solution)/shard_map/ppermute | solution.py:27
  2.1 6.4 %copy-start.1 = (bf16[1,16,256,128]{3,2,1,0:T(8,128)(2,1)S(1)}, bf16[1,16,256,128]{3,2,1,0:T(8,128)(2,1)}, u32[]{:S(2)}) copy-start(bf16[1,16,256,128]{3,2,1,0:T(8,128)(2,1)} %param.8) | copy-start | bytes 3145732
  2.1 4.8 %collective-permute-start.1 = (bf16[16,4,128]{2,1,0:T(4,128)(2,1)S(1)}, bf16[16,4,128]{2,1,0:T(4,128)(2,1)S(1)}, u32[]{:S(2)}, u32[]{:S(2)}) collective-permute-start(bf16[16,4,128]{2,1,0:T(4,128)(2,1)S(1)} %get-tuple-element.44), channel_id=1, source_target_pairs={{4,8},{8,4},{12,0},{0,12},{5,9},{9,5},{13,1},{1,13},{6,10},{10,6},... | collective-permute-start | bytes 49160 | tf_op jit(solution)/shard_map/ppermute | solution.py:27
  7.0 4.4 %collective-permute-start.2 = (bf16[272,128]{1,0:T(8,128)(2,1)S(1)}, bf16[272,128]{1,0:T(8,128)(2,1)S(1)}, u32[]{:S(2)}, u32[]{:S(2)}) collective-permute-start(bf16[272,128]{1,0:T(8,128)(2,1)S(1)} %pack_planes.1), channel_id=1, source_target_pairs={{0,16},{16,0},{1,17},{17,1},{2,18},{18,2},{3,19},{19,3},{4,20},{20... | collective-permute-start | bytes 208904 | tf_op jit(solution)/shard_map/ppermute | solution.py:27
  12.4 2.8 %copy-start.3 = (s32[3,3,3]{2,1,0:T(4,128)S(1)}, s32[3,3,3]{2,1,0:T(4,128)}, u32[]{:S(2)}) copy-start(s32[3,3,3]{2,1,0:T(4,128)} %refs_1_.1) | copy-start | bytes 328
  12.4 1.4 %collective-permute-start.3 = (f32[2,7,16,128]{3,2,1,0:T(8,128)S(1)}, f32[2,7,16,128]{3,2,1,0:T(8,128)S(1)}, u32[]{:S(2)}, u32[]{:S(2)}) collective-permute-start(f32[2,7,16,128]{3,2,1,0:T(8,128)S(1)} %get-tuple-element.59), channel_id=1, source_target_pairs={{0,4},{4,0},{8,12},{12,8},{1,5},{5,1},{9,13},{13,9},{2,6},{6,2},{1... | collective-permute-start | bytes 344072 | tf_op jit(solution)/shard_map/ppermute | solution.py:27
  12.8 5.0 %collective-permute-start.5 = (f32[2,7,16,128]{3,2,1,0:T(8,128)S(1)}, f32[2,7,16,128]{3,2,1,0:T(8,128)S(1)}, u32[]{:S(2)}, u32[]{:S(2)}) collective-permute-start(f32[2,7,16,128]{3,2,1,0:T(8,128)S(1)} %get-tuple-element.68), channel_id=1, source_target_pairs={{0,4},{4,0},{8,12},{12,8},{1,5},{5,1},{9,13},{13,9},{2,6},{6,2},{1... | collective-permute-start | bytes 344072 | tf_op jit(solution)/shard_map/ppermute | solution.py:27
  13.8 3.9 %collective-permute-start.4 = (bf16[2,7,16,128]{3,2,1,0:T(8,128)(2,1)S(1)}, bf16[2,7,16,128]{3,2,1,0:T(8,128)(2,1)S(1)}, u32[]{:S(2)}, u32[]{:S(2)}) collective-permute-start(bf16[2,7,16,128]{3,2,1,0:T(8,128)(2,1)S(1)} %add_sums.4.refs_5_), channel_id=1, source_target_pairs={{0,5},{1,4},{2,7},{3,6},{4,1},{5,0},{6,3},{7,2},{8,13},{9,12},{10,... | collective-permute-start | bytes 172040 | tf_op jit(solution)/shard_map/ppermute | solution.py:35
  17.8 4.3 %collective-permute-start.6 = (bf16[1,7,16,128]{3,2,1,0:T(8,128)(2,1)S(1)}, bf16[1,7,16,128]{3,2,1,0:T(8,128)(2,1)S(1)}, u32[]{:S(2)}, u32[]{:S(2)}) collective-permute-start(bf16[1,7,16,128]{3,2,1,0:T(8,128)(2,1)S(1)} %get-tuple-element.71), channel_id=1, source_target_pairs={{0,6},{1,7},{2,4},{3,5},{4,2},{5,3},{6,0},{7,1},{8,14},{9,15},{10,... | collective-permute-start | bytes 86024 | tf_op jit(solution)/shard_map/ppermute | solution.py:35
  20.2 6.6 %collective-permute-start.9 = (bf16[272,128]{1,0:T(8,128)(2,1)S(1)}, bf16[272,128]{1,0:T(8,128)(2,1)S(1)}, u32[]{:S(2)}, u32[]{:S(2)}) collective-permute-start(bf16[272,128]{1,0:T(8,128)(2,1)S(1)} %get-tuple-element.75), channel_id=1, source_target_pairs={{0,16},{16,0},{1,17},{17,1},{2,18},{18,2},{3,19},{19,3},{4,20},{20... | collective-permute-start | bytes 208904 | tf_op jit(solution)/shard_map/ppermute | solution.py:27
  22.1 3.4 %collective-permute-start.7 = (bf16[1,7,16,128]{3,2,1,0:T(8,128)(2,1)S(1)}, bf16[1,7,16,128]{3,2,1,0:T(8,128)(2,1)S(1)}, u32[]{:S(2)}, u32[]{:S(2)}) collective-permute-start(bf16[1,7,16,128]{3,2,1,0:T(8,128)(2,1)S(1)} %add_sums.5.refs_8_.refs_0_), channel_id=1, source_target_pairs={{0,12},{1,13},{2,14},{3,15},{4,8},{5,9},{6,10},{7,11},{8,4},{9,5},... | collective-permute-start | bytes 86024 | tf_op jit(solution)/shard_map/ppermute | solution.py:35
  25.5 3.4 %collective-permute-start.8 = (bf16[1,7,16,128]{3,2,1,0:T(8,128)(2,1)S(1)}, bf16[1,7,16,128]{3,2,1,0:T(8,128)(2,1)S(1)}, u32[]{:S(2)}, u32[]{:S(2)}) collective-permute-start(bf16[1,7,16,128]{3,2,1,0:T(8,128)(2,1)S(1)} %add_sums.6.refs_8_.refs_0_), channel_id=1, source_target_pairs={{0,20},{1,21},{2,22},{3,23},{4,16},{5,17},{6,18},{7,19},{8,28},{9,... | collective-permute-start | bytes 86024 | tf_op jit(solution)/shard_map/ppermute | solution.py:35
  28.8 1.3 %collective-permute-start.10 = (f32[7,16,128]{2,1,0:T(8,128)S(1)}, f32[7,16,128]{2,1,0:T(8,128)S(1)}, u32[]{:S(2)}, u32[]{:S(2)}) collective-permute-start(f32[7,16,128]{2,1,0:T(8,128)S(1)} %bitcast.14), channel_id=1, source_target_pairs={{0,4},{4,0},{8,12},{12,8},{1,5},{5,1},{9,13},{13,9},{2,6},{6,2},{1... | collective-permute-start | bytes 172040 | tf_op jit(solution)/shard_map/ppermute | solution.py:27

commit v8 on v7

--- a/solution.py
+++ b/solution.py
@@ -296,7 +296,7 @@
 
 def inner_kernel(
     f_ref, u_ref, y_near, y_far, pre_ref, turned, w_ref, bias_ref,
-    act, grad_ref, rim_ref, acc_ref, sums_ref,
+    act, grad_ref, rim_ref, acc_ref, sums_ref, part_ref,
     f_rim, u_rim, wide, acc,
 ):
     size_x, size_y, width = f_ref.shape
@@ -306,6 +306,12 @@
     place_rims(y_near, y_far, f_rim, u_rim, gap)
     f_rim[:, gap + THIN : RIM, :] = f_ref[:, :THIN, :]
     f_rim[:, RIM : RIM + THIN, :] = f_ref[:, size_y - THIN :, :]
+    for p, (x, row) in enumerate(((0, width), (size_x - 2, 0))):
+        part_ref[p] = jnp.dot(
+            jnp.concatenate([f_ref[x], f_ref[x + 1]], axis=1),
+            w_ref[row : row + 2 * width, :],
+            preferred_element_type=F32,
+        )
     bias = bias_ref[...]
     rows = 2 * RIM
     tall = [
@@ -401,7 +407,7 @@
             for k in range(blocks):
                 for out, d in ((away, 2 * k + 1 - bit), (stay, 2 * k + bit)):
                     if out is not None:
-                        out[k, s] = value[d * share : (d + 1) * share]
+                        out[k, s] = value[d * share : (d + 1) * share].astype(out.dtype)
 
         @pl.when(which == 0)
         def _():
@@ -428,7 +434,7 @@
 
 def edge_kernel(
     f_ref, u_ref, y_near, y_far, x_near, x_far, w_ref, bias_ref, acc_ref, sums_ref,
-    act, first_ref, last_ref, acc, bias_sums, send_ref, near_ref, *refs
+    part_ref, act, first_ref, last_ref, acc, bias_sums, send_ref, near_ref, *refs
 ):
     far_ref = refs[0] if len(refs) > 5 else None
     f_rim, u_rim, around, taps, wide = refs[-5:]
@@ -449,7 +455,12 @@
     ]
     rim_taps(taps, (0, 1), rims, weights)
     for p in range(2):
-        plane_taps(taps, (p,), bodies[p], weights)
+        row = 2 * p * width
+        result = part_ref[p] + jnp.dot(
+            around[p, :size_y], weights[row : row + width], preferred_element_type=F32
+        )
+        for b in range(3):
+            taps[b, p, PAD : PAD + size_y, :] = result[:, b * width : (b + 1) * width]
     outs = (first_ref, last_ref)
     places = (0, size_x - 1)
     for p in range(2):
@@ -685,7 +696,7 @@
         pltpu.VMEM((size_x, 2 * RIM, width), BF16),
         pltpu.VMEM((size_x, 2 * RIM, width), BF16),
     ]
-    act_inner, grad, grad_rim, acc, sums = pl.pallas_call(
+    act_inner, grad, grad_rim, acc, sums, part = pl.pallas_call(
         inner_kernel,
         out_shape=(
             shape(inner, size_y, width),
@@ -693,9 +704,10 @@
             shape(inner, 2 * RIM, width),
             shape(3 * width, 3 * width, dtype=F32),
             shape(8, width, dtype=F32),
+            shape(2, size_y, 3 * width, dtype=F32),
         ),
         in_specs=[VMEM] * 8,
-        out_specs=(VMEM,) * 5,
+        out_specs=(VMEM,) * 6,
         scratch_shapes=rims + [
             pltpu.VMEM((inner, rows, width), F32),
             pltpu.VMEM((3 * width, 3 * width), F32),
@@ -714,10 +726,10 @@
             shape(tall, width),
             shape(3 * width, 3 * width, dtype=F32),
             shape(8, width, dtype=F32),
-            shape(*blocks, dtype=F32),
+            shape(*blocks),
         )
         + (shape(tall, width),) * (1 + many),
-        in_specs=[VMEM] * 10,
+        in_specs=[VMEM] * 11,
         out_specs=(VMEM,) * (7 + many),
         scratch_shapes=rims + [
             pltpu.VMEM((2, tall, width), BF16),
@@ -728,7 +740,7 @@
         cost_estimate=cost(2.0),
         name="edge_planes",
     )(
-        cells, cotangent, y_near, y_far, x_near, x_far, forward_weights, bias, acc, sums,
+        cells, cotangent, y_near, y_far, x_near, x_far, forward_weights, bias, acc, sums, part,
     )
 
     def back(pairs, previous, after, beyond=(), acts=()):

time: 31.1 us -> 30.9 us (level)
  transfers between devices with their start and end apart: 11 -> 11, of which waited for: 7 -> 7; matrix products, arithmetic and copies ran while one was open for 0% -> 0% of each run, Pallas kernels for 34% -> 35%
where the time goes in v8:
time: 30.9 us; the launch traced here: 30.7 us
  starting transfers between devices  13.2 us (43%)
  Pallas kernels  12.5 us (40%)
  waiting for transfers between devices  3.33 us (11%)
  local copies, waits for them, and re-layouts  0.87 us (3%)
  between operations  0.79 us (3%)
    ppermute x7, starting transfers between devices, swap(): return lax.ppermute(value, axis, links)  6.99 us
    ppermute x4, starting transfers between devices, exchange(): lax.ppermute(value, axes, [(i, i ^ flip) for i in range(math.prod(sizes))])  6.2 us
    pallas_call x3, Pallas kernels, back(): pl.pallas_call(lambda *refs: back_kernel(pairs, edges, stored, *refs), ou...  4.74 us
    pallas_call x1, Pallas kernels, local(): pl.pallas_call(inner_kernel, out_shape=(shape(inner, size_y, width), shap...  2.45 us
    pallas_call x1, Pallas kernels, local(): pl.pallas_call(front_kernel, out_shape=(shape(inner, size_y, width, dtype...  2.12 us
    ppermute x7, waiting for transfers between devices, swap(): return lax.ppermute(value, axis, links)  1.85 us
    ppermute x4, waiting for transfers between devices, exchange(): lax.ppermute(value, axes, [(i, i ^ flip) for i in range(math.prod(sizes))])  1.48 us
    pallas_call x1, Pallas kernels, local(): pl.pallas_call(edge_kernel, out_shape=(shape(2, size_y, width), shape(tal...  1.01 us
  transfers between devices with their start and end apart: 11, of which 7 were waited for; matrix products, arithmetic and copies ran while one was open for 0% of the time, Pallas kernels for 35%

profile of v8, /device:TPU:0, one launch (start us, length us, event | category | flops | bytes accessed | tf_op | source)
XLA Modules:
  0.0 30.7 jit_solution(14543824591665410366)
XLA Ops:
  0.6 0.8 %fusion = (bf16[16,2,128]{2,1,0:T(2,128)(2,1)S(1)}, bf16[16,2,128]{2,1,0:T(2,128)(2,1)S(1)}, bf16[16,2,128]{2,1,0:T(2,128)(2,1)S(1)}, bf16[16,2,128]{2,1,0:T(2,128)(2,1)S(1)}) fusion(bf16[16,256,128]{2,1,0:T(8,128)(2,1)} %bitcast.9, bf16[16,256,128]{2,1,0:T(8,128)(2,1)} %bitcast.16), kind=kLoop, calls=%fused_computation.1 | loop fusion | bytes 65536 | tf_op jit(solution)/shard_map/slice | solution.py:633
  1.5 0.0 copy-start
  1.5 0.0 copy-start.2
  1.6 0.0 copy-start.4
  1.6 0.5 %collective-permute-start = (bf16[16,4,128]{2,1,0:T(4,128)(2,1)S(1)}, bf16[16,4,128]{2,1,0:T(4,128)(2,1)S(1)}, u32[]{:S(2)}, u32[]{:S(2)}) collective-permute-start(bf16[16,4,128]{2,1,0:T(4,128)(2,1)S(1)} %get-tuple-element.44), channel_id=1, source_target_pairs={{0,4},{4,0},{8,12},{12,8},{1,5},{5,1},{9,13},{13,9},{2,6},{6,2},{1... | collective-permute-start | bytes 49160 | tf_op jit(solution)/shard_map/ppermute | solution.py:27
  2.1 0.0 copy-start.1
  2.1 2.6 %collective-permute-start.1 = (bf16[16,4,128]{2,1,0:T(4,128)(2,1)S(1)}, bf16[16,4,128]{2,1,0:T(4,128)(2,1)S(1)}, u32[]{:S(2)}, u32[]{:S(2)}) collective-permute-start(bf16[16,4,128]{2,1,0:T(4,128)(2,1)S(1)} %get-tuple-element.45), channel_id=1, source_target_pairs={{4,8},{8,4},{12,0},{0,12},{5,9},{9,5},{13,1},{1,13},{6,10},{10,6},... | collective-permute-start | bytes 49160 | tf_op jit(solution)/shard_map/ppermute | solution.py:27
  4.8 0.0 copy-done
  4.8 0.0 copy-done.2
  4.8 0.0 copy-done.4
  4.8 2.1 %front_planes.1 = (f32[14,256,128]{2,1,0:T(8,128)S(1)}, bf16[16,128,256]{2,1,0:T(8,128)(2,1)S(1)}, bf16[384,384]{1,0:T(8,128)(2,1)S(1)}, f32[1,128]{1,0:T(1,128)S(1)}) custom-call(bf16[16,256,128]{2,1,0:T(8,128)(2,1)S(1)} %bitcast.10, bf16[3,3,3,64,64]{4,3,2,1,0:T(8,128)(2,1)S(1)} %copy-done.2, f32[64]{0:T(128)S(1)} %copy-done.4), custom_call_target="tpu_custom_call" | custom-call | flops 2200000000 | tf_op jit(solution)/shard_map/front_planes/pallas_call | solution.py:663
  6.9 0.0 collective-permute-done.y_near
  6.9 0.0 collective-permute-done.1.y_far
  7.0 1.6 %collective-permute-start.2 = (bf16[272,128]{1,0:T(8,128)(2,1)S(1)}, bf16[272,128]{1,0:T(8,128)(2,1)S(1)}, u32[]{:S(2)}, u32[]{:S(2)}) collective-permute-start(bf16[272,128]{1,0:T(8,128)(2,1)S(1)} %pack_planes.1), channel_id=1, source_target_pairs={{0,16},{16,0},{1,17},{17,1},{2,18},{18,2},{3,19},{19,3},{4,20},{20... | collective-permute-start | bytes 208904 | tf_op jit(solution)/shard_map/ppermute | solution.py:27
  8.5 0.0 copy-done.1
  8.5 2.5 %inner_planes.1 = (bf16[14,256,128]{2,1,0:T(8,128)(2,1)S(1)}, bf16[14,256,128]{2,1,0:T(8,128)(2,1)S(1)}, bf16[14,16,128]{2,1,0:T(8,128)(2,1)S(1)}, f32[384,384]{...) custom-call(bf16[16,256,128]{2,1,0:T(8,128)(2,1)S(1)} %bitcast.12, ...), custom_call_target="tpu_custom_call" | custom-call | flops 3300000000 | tf_op jit(solution)/shard_map/inner_planes/pallas_call | solution.py:699
  11.0 0.4 %collective-permute-done.2.x_near.x_far = bf16[272,128]{1,0:T(8,128)(2,1)S(1)} collective-permute-done((bf16[272,128]{1,0:T(8,128)(2,1)S(1)}, bf16[272,128]{1,0:T(8,128)(2,1)S(1)}, u32[]{:S(2)}, u32[]{:S(2)}) %collective-permute-start.2) | collective-permute-done | bytes 69664 | tf_op jit(solution)/shard_map/ppermute | solution.py:27
  11.4 1.0 %edge_planes.1 = (bf16[2,256,128]{2,1,0:T(8,128)(2,1)S(1)}, bf16[272,128]{1,0:T(8,128)(2,1)S(1)}, bf16[272,128]{1,0:T(8,128)(2,1)S(1)}, f32[384,384]{1,0:T(8,128...) custom-call(bf16[16,256,128]{2,1,0:T(8,128)(2,1)S(1)} %bitcast.13, ...), custom_call_target="tpu_custom_call" | custom-call | flops 2200000000 | tf_op jit(solution)/shard_map/edge_planes/pallas_call | solution.py:721
  12.4 0.0 copy-start.3
  12.4 0.0 collective-permute-start.3
  12.4 0.3 %rest_of_sums.1 = (f32[2,7,16,128]{3,2,1,0:T(8,128)S(1)}, f32[2,7,16,128]{3,2,1,0:T(8,128)S(1)}, f32[2,7,16,128]{3,2,1,0:T(8,128)S(1)}) custom-call(f32[384,384]{1,0:T(8,128)S(1)} %get-tuple-element.58.acc, f32[8,128]{1,0:T(8,128)S(1)} %get-tuple-element.59.sums), custom_call_target="tpu_custom_call" | custom-call | flops 770000000 | tf_op jit(solution)/shard_map/rest_of_sums/pallas_call | solution.py:805
  12.7 0.5 %collective-permute-start.5 = (f32[2,7,16,128]{3,2,1,0:T(8,128)S(1)}, f32[2,7,16,128]{3,2,1,0:T(8,128)S(1)}, u32[]{:S(2)}, u32[]{:S(2)}) collective-permute-start(f32[2,7,16,128]{3,2,1,0:T(8,128)S(1)} %get-tuple-element.70), channel_id=1, source_target_pairs={{0,4},{4,0},{8,12},{12,8},{1,5},{5,1},{9,13},{13,9},{2,6},{6,2},{1... | collective-permute-start | bytes 344072 | tf_op jit(solution)/shard_map/ppermute | solution.py:27
  13.2 0.4 %collective-permute-done.3.refs_1_ = bf16[2,7,16,128]{3,2,1,0:T(8,128)(2,1)S(1)} collective-permute-done((bf16[2,7,16,128]{3,2,1,0:T(8,128)(2,1)S(1)}, bf16[2,7,16,128]{3,2,1,0:T(8,128)(2,1)S(1)}, u32[]{:S(2)}, u32[]{:S(2)}) %collective-permute-start.3) | collective-permute-done | bytes 57376 | tf_op jit(solution)/shard_map/ppermute | solution.py:27
  13.7 1.4 %collective-permute-start.4 = (bf16[2,7,16,128]{3,2,1,0:T(8,128)(2,1)S(1)}, bf16[2,7,16,128]{3,2,1,0:T(8,128)(2,1)S(1)}, u32[]{:S(2)}, u32[]{:S(2)}) collective-permute-start(bf16[2,7,16,128]{3,2,1,0:T(8,128)(2,1)S(1)} %add_sums.4.refs_5_), channel_id=1, source_target_pairs={{0,5},{1,4},{2,7},{3,6},{4,1},{5,0},{6,3},{7,2},{8,13},{9,12},{10,... | collective-permute-start | bytes 172040 | tf_op jit(solution)/shard_map/ppermute | solution.py:35
  15.1 0.0 copy-done.3
  15.1 1.0 %back_weights.1 = (bf16[512,768]{1,0:T(8,128)(2,1)S(1)}, f32[14,8,128]{2,1,0:T(8,128)S(1)}) custom-call(bf16[3,3,3,64,64]{4,3,2,1,0:T(8,128)(2,1)S(1)} %copy-done.2, s32[3,3,3]{2,1,0:T(4,128)S(1)} %copy-done.3), custom_call_target="tpu_custom_call" | custom-call | flops 1100000000 | tf_op jit(solution)/shard_map/back_weights/pallas_call | solution.py:652
  16.1 1.4 %input_grad.3.refs_7_ = bf16[16,256,128]{2,1,0:T(8,128)(2,1)} custom-call(bf16[14,256,128]{2,1,0:T(8,128)(2,1)S(1)} %get-tuple-element.50.refs_0_, bf16[14,16,128]{2,1,0:T(8,128)(2,1)S(1)} %get-tuple-element.51.refs_1_, bf16[272,128]{1,0:T(8,128)(2,1)S(1)} %get-tuple-element.55.refs_2_, bf16[272,128]{1,0:T(8,128)(2,1)S(1)} %get-tuple-element.56.refs_3_, ...), custom_call_target="tpu_custom_call" | custom-call | flops 1100000000 | tf_op jit(solution)/shard_map/input_grad/pallas_call | solution.py:758
  17.4 0.2 collective-permute-done.4.refs_2_
  17.6 0.0 collective-permute-done.5.refs_1_
  17.7 2.4 %collective-permute-start.6 = (bf16[1,7,16,128]{3,2,1,0:T(8,128)(2,1)S(1)}, bf16[1,7,16,128]{3,2,1,0:T(8,128)(2,1)S(1)}, u32[]{:S(2)}, u32[]{:S(2)}) collective-permute-start(bf16[1,7,16,128]{3,2,1,0:T(8,128)(2,1)S(1)} %get-tuple-element.73), channel_id=1, source_target_pairs={{0,6},{1,7},{2,4},{3,5},{4,2},{5,3},{6,0},{7,1},{8,14},{9,15},{10,... | collective-permute-start | bytes 86024 | tf_op jit(solution)/shard_map/ppermute | solution.py:35
  20.1 1.5 %collective-permute-start.9 = (bf16[272,128]{1,0:T(8,128)(2,1)S(1)}, bf16[272,128]{1,0:T(8,128)(2,1)S(1)}, u32[]{:S(2)}, u32[]{:S(2)}) collective-permute-start(bf16[272,128]{1,0:T(8,128)(2,1)S(1)} %get-tuple-element.77), channel_id=1, source_target_pairs={{0,16},{16,0},{1,17},{17,1},{2,18},{18,2},{3,19},{19,3},{4,20},{20... | collective-permute-start | bytes 208904 | tf_op jit(solution)/shard_map/ppermute | solution.py:27
  21.6 0.3 %collective-permute-done.6.refs_1_ = bf16[1,7,16,128]{3,2,1,0:T(8,128)(2,1)S(1)} collective-permute-done((bf16[1,7,16,128]{3,2,1,0:T(8,128)(2,1)S(1)}, bf16[1,7,16,128]{3,2,1,0:T(8,128)(2,1)S(1)}, u32[]{:S(2)}, u32[]{:S(2)}) %collective-permute-start.6) | collective-permute-done | bytes 28704 | tf_op jit(solution)/shard_map/ppermute | solution.py:35
  21.9 1.0 %collective-permute-start.7 = (bf16[1,7,16,128]{3,2,1,0:T(8,128)(2,1)S(1)}, bf16[1,7,16,128]{3,2,1,0:T(8,128)(2,1)S(1)}, u32[]{:S(2)}, u32[]{:S(2)}) collective-permute-start(bf16[1,7,16,128]{3,2,1,0:T(8,128)(2,1)S(1)} %add_sums.5.refs_8_.refs_0_), channel_id=1, source_target_pairs={{0,12},{1,13},{2,14},{3,15},{4,8},{5,9},{6,10},{7,11},{8,4},{9,5},... | collective-permute-start | bytes 86024 | tf_op jit(solution)/shard_map/ppermute | solution.py:35
  22.9 1.7 %input_grad.4 = (bf16[16,256,128]{2,1,0:T(8,128)(2,1)}, bf16[16,256,128]{2,1,0:T(8,128)(2,1)}) custom-call(bf16[14,256,128]{2,1,0:T(8,128)(2,1)S(1)} %get-tuple-element.50.refs_0_, bf16[14,16,128]{2,1,0:T(8,128)(2,1)S(1)} %get-tuple-element.51.refs_1_, bf16[272,128]{1,0:T(8,128)(2,1)S(1)} %get-tuple-element.55.refs_2_, ...), custom_call_target="tpu_custom_call", output_to_operand_aliasing={{0}: (7, {})} | custom-call | flops 2750000128 | tf_op jit(solution)/shard_map/input_grad/pallas_call | solution.py:758
  24.6 0.7 %collective-permute-done.7.refs_1_ = bf16[1,7,16,128]{3,2,1,0:T(8,128)(2,1)S(1)} collective-permute-done((bf16[1,7,16,128]{3,2,1,0:T(8,128)(2,1)S(1)}, bf16[1,7,16,128]{3,2,1,0:T(8,128)(2,1)S(1)}, u32[]{:S(2)}, u32[]{:S(2)}) %collective-permute-start.7) | collective-permute-done | bytes 28704 | tf_op jit(solution)/shard_map/ppermute | solution.py:35
  25.3 1.3 %collective-permute-start.8 = (bf16[1,7,16,128]{3,2,1,0:T(8,128)(2,1)S(1)}, bf16[1,7,16,128]{3,2,1,0:T(8,128)(2,1)S(1)}, u32[]{:S(2)}, u32[]{:S(2)}) collective-permute-start(bf16[1,7,16,128]{3,2,1,0:T(8,128)(2,1)S(1)} %add_sums.6.refs_8_.refs_0_), channel_id=1, source_target_pairs={{0,20},{1,21},{2,22},{3,23},{4,16},{5,17},{6,18},{7,19},{8,28},{9,... | collective-permute-start | bytes 86024 | tf_op jit(solution)/shard_map/ppermute | solution.py:35
  26.6 0.0 collective-permute-done.9.refs_4_.refs_5_
  26.7 1.7 %input_grad.5 = bf16[16,256,128]{2,1,0:T(8,128)(2,1)} custom-call(bf16[14,256,128]{2,1,0:T(8,128)(2,1)S(1)} %get-tuple-element.50.refs_0_, bf16[14,16,128]{2,1,0:T(8,128)(2,1)S(1)} %get-tuple-element.51.refs_1_, bf16[272,128]{1,0:T(8,128)(2,1)S(1)} %get-tuple-element.55.refs_2_, ...), custom_call_target="tpu_custom_call", output_to_operand_aliasing={{}: (7, {})} | custom-call | flops 2750000128 | tf_op jit(solution)/shard_map/input_grad/pallas_call | solution.py:758
  28.4 0.3 %collective-permute-done.8.refs_1_ = bf16[1,7,16,128]{3,2,1,0:T(8,128)(2,1)S(1)} collective-permute-done((bf16[1,7,16,128]{3,2,1,0:T(8,128)(2,1)S(1)}, bf16[1,7,16,128]{3,2,1,0:T(8,128)(2,1)S(1)}, u32[]{:S(2)}, u32[]{:S(2)}) %collective-permute-start.8) | collective-permute-done | bytes 28704 | tf_op jit(solution)/shard_map/ppermute | solution.py:35
  28.7 0.3 collective-permute-start.10
  28.9 1.1 %collective-permute-done.10.other = f32[7,16,128]{2,1,0:T(8,128)S(1)} collective-permute-done((f32[7,16,128]{2,1,0:T(8,128)S(1)}, f32[7,16,128]{2,1,0:T(8,128)S(1)}, u32[]{:S(2)}, u32[]{:S(2)}) %collective-permute-start.10) | collective-permute-done | bytes 57376 | tf_op jit(solution)/shard_map/ppermute | solution.py:27
  30.0 0.7 %scale_weight_grad.1 = (bf16[27,16,64]{2,1,0:T(8,128)(2,1)}, f32[1,16]{1,0:T(1,128)}) custom-call(f32[7,16,128]{2,1,0:T(8,128)S(1)} %bitcast.15, f32[7,16,128]{2,1,0:T(8,128)S(1)} %collective-permute-done.10.other, f32[14,8,128]{2,1,0:T(8,128)S(1)} %get-tuple-element.81.scale_ref), custom_call_target="tpu_custom_call" | custom-call | tf_op jit(solution)/shard_map/scale_weight_grad/pallas_call | solution.py:847
  (8 shorter events, 0.2 us)
Async XLA Ops:
  1.5 3.2 %copy-start = (bf16[1,16,256,128]{3,2,1,0:T(8,128)(2,1)S(1)}, bf16[1,16,256,128]{3,2,1,0:T(8,128)(2,1)}, u32[]{:S(2)}) copy-start(bf16[1,16,256,128]{3,2,1,0:T(8,128)(2,1)} %param.5) | copy-start | bytes 3145732
  1.5 3.2 %copy-start.2 = (bf16[3,3,3,64,64]{4,3,2,1,0:T(8,128)(2,1)S(1)}, bf16[3,3,3,64,64]{4,3,2,1,0:T(8,128)(2,1)}, u32[]{:S(2)}) copy-start(bf16[3,3,3,64,64]{4,3,2,1,0:T(8,128)(2,1)} %refs_0_) | copy-start | bytes 663556
  1.6 3.2 %copy-start.4 = (f32[64]{0:T(128)S(1)}, f32[64]{0:T(128)}, u32[]{:S(2)}) copy-start(f32[64]{0:T(128)} %offsets.1) | copy-start | bytes 772
  1.6 5.3 %collective-permute-start = (bf16[16,4,128]{2,1,0:T(4,128)(2,1)S(1)}, bf16[16,4,128]{2,1,0:T(4,128)(2,1)S(1)}, u32[]{:S(2)}, u32[]{:S(2)}) collective-permute-start(bf16[16,4,128]{2,1,0:T(4,128)(2,1)S(1)} %get-tuple-element.44), channel_id=1, source_target_pairs={{0,4},{4,0},{8,12},{12,8},{1,5},{5,1},{9,13},{13,9},{2,6},{6,2},{1... | collective-permute-start | bytes 49160 | tf_op jit(solution)/shard_map/ppermute | solution.py:27
  2.1 6.4 %copy-start.1 = (bf16[1,16,256,128]{3,2,1,0:T(8,128)(2,1)S(1)}, bf16[1,16,256,128]{3,2,1,0:T(8,128)(2,1)}, u32[]{:S(2)}) copy-start(bf16[1,16,256,128]{3,2,1,0:T(8,128)(2,1)} %param.8) | copy-start | bytes 3145732
  2.1 4.8 %collective-permute-start.1 = (bf16[16,4,128]{2,1,0:T(4,128)(2,1)S(1)}, bf16[16,4,128]{2,1,0:T(4,128)(2,1)S(1)}, u32[]{:S(2)}, u32[]{:S(2)}) collective-permute-start(bf16[16,4,128]{2,1,0:T(4,128)(2,1)S(1)} %get-tuple-element.45), channel_id=1, source_target_pairs={{4,8},{8,4},{12,0},{0,12},{5,9},{9,5},{13,1},{1,13},{6,10},{10,6},... | collective-permute-start | bytes 49160 | tf_op jit(solution)/shard_map/ppermute | solution.py:27
  7.0 4.4 %collective-permute-start.2 = (bf16[272,128]{1,0:T(8,128)(2,1)S(1)}, bf16[272,128]{1,0:T(8,128)(2,1)S(1)}, u32[]{:S(2)}, u32[]{:S(2)}) collective-permute-start(bf16[272,128]{1,0:T(8,128)(2,1)S(1)} %pack_planes.1), channel_id=1, source_target_pairs={{0,16},{16,0},{1,17},{17,1},{2,18},{18,2},{3,19},{19,3},{4,20},{20... | collective-permute-start | bytes 208904 | tf_op jit(solution)/shard_map/ppermute | solution.py:27
  12.4 2.7 %copy-start.3 = (s32[3,3,3]{2,1,0:T(4,128)S(1)}, s32[3,3,3]{2,1,0:T(4,128)}, u32[]{:S(2)}) copy-start(s32[3,3,3]{2,1,0:T(4,128)} %refs_1_.1) | copy-start | bytes 328
  12.4 1.3 %collective-permute-start.3 = (bf16[2,7,16,128]{3,2,1,0:T(8,128)(2,1)S(1)}, bf16[2,7,16,128]{3,2,1,0:T(8,128)(2,1)S(1)}, u32[]{:S(2)}, u32[]{:S(2)}) collective-permute-start(bf16[2,7,16,128]{3,2,1,0:T(8,128)(2,1)S(1)} %get-tuple-element.61), channel_id=1, source_target_pairs={{0,4},{4,0},{8,12},{12,8},{1,5},{5,1},{9,13},{13,9},{2,6},{6,2},{1... | collective-permute-start | bytes 172040 | tf_op jit(solution)/shard_map/ppermute | solution.py:27
  12.7 4.9 %collective-permute-start.5 = (f32[2,7,16,128]{3,2,1,0:T(8,128)S(1)}, f32[2,7,16,128]{3,2,1,0:T(8,128)S(1)}, u32[]{:S(2)}, u32[]{:S(2)}) collective-permute-start(f32[2,7,16,128]{3,2,1,0:T(8,128)S(1)} %get-tuple-element.70), channel_id=1, source_target_pairs={{0,4},{4,0},{8,12},{12,8},{1,5},{5,1},{9,13},{13,9},{2,6},{6,2},{1... | collective-permute-start | bytes 344072 | tf_op jit(solution)/shard_map/ppermute | solution.py:27
  13.7 3.9 %collective-permute-start.4 = (bf16[2,7,16,128]{3,2,1,0:T(8,128)(2,1)S(1)}, bf16[2,7,16,128]{3,2,1,0:T(8,128)(2,1)S(1)}, u32[]{:S(2)}, u32[]{:S(2)}) collective-permute-start(bf16[2,7,16,128]{3,2,1,0:T(8,128)(2,1)S(1)} %add_sums.4.refs_5_), channel_id=1, source_target_pairs={{0,5},{1,4},{2,7},{3,6},{4,1},{5,0},{6,3},{7,2},{8,13},{9,12},{10,... | collective-permute-start | bytes 172040 | tf_op jit(solution)/shard_map/ppermute | solution.py:35
  17.7 4.3 %collective-permute-start.6 = (bf16[1,7,16,128]{3,2,1,0:T(8,128)(2,1)S(1)}, bf16[1,7,16,128]{3,2,1,0:T(8,128)(2,1)S(1)}, u32[]{:S(2)}, u32[]{:S(2)}) collective-permute-start(bf16[1,7,16,128]{3,2,1,0:T(8,128)(2,1)S(1)} %get-tuple-element.73), channel_id=1, source_target_pairs={{0,6},{1,7},{2,4},{3,5},{4,2},{5,3},{6,0},{7,1},{8,14},{9,15},{10,... | collective-permute-start | bytes 86024 | tf_op jit(solution)/shard_map/ppermute | solution.py:35
  20.1 6.5 %collective-permute-start.9 = (bf16[272,128]{1,0:T(8,128)(2,1)S(1)}, bf16[272,128]{1,0:T(8,128)(2,1)S(1)}, u32[]{:S(2)}, u32[]{:S(2)}) collective-permute-start(bf16[272,128]{1,0:T(8,128)(2,1)S(1)} %get-tuple-element.77), channel_id=1, source_target_pairs={{0,16},{16,0},{1,17},{17,1},{2,18},{18,2},{3,19},{19,3},{4,20},{20... | collective-permute-start | bytes 208904 | tf_op jit(solution)/shard_map/ppermute | solution.py:27
  21.9 3.4 %collective-permute-start.7 = (bf16[1,7,16,128]{3,2,1,0:T(8,128)(2,1)S(1)}, bf16[1,7,16,128]{3,2,1,0:T(8,128)(2,1)S(1)}, u32[]{:S(2)}, u32[]{:S(2)}) collective-permute-start(bf16[1,7,16,128]{3,2,1,0:T(8,128)(2,1)S(1)} %add_sums.5.refs_8_.refs_0_), channel_id=1, source_target_pairs={{0,12},{1,13},{2,14},{3,15},{4,8},{5,9},{6,10},{7,11},{8,4},{9,5},... | collective-permute-start | bytes 86024 | tf_op jit(solution)/shard_map/ppermute | solution.py:35
  25.3 3.4 %collective-permute-start.8 = (bf16[1,7,16,128]{3,2,1,0:T(8,128)(2,1)S(1)}, bf16[1,7,16,128]{3,2,1,0:T(8,128)(2,1)S(1)}, u32[]{:S(2)}, u32[]{:S(2)}) collective-permute-start(bf16[1,7,16,128]{3,2,1,0:T(8,128)(2,1)S(1)} %add_sums.6.refs_8_.refs_0_), channel_id=1, source_target_pairs={{0,20},{1,21},{2,22},{3,23},{4,16},{5,17},{6,18},{7,19},{8,28},{9,... | collective-permute-start | bytes 86024 | tf_op jit(solution)/shard_map/ppermute | solution.py:35
  28.7 1.3 %collective-permute-start.10 = (f32[7,16,128]{2,1,0:T(8,128)S(1)}, f32[7,16,128]{2,1,0:T(8,128)S(1)}, u32[]{:S(2)}, u32[]{:S(2)}) collective-permute-start(f32[7,16,128]{2,1,0:T(8,128)S(1)} %bitcast.14), channel_id=1, source_target_pairs={{0,4},{4,0},{8,12},{12,8},{1,5},{5,1},{9,13},{13,9},{2,6},{6,2},{1... | collective-permute-start | bytes 172040 | tf_op jit(solution)/shard_map/ppermute | solution.py:27

commit v9 on v8

--- a/solution.py
+++ b/solution.py
@@ -10,7 +10,7 @@
 RIM = 8
 THIN = 2
 PAD = 16
-CHUNK = 64
+CHUNK = 32
 SLOTS = 14
 VMEM = pl.BlockSpec(memory_space=pltpu.VMEM)
 SMEM = pl.BlockSpec(memory_space=pltpu.SMEM)

time: 30.9 us -> 30.9 us (level)
  no operation moved by 1% of the time
where the time goes in v9:
time: 30.9 us; the launch traced here: 30.7 us
  starting transfers between devices  13.2 us (43%)
  Pallas kernels  12.5 us (40%)
  waiting for transfers between devices  3.3 us (11%)
  local copies, waits for them, and re-layouts  0.87 us (3%)
  between operations  0.79 us (3%)
    ppermute x7, starting transfers between devices, swap(): return lax.ppermute(value, axis, links)  6.99 us
    ppermute x4, starting transfers between devices, exchange(): lax.ppermute(value, axes, [(i, i ^ flip) for i in range(math.prod(sizes))])  6.2 us
    pallas_call x3, Pallas kernels, back(): pl.pallas_call(lambda *refs: back_kernel(pairs, edges, stored, *refs), ou...  4.74 us
    pallas_call x1, Pallas kernels, local(): pl.pallas_call(inner_kernel, out_shape=(shape(inner, size_y, width), shap...  2.48 us
    pallas_call x1, Pallas kernels, local(): pl.pallas_call(front_kernel, out_shape=(shape(inner, size_y, width, dtype...  2.12 us
    ppermute x7, waiting for transfers between devices, swap(): return lax.ppermute(value, axis, links)  1.82 us
    ppermute x4, waiting for transfers between devices, exchange(): lax.ppermute(value, axes, [(i, i ^ flip) for i in range(math.prod(sizes))])  1.48 us
    pallas_call x1, Pallas kernels, local(): pl.pallas_call(edge_kernel, out_shape=(shape(2, size_y, width), shape(tal...  1.01 us
  transfers between devices with their start and end apart: 11, of which 7 were waited for; matrix products, arithmetic and copies ran while one was open for 0% of the time, Pallas kernels for 35%

profile of v9, /device:TPU:0, one launch (start us, length us, event | category | flops | bytes accessed | tf_op | source)
XLA Modules:
  0.0 30.7 jit_solution(4382996973241689461)
XLA Ops:
  0.6 0.8 %fusion = (bf16[16,2,128]{2,1,0:T(2,128)(2,1)S(1)}, bf16[16,2,128]{2,1,0:T(2,128)(2,1)S(1)}, bf16[16,2,128]{2,1,0:T(2,128)(2,1)S(1)}, bf16[16,2,128]{2,1,0:T(2,128)(2,1)S(1)}) fusion(bf16[16,256,128]{2,1,0:T(8,128)(2,1)} %bitcast.9, bf16[16,256,128]{2,1,0:T(8,128)(2,1)} %bitcast.16), kind=kLoop, calls=%fused_computation.1 | loop fusion | bytes 65536 | tf_op jit(solution)/shard_map/slice | solution.py:633
  1.5 0.0 copy-start
  1.5 0.0 copy-start.2
  1.6 0.0 copy-start.4
  1.6 0.5 %collective-permute-start = (bf16[16,4,128]{2,1,0:T(4,128)(2,1)S(1)}, bf16[16,4,128]{2,1,0:T(4,128)(2,1)S(1)}, u32[]{:S(2)}, u32[]{:S(2)}) collective-permute-start(bf16[16,4,128]{2,1,0:T(4,128)(2,1)S(1)} %get-tuple-element.44), channel_id=1, source_target_pairs={{0,4},{4,0},{8,12},{12,8},{1,5},{5,1},{9,13},{13,9},{2,6},{6,2},{1... | collective-permute-start | bytes 49160 | tf_op jit(solution)/shard_map/ppermute | solution.py:27
  2.1 0.0 copy-start.1
  2.1 2.6 %collective-permute-start.1 = (bf16[16,4,128]{2,1,0:T(4,128)(2,1)S(1)}, bf16[16,4,128]{2,1,0:T(4,128)(2,1)S(1)}, u32[]{:S(2)}, u32[]{:S(2)}) collective-permute-start(bf16[16,4,128]{2,1,0:T(4,128)(2,1)S(1)} %get-tuple-element.45), channel_id=1, source_target_pairs={{4,8},{8,4},{12,0},{0,12},{5,9},{9,5},{13,1},{1,13},{6,10},{10,6},... | collective-permute-start | bytes 49160 | tf_op jit(solution)/shard_map/ppermute | solution.py:27
  4.8 0.0 copy-done
  4.8 0.0 copy-done.2
  4.8 0.0 copy-done.4
  4.8 2.1 %front_planes.1 = (f32[14,256,128]{2,1,0:T(8,128)S(1)}, bf16[16,128,256]{2,1,0:T(8,128)(2,1)S(1)}, bf16[384,384]{1,0:T(8,128)(2,1)S(1)}, f32[1,128]{1,0:T(1,128)S(1)}) custom-call(bf16[16,256,128]{2,1,0:T(8,128)(2,1)S(1)} %bitcast.10, bf16[3,3,3,64,64]{4,3,2,1,0:T(8,128)(2,1)S(1)} %copy-done.2, f32[64]{0:T(128)S(1)} %copy-done.4), custom_call_target="tpu_custom_call" | custom-call | flops 2200000000 | tf_op jit(solution)/shard_map/front_planes/pallas_call | solution.py:663
  6.9 0.0 collective-permute-done.y_near
  6.9 0.0 collective-permute-done.1.y_far
  7.0 1.6 %collective-permute-start.2 = (bf16[272,128]{1,0:T(8,128)(2,1)S(1)}, bf16[272,128]{1,0:T(8,128)(2,1)S(1)}, u32[]{:S(2)}, u32[]{:S(2)}) collective-permute-start(bf16[272,128]{1,0:T(8,128)(2,1)S(1)} %pack_planes.1), channel_id=1, source_target_pairs={{0,16},{16,0},{1,17},{17,1},{2,18},{18,2},{3,19},{19,3},{4,20},{20... | collective-permute-start | bytes 208904 | tf_op jit(solution)/shard_map/ppermute | solution.py:27
  8.5 0.0 copy-done.1
  8.5 2.5 %inner_planes.1 = (bf16[14,256,128]{2,1,0:T(8,128)(2,1)S(1)}, bf16[14,256,128]{2,1,0:T(8,128)(2,1)S(1)}, bf16[14,16,128]{2,1,0:T(8,128)(2,1)S(1)}, f32[384,384]{...) custom-call(bf16[16,256,128]{2,1,0:T(8,128)(2,1)S(1)} %bitcast.12, ...), custom_call_target="tpu_custom_call" | custom-call | flops 3300000000 | tf_op jit(solution)/shard_map/inner_planes/pallas_call | solution.py:699
  11.0 0.3 %collective-permute-done.2.x_near.x_far = bf16[272,128]{1,0:T(8,128)(2,1)S(1)} collective-permute-done((bf16[272,128]{1,0:T(8,128)(2,1)S(1)}, bf16[272,128]{1,0:T(8,128)(2,1)S(1)}, u32[]{:S(2)}, u32[]{:S(2)}) %collective-permute-start.2) | collective-permute-done | bytes 69664 | tf_op jit(solution)/shard_map/ppermute | solution.py:27
  11.4 1.0 %edge_planes.1 = (bf16[2,256,128]{2,1,0:T(8,128)(2,1)S(1)}, bf16[272,128]{1,0:T(8,128)(2,1)S(1)}, bf16[272,128]{1,0:T(8,128)(2,1)S(1)}, f32[384,384]{1,0:T(8,128...) custom-call(bf16[16,256,128]{2,1,0:T(8,128)(2,1)S(1)} %bitcast.13, ...), custom_call_target="tpu_custom_call" | custom-call | flops 2200000000 | tf_op jit(solution)/shard_map/edge_planes/pallas_call | solution.py:721
  12.4 0.0 copy-start.3
  12.4 0.0 collective-permute-start.3
  12.4 0.3 %rest_of_sums.1 = (f32[2,7,16,128]{3,2,1,0:T(8,128)S(1)}, f32[2,7,16,128]{3,2,1,0:T(8,128)S(1)}, f32[2,7,16,128]{3,2,1,0:T(8,128)S(1)}) custom-call(f32[384,384]{1,0:T(8,128)S(1)} %get-tuple-element.58.acc, f32[8,128]{1,0:T(8,128)S(1)} %get-tuple-element.59.sums), custom_call_target="tpu_custom_call" | custom-call | flops 770000000 | tf_op jit(solution)/shard_map/rest_of_sums/pallas_call | solution.py:805
  12.7 0.5 %collective-permute-start.5 = (f32[2,7,16,128]{3,2,1,0:T(8,128)S(1)}, f32[2,7,16,128]{3,2,1,0:T(8,128)S(1)}, u32[]{:S(2)}, u32[]{:S(2)}) collective-permute-start(f32[2,7,16,128]{3,2,1,0:T(8,128)S(1)} %get-tuple-element.70), channel_id=1, source_target_pairs={{0,4},{4,0},{8,12},{12,8},{1,5},{5,1},{9,13},{13,9},{2,6},{6,2},{1... | collective-permute-start | bytes 344072 | tf_op jit(solution)/shard_map/ppermute | solution.py:27
  13.2 0.4 %collective-permute-done.3.refs_1_ = bf16[2,7,16,128]{3,2,1,0:T(8,128)(2,1)S(1)} collective-permute-done((bf16[2,7,16,128]{3,2,1,0:T(8,128)(2,1)S(1)}, bf16[2,7,16,128]{3,2,1,0:T(8,128)(2,1)S(1)}, u32[]{:S(2)}, u32[]{:S(2)}) %collective-permute-start.3) | collective-permute-done | bytes 57376 | tf_op jit(solution)/shard_map/ppermute | solution.py:27
  13.7 1.4 %collective-permute-start.4 = (bf16[2,7,16,128]{3,2,1,0:T(8,128)(2,1)S(1)}, bf16[2,7,16,128]{3,2,1,0:T(8,128)(2,1)S(1)}, u32[]{:S(2)}, u32[]{:S(2)}) collective-permute-start(bf16[2,7,16,128]{3,2,1,0:T(8,128)(2,1)S(1)} %add_sums.4.refs_5_), channel_id=1, source_target_pairs={{0,5},{1,4},{2,7},{3,6},{4,1},{5,0},{6,3},{7,2},{8,13},{9,12},{10,... | collective-permute-start | bytes 172040 | tf_op jit(solution)/shard_map/ppermute | solution.py:35
  15.1 0.0 copy-done.3
  15.1 1.0 %back_weights.1 = (bf16[512,768]{1,0:T(8,128)(2,1)S(1)}, f32[14,8,128]{2,1,0:T(8,128)S(1)}) custom-call(bf16[3,3,3,64,64]{4,3,2,1,0:T(8,128)(2,1)S(1)} %copy-done.2, s32[3,3,3]{2,1,0:T(4,128)S(1)} %copy-done.3), custom_call_target="tpu_custom_call" | custom-call | flops 1100000000 | tf_op jit(solution)/shard_map/back_weights/pallas_call | solution.py:652
  16.1 1.4 %input_grad.3.refs_7_ = bf16[16,256,128]{2,1,0:T(8,128)(2,1)} custom-call(bf16[14,256,128]{2,1,0:T(8,128)(2,1)S(1)} %get-tuple-element.50.refs_0_, bf16[14,16,128]{2,1,0:T(8,128)(2,1)S(1)} %get-tuple-element.51.refs_1_, bf16[272,128]{1,0:T(8,128)(2,1)S(1)} %get-tuple-element.55.refs_2_, bf16[272,128]{1,0:T(8,128)(2,1)S(1)} %get-tuple-element.56.refs_3_, ...), custom_call_target="tpu_custom_call" | custom-call | flops 1100000000 | tf_op jit(solution)/shard_map/input_grad/pallas_call | solution.py:758
  17.4 0.2 collective-permute-done.4.refs_2_
  17.6 0.0 collective-permute-done.5.refs_1_
  17.7 2.4 %collective-permute-start.6 = (bf16[1,7,16,128]{3,2,1,0:T(8,128)(2,1)S(1)}, bf16[1,7,16,128]{3,2,1,0:T(8,128)(2,1)S(1)}, u32[]{:S(2)}, u32[]{:S(2)}) collective-permute-start(bf16[1,7,16,128]{3,2,1,0:T(8,128)(2,1)S(1)} %get-tuple-element.73), channel_id=1, source_target_pairs={{0,6},{1,7},{2,4},{3,5},{4,2},{5,3},{6,0},{7,1},{8,14},{9,15},{10,... | collective-permute-start | bytes 86024 | tf_op jit(solution)/shard_map/ppermute | solution.py:35
  20.1 1.5 %collective-permute-start.9 = (bf16[272,128]{1,0:T(8,128)(2,1)S(1)}, bf16[272,128]{1,0:T(8,128)(2,1)S(1)}, u32[]{:S(2)}, u32[]{:S(2)}) collective-permute-start(bf16[272,128]{1,0:T(8,128)(2,1)S(1)} %get-tuple-element.77), channel_id=1, source_target_pairs={{0,16},{16,0},{1,17},{17,1},{2,18},{18,2},{3,19},{19,3},{4,20},{20... | collective-permute-start | bytes 208904 | tf_op jit(solution)/shard_map/ppermute | solution.py:27
  21.6 0.3 %collective-permute-done.6.refs_1_ = bf16[1,7,16,128]{3,2,1,0:T(8,128)(2,1)S(1)} collective-permute-done((bf16[1,7,16,128]{3,2,1,0:T(8,128)(2,1)S(1)}, bf16[1,7,16,128]{3,2,1,0:T(8,128)(2,1)S(1)}, u32[]{:S(2)}, u32[]{:S(2)}) %collective-permute-start.6) | collective-permute-done | bytes 28704 | tf_op jit(solution)/shard_map/ppermute | solution.py:35
  21.9 1.0 %collective-permute-start.7 = (bf16[1,7,16,128]{3,2,1,0:T(8,128)(2,1)S(1)}, bf16[1,7,16,128]{3,2,1,0:T(8,128)(2,1)S(1)}, u32[]{:S(2)}, u32[]{:S(2)}) collective-permute-start(bf16[1,7,16,128]{3,2,1,0:T(8,128)(2,1)S(1)} %add_sums.5.refs_8_.refs_0_), channel_id=1, source_target_pairs={{0,12},{1,13},{2,14},{3,15},{4,8},{5,9},{6,10},{7,11},{8,4},{9,5},... | collective-permute-start | bytes 86024 | tf_op jit(solution)/shard_map/ppermute | solution.py:35
  22.9 1.7 %input_grad.4 = (bf16[16,256,128]{2,1,0:T(8,128)(2,1)}, bf16[16,256,128]{2,1,0:T(8,128)(2,1)}) custom-call(bf16[14,256,128]{2,1,0:T(8,128)(2,1)S(1)} %get-tuple-element.50.refs_0_, bf16[14,16,128]{2,1,0:T(8,128)(2,1)S(1)} %get-tuple-element.51.refs_1_, bf16[272,128]{1,0:T(8,128)(2,1)S(1)} %get-tuple-element.55.refs_2_, ...), custom_call_target="tpu_custom_call", output_to_operand_aliasing={{0}: (7, {})} | custom-call | flops 2750000128 | tf_op jit(solution)/shard_map/input_grad/pallas_call | solution.py:758
  24.6 0.7 %collective-permute-done.7.refs_1_ = bf16[1,7,16,128]{3,2,1,0:T(8,128)(2,1)S(1)} collective-permute-done((bf16[1,7,16,128]{3,2,1,0:T(8,128)(2,1)S(1)}, bf16[1,7,16,128]{3,2,1,0:T(8,128)(2,1)S(1)}, u32[]{:S(2)}, u32[]{:S(2)}) %collective-permute-start.7) | collective-permute-done | bytes 28704 | tf_op jit(solution)/shard_map/ppermute | solution.py:35
  25.3 1.3 %collective-permute-start.8 = (bf16[1,7,16,128]{3,2,1,0:T(8,128)(2,1)S(1)}, bf16[1,7,16,128]{3,2,1,0:T(8,128)(2,1)S(1)}, u32[]{:S(2)}, u32[]{:S(2)}) collective-permute-start(bf16[1,7,16,128]{3,2,1,0:T(8,128)(2,1)S(1)} %add_sums.6.refs_8_.refs_0_), channel_id=1, source_target_pairs={{0,20},{1,21},{2,22},{3,23},{4,16},{5,17},{6,18},{7,19},{8,28},{9,... | collective-permute-start | bytes 86024 | tf_op jit(solution)/shard_map/ppermute | solution.py:35
  26.7 0.0 collective-permute-done.9.refs_4_.refs_5_
  26.7 1.7 %input_grad.5 = bf16[16,256,128]{2,1,0:T(8,128)(2,1)} custom-call(bf16[14,256,128]{2,1,0:T(8,128)(2,1)S(1)} %get-tuple-element.50.refs_0_, bf16[14,16,128]{2,1,0:T(8,128)(2,1)S(1)} %get-tuple-element.51.refs_1_, bf16[272,128]{1,0:T(8,128)(2,1)S(1)} %get-tuple-element.55.refs_2_, ...), custom_call_target="tpu_custom_call", output_to_operand_aliasing={{}: (7, {})} | custom-call | flops 2750000128 | tf_op jit(solution)/shard_map/input_grad/pallas_call | solution.py:758
  28.4 0.3 %collective-permute-done.8.refs_1_ = bf16[1,7,16,128]{3,2,1,0:T(8,128)(2,1)S(1)} collective-permute-done((bf16[1,7,16,128]{3,2,1,0:T(8,128)(2,1)S(1)}, bf16[1,7,16,128]{3,2,1,0:T(8,128)(2,1)S(1)}, u32[]{:S(2)}, u32[]{:S(2)}) %collective-permute-start.8) | collective-permute-done | bytes 28704 | tf_op jit(solution)/shard_map/ppermute | solution.py:35
  28.7 0.3 collective-permute-start.10
  28.9 1.1 %collective-permute-done.10.other = f32[7,16,128]{2,1,0:T(8,128)S(1)} collective-permute-done((f32[7,16,128]{2,1,0:T(8,128)S(1)}, f32[7,16,128]{2,1,0:T(8,128)S(1)}, u32[]{:S(2)}, u32[]{:S(2)}) %collective-permute-start.10) | collective-permute-done | bytes 57376 | tf_op jit(solution)/shard_map/ppermute | solution.py:27
  30.0 0.7 %scale_weight_grad.1 = (bf16[27,16,64]{2,1,0:T(8,128)(2,1)}, f32[1,16]{1,0:T(1,128)}) custom-call(f32[7,16,128]{2,1,0:T(8,128)S(1)} %bitcast.15, f32[7,16,128]{2,1,0:T(8,128)S(1)} %collective-permute-done.10.other, f32[14,8,128]{2,1,0:T(8,128)S(1)} %get-tuple-element.81.scale_ref), custom_call_target="tpu_custom_call" | custom-call | tf_op jit(solution)/shard_map/scale_weight_grad/pallas_call | solution.py:847
  (8 shorter events, 0.2 us)
Async XLA Ops:
  1.5 3.2 %copy-start = (bf16[1,16,256,128]{3,2,1,0:T(8,128)(2,1)S(1)}, bf16[1,16,256,128]{3,2,1,0:T(8,128)(2,1)}, u32[]{:S(2)}) copy-start(bf16[1,16,256,128]{3,2,1,0:T(8,128)(2,1)} %param.5) | copy-start | bytes 3145732
  1.5 3.2 %copy-start.2 = (bf16[3,3,3,64,64]{4,3,2,1,0:T(8,128)(2,1)S(1)}, bf16[3,3,3,64,64]{4,3,2,1,0:T(8,128)(2,1)}, u32[]{:S(2)}) copy-start(bf16[3,3,3,64,64]{4,3,2,1,0:T(8,128)(2,1)} %refs_0_) | copy-start | bytes 663556
  1.6 3.2 %copy-start.4 = (f32[64]{0:T(128)S(1)}, f32[64]{0:T(128)}, u32[]{:S(2)}) copy-start(f32[64]{0:T(128)} %offsets.1) | copy-start | bytes 772
  1.6 5.3 %collective-permute-start = (bf16[16,4,128]{2,1,0:T(4,128)(2,1)S(1)}, bf16[16,4,128]{2,1,0:T(4,128)(2,1)S(1)}, u32[]{:S(2)}, u32[]{:S(2)}) collective-permute-start(bf16[16,4,128]{2,1,0:T(4,128)(2,1)S(1)} %get-tuple-element.44), channel_id=1, source_target_pairs={{0,4},{4,0},{8,12},{12,8},{1,5},{5,1},{9,13},{13,9},{2,6},{6,2},{1... | collective-permute-start | bytes 49160 | tf_op jit(solution)/shard_map/ppermute | solution.py:27
  2.1 6.4 %copy-start.1 = (bf16[1,16,256,128]{3,2,1,0:T(8,128)(2,1)S(1)}, bf16[1,16,256,128]{3,2,1,0:T(8,128)(2,1)}, u32[]{:S(2)}) copy-start(bf16[1,16,256,128]{3,2,1,0:T(8,128)(2,1)} %param.8) | copy-start | bytes 3145732
  2.1 4.8 %collective-permute-start.1 = (bf16[16,4,128]{2,1,0:T(4,128)(2,1)S(1)}, bf16[16,4,128]{2,1,0:T(4,128)(2,1)S(1)}, u32[]{:S(2)}, u32[]{:S(2)}) collective-permute-start(bf16[16,4,128]{2,1,0:T(4,128)(2,1)S(1)} %get-tuple-element.45), channel_id=1, source_target_pairs={{4,8},{8,4},{12,0},{0,12},{5,9},{9,5},{13,1},{1,13},{6,10},{10,6},... | collective-permute-start | bytes 49160 | tf_op jit(solution)/shard_map/ppermute | solution.py:27
  7.0 4.4 %collective-permute-start.2 = (bf16[272,128]{1,0:T(8,128)(2,1)S(1)}, bf16[272,128]{1,0:T(8,128)(2,1)S(1)}, u32[]{:S(2)}, u32[]{:S(2)}) collective-permute-start(bf16[272,128]{1,0:T(8,128)(2,1)S(1)} %pack_planes.1), channel_id=1, source_target_pairs={{0,16},{16,0},{1,17},{17,1},{2,18},{18,2},{3,19},{19,3},{4,20},{20... | collective-permute-start | bytes 208904 | tf_op jit(solution)/shard_map/ppermute | solution.py:27
  12.4 2.7 %copy-start.3 = (s32[3,3,3]{2,1,0:T(4,128)S(1)}, s32[3,3,3]{2,1,0:T(4,128)}, u32[]{:S(2)}) copy-start(s32[3,3,3]{2,1,0:T(4,128)} %refs_1_.1) | copy-start | bytes 328
  12.4 1.3 %collective-permute-start.3 = (bf16[2,7,16,128]{3,2,1,0:T(8,128)(2,1)S(1)}, bf16[2,7,16,128]{3,2,1,0:T(8,128)(2,1)S(1)}, u32[]{:S(2)}, u32[]{:S(2)}) collective-permute-start(bf16[2,7,16,128]{3,2,1,0:T(8,128)(2,1)S(1)} %get-tuple-element.61), channel_id=1, source_target_pairs={{0,4},{4,0},{8,12},{12,8},{1,5},{5,1},{9,13},{13,9},{2,6},{6,2},{1... | collective-permute-start | bytes 172040 | tf_op jit(solution)/shard_map/ppermute | solution.py:27
  12.7 4.9 %collective-permute-start.5 = (f32[2,7,16,128]{3,2,1,0:T(8,128)S(1)}, f32[2,7,16,128]{3,2,1,0:T(8,128)S(1)}, u32[]{:S(2)}, u32[]{:S(2)}) collective-permute-start(f32[2,7,16,128]{3,2,1,0:T(8,128)S(1)} %get-tuple-element.70), channel_id=1, source_target_pairs={{0,4},{4,0},{8,12},{12,8},{1,5},{5,1},{9,13},{13,9},{2,6},{6,2},{1... | collective-permute-start | bytes 344072 | tf_op jit(solution)/shard_map/ppermute | solution.py:27
  13.7 3.9 %collective-permute-start.4 = (bf16[2,7,16,128]{3,2,1,0:T(8,128)(2,1)S(1)}, bf16[2,7,16,128]{3,2,1,0:T(8,128)(2,1)S(1)}, u32[]{:S(2)}, u32[]{:S(2)}) collective-permute-start(bf16[2,7,16,128]{3,2,1,0:T(8,128)(2,1)S(1)} %add_sums.4.refs_5_), channel_id=1, source_target_pairs={{0,5},{1,4},{2,7},{3,6},{4,1},{5,0},{6,3},{7,2},{8,13},{9,12},{10,... | collective-permute-start | bytes 172040 | tf_op jit(solution)/shard_map/ppermute | solution.py:35
  17.7 4.3 %collective-permute-start.6 = (bf16[1,7,16,128]{3,2,1,0:T(8,128)(2,1)S(1)}, bf16[1,7,16,128]{3,2,1,0:T(8,128)(2,1)S(1)}, u32[]{:S(2)}, u32[]{:S(2)}) collective-permute-start(bf16[1,7,16,128]{3,2,1,0:T(8,128)(2,1)S(1)} %get-tuple-element.73), channel_id=1, source_target_pairs={{0,6},{1,7},{2,4},{3,5},{4,2},{5,3},{6,0},{7,1},{8,14},{9,15},{10,... | collective-permute-start | bytes 86024 | tf_op jit(solution)/shard_map/ppermute | solution.py:35
  20.1 6.5 %collective-permute-start.9 = (bf16[272,128]{1,0:T(8,128)(2,1)S(1)}, bf16[272,128]{1,0:T(8,128)(2,1)S(1)}, u32[]{:S(2)}, u32[]{:S(2)}) collective-permute-start(bf16[272,128]{1,0:T(8,128)(2,1)S(1)} %get-tuple-element.77), channel_id=1, source_target_pairs={{0,16},{16,0},{1,17},{17,1},{2,18},{18,2},{3,19},{19,3},{4,20},{20... | collective-permute-start | bytes 208904 | tf_op jit(solution)/shard_map/ppermute | solution.py:27
  21.9 3.4 %collective-permute-start.7 = (bf16[1,7,16,128]{3,2,1,0:T(8,128)(2,1)S(1)}, bf16[1,7,16,128]{3,2,1,0:T(8,128)(2,1)S(1)}, u32[]{:S(2)}, u32[]{:S(2)}) collective-permute-start(bf16[1,7,16,128]{3,2,1,0:T(8,128)(2,1)S(1)} %add_sums.5.refs_8_.refs_0_), channel_id=1, source_target_pairs={{0,12},{1,13},{2,14},{3,15},{4,8},{5,9},{6,10},{7,11},{8,4},{9,5},... | collective-permute-start | bytes 86024 | tf_op jit(solution)/shard_map/ppermute | solution.py:35
  25.3 3.4 %collective-permute-start.8 = (bf16[1,7,16,128]{3,2,1,0:T(8,128)(2,1)S(1)}, bf16[1,7,16,128]{3,2,1,0:T(8,128)(2,1)S(1)}, u32[]{:S(2)}, u32[]{:S(2)}) collective-permute-start(bf16[1,7,16,128]{3,2,1,0:T(8,128)(2,1)S(1)} %add_sums.6.refs_8_.refs_0_), channel_id=1, source_target_pairs={{0,20},{1,21},{2,22},{3,23},{4,16},{5,17},{6,18},{7,19},{8,28},{9,... | collective-permute-start | bytes 86024 | tf_op jit(solution)/shard_map/ppermute | solution.py:35
  28.7 1.3 %collective-permute-start.10 = (f32[7,16,128]{2,1,0:T(8,128)S(1)}, f32[7,16,128]{2,1,0:T(8,128)S(1)}, u32[]{:S(2)}, u32[]{:S(2)}) collective-permute-start(f32[7,16,128]{2,1,0:T(8,128)S(1)} %bitcast.14), channel_id=1, source_target_pairs={{0,4},{4,0},{8,12},{12,8},{1,5},{5,1},{9,13},{13,9},{2,6},{6,2},{1... | collective-permute-start | bytes 172040 | tf_op jit(solution)/shard_map/ppermute | solution.py:27
